TPU v7x, 1024 devices: a whole 4x8x16 slice. The times are simulated.
1024 devices in a mesh: blk: 16 (over z), rep: 16 (over x_lo, y), pair: 4 (over x_hi, core).
Axes of the slice: x: 4 (x_hi: 2, x_lo: 2; x = x_hi * 2 + x_lo), y: 8, z: 16, core: 2. Of those that a mesh axis runs over, the one named last changes fastest.
Arguments:
- tokens: bfloat16 [163840, 4096], P(('blk', 'rep', 'pair')), may hold values from -24 to 24
- cotangent: bfloat16 [163840, 4096], P(('blk', 'rep', 'pair')), may hold values from -0.0390625 to 0.0390625
- gate_weight: bfloat16 [4096, 3584], P(None, 'blk'), may hold values from -0.09375 to 0.09375
- up_weight: bfloat16 [4096, 3584], P(None, 'blk'), may hold values from -0.09375 to 0.09375
- down_weight: bfloat16 [3584, 4096], P('blk'), may hold values from -0.25 to 0.25
- lengths: int32 [1024, 4], P(('blk', 'rep', 'pair')), may hold values from 1 to 157, as said below
- rewards: int32 [1024, 4], P(('blk', 'rep', 'pair')), may hold values from -65536 to 65536
Outputs:
- grad_gate: float32 [4096, 3584], P(('rep', 'pair'), 'blk')
- grad_up: float32 [4096, 3584], P(('rep', 'pair'), 'blk')
Inputs may be any that keep to these rules, and one draw needn't show every extreme that they name: `lengths`: every completion has at least one token. A device's live tokens fill its first rows; their count is at most 160 and equals 160 on some device. Two devices whose pair indices differ only in the lowest bit hold together at most 256 live tokens, and exactly that many for some such two.
All inputs are finite; a program needn't handle non-finite values.
Results may differ from a plain program's by a relative error of at most 0.024.
Values may be sent and summed in bfloat16 or wider, within the bound.
No kernel may reach another device: no remote copies, remote signals or barrier semaphores. Data moves between devices by JAX's collectives and lax.ppermute only.
A program may use at most 64 MiB of HBM per device.

v0:
```python
import jax
import jax.numpy as jnp
from jax import lax
from jax.sharding import PartitionSpec as P


def shifted(block, axis, distance):
    devices = range(lax.axis_size(axis))
    route = [((i - distance) % len(devices), i) for i in devices]
    return lax.ppermute(block, axis, route)


def row_weights(lengths, rewards, slot_count):
    position = jnp.arange(slot_count, dtype=jnp.int32)
    end_index = jnp.cumsum(lengths, axis=1)
    starts = end_index - lengths
    inside = (position[None, None, :] >= starts[:, :, None]) & (
        position[None, None, :] < end_index[:, :, None]
    )
    scaled = rewards.astype(jnp.float32)[:, :, None] / 65536.0
    return jnp.sum(jnp.where(inside, scaled, jnp.zeros_like(scaled)), axis=1)


def pieces(row_block, cot_block, gate_block, up_block, down_block):
    gate_pre = jnp.dot(row_block, gate_block, preferred_element_type=jnp.float32)
    up_pre = jnp.dot(row_block, up_block, preferred_element_type=jnp.float32)
    sigmoid_gate = jax.nn.sigmoid(gate_pre)
    active = gate_pre * sigmoid_gate
    back_hidden = lax.dot_general(
        cot_block, down_block, (((1,), (1,)), ((), ())), preferred_element_type=jnp.float32
    )
    gate_back = (
        back_hidden * up_pre * sigmoid_gate * (1.0 + gate_pre * (1.0 - sigmoid_gate))
    ).astype(jnp.bfloat16)
    up_back = (back_hidden * active).astype(jnp.bfloat16)
    return (gate_back, up_back)


def contract(left_side, right_side):
    return lax.dot_general(
        left_side, right_side, (((0,), (0,)), ((), ())), preferred_element_type=jnp.float32
    )


def on_device(tokens, cotangent, gate_weight, up_weight, down_weight, lengths, rewards):
    row_count = tokens.shape[0]
    weight = row_weights(lengths, rewards, row_count)[0]
    weighted = (weight[:, None] * cotangent.astype(jnp.float32)).astype(jnp.bfloat16)
    far_rows, far_cot = shifted((tokens, weighted), "blk", 1)
    all_rows = jnp.concatenate([tokens, far_rows], axis=0)
    all_cot = jnp.concatenate([weighted, far_cot], axis=0)
    gate_back, up_back = pieces(all_rows, all_cot, gate_weight, up_weight, down_weight)
    gate_term = contract(all_rows, gate_back)
    up_term = contract(all_rows, up_back)
    gate_sum, up_sum = (
        lax.psum_scatter(
            gate_term.astype(jnp.bfloat16), "rep", scatter_dimension=0, tiled=True
        ).astype(jnp.float32),
        lax.psum_scatter(
            up_term.astype(jnp.bfloat16), "rep", scatter_dimension=0, tiled=True
        ).astype(jnp.float32),
    )
    grad_gate, grad_up = (
        lax.psum_scatter(
            gate_sum.astype(jnp.bfloat16), "pair", scatter_dimension=0, tiled=True
        ).astype(jnp.float32),
        lax.psum_scatter(
            up_sum.astype(jnp.bfloat16), "pair", scatter_dimension=0, tiled=True
        ).astype(jnp.float32),
    )
    return (grad_gate, grad_up)


def solution(mesh):
    placed = (
        P(("blk", "rep", "pair"), None),
        P(("blk", "rep", "pair"), None),
        P(None, "blk"),
        P(None, "blk"),
        P("blk", None),
        P(("blk", "rep", "pair"), None),
        P(("blk", "rep", "pair"), None),
    )
    return jax.shard_map(
        on_device,
        mesh=mesh,
        in_specs=placed,
        out_specs=(P(("rep", "pair"), "blk"), P(("rep", "pair"), "blk")),
        check_vma=False,
    )
```

profile of v0, /device:TPU:1, one launch (start us, length us, event | category | flops | bytes accessed | tf_op | source)
XLA Modules:
  0.0 356.4 jit_solution(18418581194890677050)
XLA Ops:
  7.2 0.0 reduce-scatter.9.cloned.1.call-start
  7.2 5.1 %collective-permute-start = (bf16[160,4096]{1,0:T(8,128)(2,1)}, bf16[160,4096]{1,0:T(8,128)(2,1)}, u32[]{:S(2)}, u32[]{:S(2)}) collective-permute-start(bf16[160,4096]{1,0:T(8,128)(2,1)} %param.7), channel_id=1, source_target_pairs={{960,0},{0,64},{64,128},{128,192},{192,256},{256,320},{320,384},{3... | collective-permute-start | bytes 3932168 | tf_op jit(solution)/shard_map/ppermute | solution.py:10
  12.3 0.7 multiply_bitcast_fusion
  13.0 0.8 reduce_window_sum.13
  13.8 0.7 subtract_bitcast_fusion
  14.5 0.1 select_reduce_fusion
  14.6 1.6 multiply_convert_fusion
  16.2 4.1 %collective-permute-start.1 = (bf16[160,4096]{1,0:T(8,128)(2,1)S(1)}, bf16[160,4096]{1,0:T(8,128)(2,1)S(1)}, u32[]{:S(2)}, u32[]{:S(2)}) collective-permute-start(bf16[160,4096]{1,0:T(8,128)(2,1)S(1)} %multiply_convert_fusion), channel_id=1, source_target_pairs={{960,0},{0,64},{64,128},{128,192},{192,256},{256,320},{320,384},{3... | collective-permute-start | bytes 3932168 | tf_op jit(solution)/shard_map/ppermute | solution.py:10
  20.4 0.1 constant_dynamic-update-slice_fusion.1
  20.5 34.6 %collective-permute-done = bf16[160,4096]{1,0:T(8,128)(2,1)} collective-permute-done((bf16[160,4096]{1,0:T(8,128)(2,1)}, bf16[160,4096]{1,0:T(8,128)(2,1)}, u32[]{:S(2)}, u32[]{:S(2)}) %collective-permute-start) | collective-permute-done | bytes 1310752 | tf_op jit(solution)/shard_map/ppermute | solution.py:10
  55.1 1.4 constant_dynamic-update-slice_fusion
  56.5 1.0 fusion.16
  57.5 0.5 copy-done.2
  58.0 25.1 %collective-permute-done.1 = bf16[160,4096]{1,0:T(8,128)(2,1)S(1)} collective-permute-done((bf16[160,4096]{1,0:T(8,128)(2,1)S(1)}, bf16[160,4096]{1,0:T(8,128)(2,1)S(1)}, u32[]{:S(2)}, u32[]{:S(2)}) %collective-permute-start.1) | collective-permute-done | bytes 1310752 | tf_op jit(solution)/shard_map/ppermute | solution.py:10
  83.1 0.9 fusion
  83.9 7.1 %convolution_convert_fusion.1 = bf16[4096,224]{0,1:T(8,128)(2,1)} fusion(bf16[320,4096]{1,0:T(8,128)(2,1)} %copy-done.2, f32[320,224]{1,0:T(8,128)S(1)} %fusion, bf16[4096,224]{0,1:T(8,128)(2,1)S(1)} %copy-done, f32[320,224]{1,0:T(8,128)S(1)} %fusion.16), kind=kOutput, calls=%fused_computation.1 | convolution fusion | flops 1176039424 | bytes 6864896 | tf_op jit(solution)/shard_map/dot_general | solution.py:40
  91.1 0.0 reduce-scatter.9.cloned.1.call-update
  91.1 0.0 reduce-scatter.11.cloned.1.call-start
  91.1 4.2 %convolution_convert_fusion = bf16[4096,224]{0,1:T(8,128)(2,1)} fusion(bf16[320,4096]{1,0:T(8,128)(2,1)} %copy-done.2, f32[320,224]{1,0:T(8,128)S(1)} %fusion, f32[320,224]{1,0:T(8,128)S(1)} %fusion.16), kind=kOutput, calls=%fused_computation | convolution fusion | flops 588550144 | bytes 5029888 | tf_op jit(solution)/shard_map/dot_general | solution.py:40
  95.3 0.0 reduce-scatter.11.cloned.1.call-update
  95.3 0.0 reduce-scatter.13.cloned.1.call-start
  95.4 61.1 %reduce-scatter.9.cloned.1.call-done = bf16[256,224]{0,1:T(8,128)(2,1)} async-done(((bf16[4096,224]{0,1:T(8,128)(2,1)}), bf16[256,224]{0,1:T(8,128)(2,1)}) %reduce-scatter.9.cloned.1.call-update) | async-done | bytes 114704 | tf_op jit(solution)/shard_map/reduce_scatter | solution.py:56
  156.5 1.6 copy.15
  158.2 0.0 reduce-scatter.15.cloned.1.call-start
  158.2 79.9 %reduce-scatter.11.cloned.1.call-done = bf16[256,224]{0,1:T(8,128)(2,1)} async-done(((bf16[4096,224]{0,1:T(8,128)(2,1)}), bf16[256,224]{0,1:T(8,128)(2,1)}) %reduce-scatter.11.cloned.1.call-update) | async-done | bytes 114704 | tf_op jit(solution)/shard_map/reduce_scatter | solution.py:59
  238.1 1.6 copy.17
  239.8 56.8 %reduce-scatter.13.cloned.1.call-done = bf16[64,224]{1,0:T(8,128)(2,1)} async-done(((bf16[256,224]{1,0:T(8,128)(2,1)}), bf16[64,224]{1,0:T(8,128)(2,1)}) %reduce-scatter.13.cloned.1.call-update) | async-done | bytes 28688
  296.6 0.9 copy.16
  297.4 0.7 copy.13
  298.2 50.1 %reduce-scatter.15.cloned.1.call-done = bf16[64,224]{1,0:T(8,128)(2,1)} async-done(((bf16[256,224]{1,0:T(8,128)(2,1)}), bf16[64,224]{1,0:T(8,128)(2,1)}) %reduce-scatter.15.cloned.1.call-update) | async-done | bytes 28688
  348.2 0.9 copy.18
  349.1 0.7 copy.14
  (11 shorter events, 0.1 us)
Async XLA Ops:
  7.2 76.8 %copy-start = (bf16[4096,224]{0,1:T(8,128)(2,1)S(1)}, bf16[4096,224]{0,1:T(8,128)(2,1)}, u32[]{:S(2)}) copy-start(bf16[4096,224]{0,1:T(8,128)(2,1)} %param.10) | copy-start | bytes 5505028
  7.2 13.2 %copy-start.1 = (bf16[160,4096]{1,0:T(8,128)(2,1)S(1)}, bf16[160,4096]{1,0:T(8,128)(2,1)}, u32[]{:S(2)}) copy-start(bf16[160,4096]{1,0:T(8,128)(2,1)} %param.7) | copy-start | bytes 3932164
  7.2 149.3 %reduce-scatter.9.cloned.1.call-start = ((), (), s32[]{:S(2)}) async-start(), calls=%async_computation.4 | async-start | bytes 1949696 | tf_op jit(solution)/shard_map/reduce_scatter | solution.py:56
  7.2 47.8 %collective-permute-start = (bf16[160,4096]{1,0:T(8,128)(2,1)}, bf16[160,4096]{1,0:T(8,128)(2,1)}, u32[]{:S(2)}, u32[]{:S(2)}) collective-permute-start(bf16[160,4096]{1,0:T(8,128)(2,1)} %param.7), channel_id=1, source_target_pairs={{960,0},{0,64},{64,128},{128,192},{192,256},{256,320},{320,384},{3... | collective-permute-start | bytes 3932168 | tf_op jit(solution)/shard_map/ppermute | solution.py:10
  16.2 40.3 %copy-start.3 = (bf16[4096,224]{0,1:T(8,128)(2,1)S(1)}, bf16[4096,224]{0,1:T(8,128)(2,1)}, u32[]{:S(2)}) copy-start(bf16[4096,224]{0,1:T(8,128)(2,1)} %param.9) | copy-start | bytes 5505028
  16.2 66.9 %collective-permute-start.1 = (bf16[160,4096]{1,0:T(8,128)(2,1)S(1)}, bf16[160,4096]{1,0:T(8,128)(2,1)S(1)}, u32[]{:S(2)}, u32[]{:S(2)}) collective-permute-start(bf16[160,4096]{1,0:T(8,128)(2,1)S(1)} %multiply_convert_fusion), channel_id=1, source_target_pairs={{960,0},{0,64},{64,128},{128,192},{192,256},{256,320},{320,384},{3... | collective-permute-start | bytes 3932168 | tf_op jit(solution)/shard_map/ppermute | solution.py:10
  56.5 1.5 copy-start.2
  56.5 26.6 %copy-start.4 = (bf16[224,4096]{1,0:T(8,128)(2,1)S(1)}, bf16[224,4096]{1,0:T(8,128)(2,1)}, u32[]{:S(2)}) copy-start(bf16[224,4096]{1,0:T(8,128)(2,1)} %param.11) | copy-start | bytes 5505028
  91.1 147.0 %reduce-scatter.11.cloned.1.call-start = ((), (), s32[]{:S(2)}) async-start(), calls=%async_computation.5 | async-start | bytes 1949696 | tf_op jit(solution)/shard_map/reduce_scatter | solution.py:59
  95.3 201.2 %reduce-scatter.13.cloned.1.call-start = ((), (), s32[]{:S(2)}) async-start(), calls=%async_computation.6 | async-start | bytes 163840
  158.2 190.1 %reduce-scatter.15.cloned.1.call-start = ((), (), s32[]{:S(2)}) async-start(), calls=%async_computation.7 | async-start | bytes 163840
Sparse Core Ops, SparseCore 0:
  91.2 65.2 reduce-scatter.8
  160.3 77.7 reduce-scatter.10
  241.7 54.8 reduce-scatter.12
  300.4 47.8 reduce-scatter.14
where the time goes:
time: 357 us; the launch traced here: 356 us
  waiting for transfers between devices  308 us (86%)
  between operations  13.9 us (4%)
  matrix products  13.1 us (4%)
  starting transfers between devices  9.39 us (3%)
  local copies, waits for them, and re-layouts  8.53 us (2%)
  other arithmetic  3.85 us (1%)
    unnamed x6, waiting for transfers between devices  107 us
    reduce_scatter x1, waiting for transfers between devices, on_device(): lax.psum_scatter(up_term.astype(jnp.bfloat16), 'rep', scatter_dimension=0...  79.9 us
    reduce_scatter x1, waiting for transfers between devices, on_device(): lax.psum_scatter(gate_term.astype(jnp.bfloat16), 'rep', scatter_dimension...  61.1 us
    ppermute x2, waiting for transfers between devices, shifted(): return lax.ppermute(block, axis, route)  59.7 us
    dot_general x2, matrix products, contract(): lax.dot_general(left_side, right_side, (((0,), (0,)), ((), ())), preferre...  11.3 us
    ppermute x2, starting transfers between devices, shifted(): return lax.ppermute(block, axis, route)  9.23 us
  transfers between devices with their start and end apart: 6, of which 6 were waited for; matrix products, arithmetic and copies ran while one was open for 4% of the time, Pallas kernels for 0%

commit v1 on v0

--- a/solution.py
+++ b/solution.py
@@ -1,7 +1,11 @@
 import jax
 import jax.numpy as jnp
 from jax import lax
+from jax.sharding import Mesh
 from jax.sharding import PartitionSpec as P
+
+HB = 224
+ROWS = 64
 
 
 def shifted(block, axis, distance):
@@ -46,45 +50,26 @@
     row_count = tokens.shape[0]
     weight = row_weights(lengths, rewards, row_count)[0]
     weighted = (weight[:, None] * cotangent.astype(jnp.float32)).astype(jnp.bfloat16)
-    far_rows, far_cot = shifted((tokens, weighted), "blk", 1)
+    far_rows, far_cot = shifted((tokens, weighted), "z", 1)
     all_rows = jnp.concatenate([tokens, far_rows], axis=0)
     all_cot = jnp.concatenate([weighted, far_cot], axis=0)
     gate_back, up_back = pieces(all_rows, all_cot, gate_weight, up_weight, down_weight)
-    gate_term = contract(all_rows, gate_back)
-    up_term = contract(all_rows, up_back)
-    gate_sum, up_sum = (
-        lax.psum_scatter(
-            gate_term.astype(jnp.bfloat16), "rep", scatter_dimension=0, tiled=True
-        ).astype(jnp.float32),
-        lax.psum_scatter(
-            up_term.astype(jnp.bfloat16), "rep", scatter_dimension=0, tiled=True
-        ).astype(jnp.float32),
-    )
-    grad_gate, grad_up = (
-        lax.psum_scatter(
-            gate_sum.astype(jnp.bfloat16), "pair", scatter_dimension=0, tiled=True
-        ).astype(jnp.float32),
-        lax.psum_scatter(
-            up_sum.astype(jnp.bfloat16), "pair", scatter_dimension=0, tiled=True
-        ).astype(jnp.float32),
-    )
-    return (grad_gate, grad_up)
+    both = jnp.concatenate([gate_back, up_back], axis=1)
+    ordered = all_rows.reshape(-1, 2, 8, 2, 2, ROWS).transpose(0, 4, 2, 3, 1, 5)
+    ordered = ordered.reshape(all_rows.shape)
+    term = contract(ordered, both).astype(jnp.bfloat16)
+    term = lax.psum_scatter(term, "c", scatter_dimension=0, tiled=True)
+    term = lax.psum_scatter(term, "y", scatter_dimension=0, tiled=True)
+    term = lax.all_to_all(term, ("xh", "xl"), split_axis=0, concat_axis=0, tiled=True)
+    total = jnp.sum(term.reshape(4, ROWS, 2 * HB).astype(jnp.float32), axis=0)
+    return (total[:, :HB], total[:, HB:])
 
 
 def solution(mesh):
-    placed = (
-        P(("blk", "rep", "pair"), None),
-        P(("blk", "rep", "pair"), None),
-        P(None, "blk"),
-        P(None, "blk"),
-        P("blk", None),
-        P(("blk", "rep", "pair"), None),
-        P(("blk", "rep", "pair"), None),
+    fine = Mesh(mesh.devices.reshape(16, 2, 8, 2, 2), ("z", "xl", "y", "xh", "c"))
+    rows = P(("z", "xl", "y", "xh", "c"), None)
+    placed = (rows, rows, P(None, "z"), P(None, "z"), P("z", None), rows, rows)
+    out = P(("xl", "y", "xh", "c"), "z")
+    return jax.shard_map(
+        on_device, mesh=fine, in_specs=placed, out_specs=(out, out), check_vma=False
     )
-    return jax.shard_map(
-        on_device,
-        mesh=mesh,
-        in_specs=placed,
-        out_specs=(P(("rep", "pair"), "blk"), P(("rep", "pair"), "blk")),
-        check_vma=False,
-    )

time: 357 us -> 184 us (0.52)
  the two profiles are of different devices: /device:TPU:1 before, /device:TPU:24 now
where the time goes in v1:
time: 184 us
  waiting for transfers between devices  123 us (67%)
  between operations  14.1 us (8%)
  blocking collectives  10.7 us (6%)
  local copies, waits for them, and re-layouts  9.47 us (5%)
  matrix products  8.93 us (5%)
  starting transfers between devices  8.89 us (5%)
  other arithmetic  8.39 us (5%)
    reduce_scatter x1, waiting for transfers between devices, on_device(): term = lax.psum_scatter(term, 'y', scatter_dimension=0, tiled=True)  54.4 us
    ppermute x2, waiting for transfers between devices, shifted(): return lax.ppermute(block, axis, route)  49.7 us
    reduce_scatter x1, waiting for transfers between devices, on_device(): term = lax.psum_scatter(term, 'c', scatter_dimension=0, tiled=True)  19.2 us
    all_to_all x1, blocking collectives, on_device(): lax.all_to_all(term, ('xh', 'xl'), split_axis=0, concat_axis=0, tiled=True)  10.7 us
    ppermute x2, starting transfers between devices, shifted(): return lax.ppermute(block, axis, route)  8.81 us
    dot_general x1, matrix products, contract(): lax.dot_general(left_side, right_side, (((0,), (0,)), ((), ())), preferre...  4.08 us
    ppermute x1, local copies, waits for them, and re-layouts, shifted(): return lax.ppermute(block, axis, route)  3.73 us
  transfers between devices with their start and end apart: 4, of which 4 were waited for; matrix products, arithmetic and copies ran while one was open for 9% of the time, Pallas kernels for 0%

profile of v1, /device:TPU:24, one launch (start us, length us, event | category | flops | bytes accessed | tf_op | source)
XLA Modules:
  0.0 183.9 jit_solution(14546081343474212519)
XLA Ops:
  7.2 0.0 copy-start
  7.2 0.0 reduce-scatter.3.cloned.1.call-start
  7.2 4.5 %collective-permute-start = (bf16[160,4096]{1,0:T(8,128)(2,1)}, bf16[160,4096]{1,0:T(8,128)(2,1)}, u32[]{:S(2)}, u32[]{:S(2)}) collective-permute-start(bf16[160,4096]{1,0:T(8,128)(2,1)} %param.7), channel_id=1, source_target_pairs={{960,0},{0,64},{64,128},{128,192},{192,256},{256,320},{320,384},{3... | collective-permute-start | bytes 3932168 | tf_op jit(solution)/shard_map/ppermute | solution.py:14
  11.8 0.8 reduce_window_sum.13
  12.6 0.7 subtract_bitcast_fusion
  13.3 0.7 multiply_bitcast_fusion
  13.9 0.1 select_reduce_fusion
  14.0 2.7 %multiply_convert_fusion = bf16[160,4096]{1,0:T(8,128)(2,1)} fusion(bf16[160,4096]{1,0:T(8,128)(2,1)} %param.8, f32[160]{0:T(256)S(1)} %select_reduce_fusion), kind=kLoop, calls=%fused_computation.6 | loop fusion | flops 1966080 | bytes 2622080 | tf_op jit(solution)/shard_map/convert_element_type | solution.py:52
  16.7 4.3 %collective-permute-start.1 = (bf16[160,4096]{1,0:T(8,128)(2,1)}, bf16[160,4096]{1,0:T(8,128)(2,1)}, u32[]{:S(2)}, u32[]{:S(2)}) collective-permute-start(bf16[160,4096]{1,0:T(8,128)(2,1)} %multiply_convert_fusion), channel_id=1, source_target_pairs={{960,0},{0,64},{64,128},{128,192},{192,256},{256,320},{320,384},{3... | collective-permute-start | bytes 3932168 | tf_op jit(solution)/shard_map/ppermute | solution.py:14
  21.0 0.0 copy-done.1
  21.0 2.4 %copy.17 = bf16[160,4096]{0,1:T(8,128)(2,1)} copy(bf16[160,4096]{1,0:T(8,128)(2,1)S(1)} %copy-done.1) | data formatting | bytes 2621440 | tf_op args[0]
  23.4 32.2 %collective-permute-done = bf16[160,4096]{1,0:T(8,128)(2,1)} collective-permute-done((bf16[160,4096]{1,0:T(8,128)(2,1)}, bf16[160,4096]{1,0:T(8,128)(2,1)}, u32[]{:S(2)}, u32[]{:S(2)}) %collective-permute-start) | collective-permute-done | bytes 1310752 | tf_op jit(solution)/shard_map/ppermute | solution.py:14
  55.6 3.7 %copy.18 = bf16[160,4096]{0,1:T(8,128)(2,1)} copy(bf16[160,4096]{1,0:T(8,128)(2,1)} %collective-permute-done) | data formatting | bytes 2621440 | tf_op jit(solution)/shard_map/ppermute | solution.py:14
  59.4 3.4 %pad_maximum_fusion = bf16[320,4096]{0,1:T(8,128)(2,1)S(1)} fusion(bf16[160,4096]{0,1:T(8,128)(2,1)} %copy.18, bf16[160,4096]{0,1:T(8,128)(2,1)} %copy.17), kind=kLoop, calls=%fused_computation.1 | loop fusion | flops 5242880 | bytes 5242880 | tf_op jit(solution)/shard_map/concatenate | solution.py:54
  62.8 0.0 copy-start.2
  62.8 0.4 copy.19
  63.2 1.1 copy-done.2
  64.3 1.1 fusion.14
  65.4 0.0 copy-start.3
  65.4 17.5 %collective-permute-done.1 = bf16[160,4096]{1,0:T(8,128)(2,1)} collective-permute-done((bf16[160,4096]{1,0:T(8,128)(2,1)}, bf16[160,4096]{1,0:T(8,128)(2,1)}, u32[]{:S(2)}, u32[]{:S(2)}) %collective-permute-start.1) | collective-permute-done | bytes 1310752 | tf_op jit(solution)/shard_map/ppermute | solution.py:14
  82.9 0.0 copy-done
  82.9 2.6 %multiply_convert_fusion.1 = (bf16[320,224]{1,0:T(8,128)(2,1)S(1)}, f32[320,224]{1,0:T(8,128)S(1)}) fusion(f32[320,224]{1,0:T(8,128)S(1)} %fusion.14, bf16[224,4096]{1,0:T(8,128)(2,1)S(1)} %copy-done, bf16[160,4096]{1,0:T(8,128)(2,1)} %collective-permute-done.1, bf16[160,4096]{1,0:T(8,128)(2,1)} %multiply_convert_fusion), kind=kOutput, calls=%fused_computation.15 | convolution fusion | flops 592875520 | bytes 5173248 | tf_op jit(solution)/shard_map/dot_general | solution.py:33
  85.5 1.2 fusion.6
  86.7 4.1 %convolution_convert_fusion = bf16[4096,448]{0,1:T(8,128)(2,1)} fusion(bf16[320,4096]{0,1:T(8,128)(2,1)S(1)} %bitcast.16, bf16[320,224]{1,0:T(8,128)(2,1)S(1)} %get-tuple-element.4, bf16[320,224]{1,0:T(8,128)(2,1)S(1)} %fusion.6), kind=kOutput, calls=%fused_computation | convolution fusion | flops 1176813568 | bytes 6578176 | tf_op jit(solution)/shard_map/dot_general | solution.py:44
  90.8 0.0 reduce-scatter.3.cloned.1.call-update
  90.8 0.0 reduce-scatter.5.cloned.1.call-start
  90.9 19.2 %reduce-scatter.3.cloned.1.call-done = bf16[2048,448]{0,1:T(8,128)(2,1)} async-done(((bf16[4096,448]{0,1:T(8,128)(2,1)}), bf16[2048,448]{0,1:T(8,128)(2,1)}) %reduce-scatter.3.cloned.1.call-update) | async-done | bytes 1835024 | tf_op jit(solution)/shard_map/reduce_scatter | solution.py:61
  110.1 0.0 reduce-scatter.5.cloned.1.call-update
  110.1 54.4 %reduce-scatter.5.cloned.1.call-done = bf16[256,448]{0,1:T(8,128)(2,1)} async-done(((bf16[2048,448]{0,1:T(8,128)(2,1)}), bf16[256,448]{0,1:T(8,128)(2,1)}) %reduce-scatter.5.cloned.1.call-update) | async-done | bytes 229392 | tf_op jit(solution)/shard_map/reduce_scatter | solution.py:62
  164.5 1.1 copy.20
  165.6 10.7 %all_to_all.9 = bf16[4,64,448]{2,1,0:T(8,128)(2,1)S(1)} all-to-all(bf16[4,64,448]{2,1,0:T(8,128)(2,1)S(1)} %bitcast.18), channel_id=1, replica_groups=mesh['z'=16,'xl'=2,'y'=8,'xh'=2,'c'=2] {'xh','xl'}, dimensions={0} | all-to-all | bytes 458752 | tf_op jit(solution)/shard_map/all_to_all | solution.py:63
  176.4 0.7 fusion.13
  (3 shorter events, 0.0 us)
Async XLA Ops:
  7.2 75.7 %copy-start = (bf16[224,4096]{1,0:T(8,128)(2,1)S(1)}, bf16[224,4096]{1,0:T(8,128)(2,1)}, u32[]{:S(2)}) copy-start(bf16[224,4096]{1,0:T(8,128)(2,1)} %param.11) | copy-start | bytes 5505028
  7.2 13.8 %copy-start.1 = (bf16[160,4096]{1,0:T(8,128)(2,1)S(1)}, bf16[160,4096]{1,0:T(8,128)(2,1)}, u32[]{:S(2)}) copy-start(bf16[160,4096]{1,0:T(8,128)(2,1)} %param.7) | copy-start | bytes 3932164
  7.2 102.9 %reduce-scatter.3.cloned.1.call-start = ((), (), s32[]{:S(2)}) async-start(), calls=%async_computation.3 | async-start | bytes 5505024 | tf_op jit(solution)/shard_map/reduce_scatter | solution.py:61
  7.2 48.4 %collective-permute-start = (bf16[160,4096]{1,0:T(8,128)(2,1)}, bf16[160,4096]{1,0:T(8,128)(2,1)}, u32[]{:S(2)}, u32[]{:S(2)}) collective-permute-start(bf16[160,4096]{1,0:T(8,128)(2,1)} %param.7), channel_id=1, source_target_pairs={{960,0},{0,64},{64,128},{128,192},{192,256},{256,320},{320,384},{3... | collective-permute-start | bytes 3932168 | tf_op jit(solution)/shard_map/ppermute | solution.py:14
  16.7 66.2 %collective-permute-start.1 = (bf16[160,4096]{1,0:T(8,128)(2,1)}, bf16[160,4096]{1,0:T(8,128)(2,1)}, u32[]{:S(2)}, u32[]{:S(2)}) collective-permute-start(bf16[160,4096]{1,0:T(8,128)(2,1)} %multiply_convert_fusion), channel_id=1, source_target_pairs={{960,0},{0,64},{64,128},{128,192},{192,256},{256,320},{320,384},{3... | collective-permute-start | bytes 3932168 | tf_op jit(solution)/shard_map/ppermute | solution.py:14
  62.8 1.5 copy-start.2
  65.4 20.1 %copy-start.3 = (bf16[4096,224]{0,1:T(8,128)(2,1)S(1)}, bf16[4096,224]{0,1:T(8,128)(2,1)}, u32[]{:S(2)}) copy-start(bf16[4096,224]{0,1:T(8,128)(2,1)} %param.10) | copy-start | bytes 5505028
  90.8 73.7 %reduce-scatter.5.cloned.1.call-start = ((), (), s32[]{:S(2)}) async-start(), calls=%async_computation.4 | async-start | bytes 2064384 | tf_op jit(solution)/shard_map/reduce_scatter | solution.py:62
Sparse Core Ops, SparseCore 0:
  90.9 19.0 reduce-scatter.2
  113.9 50.5 reduce-scatter.4

commit v2 on v1

v2 whole, which is shorter than its diff:
```python
import functools

import jax
import jax.numpy as jnp
from jax import lax
from jax.experimental import pallas as pl
from jax.experimental.pallas import tpu as pltpu
from jax.sharding import Mesh
from jax.sharding import PartitionSpec as P

D = 4096
HALF = D // 2
HB = 224
SLOTS = 160
CAP = 128
HEAD = 96
TAIL = CAP - HEAD
SPARE = SLOTS - CAP
UP = 256
MARK = 16
FIRST, SECOND = 4, 8
PARTS = 4
BF, F32 = jnp.bfloat16, jnp.float32
VMEM = pl.BlockSpec(memory_space=pltpu.VMEM)
SMEM = pl.BlockSpec(memory_space=pltpu.SMEM)
HBM = pl.BlockSpec(memory_space=pltpu.HBM)


def source_tile(first, second):
    x_hi, x_lo, y = first // 2, first % 2, second
    return (x_lo * 8 + y) * 2 + x_hi


def call(body, outs, scratch=(), room=32, cost=0.0, **more):
    return pl.pallas_call(
        body,
        out_shape=outs,
        scratch_shapes=scratch,
        cost_estimate=pl.CostEstimate(flops=int(cost * 1e10), bytes_accessed=int(cost * 1e6), transcendentals=0),
        compiler_params=pltpu.CompilerParams(vmem_limit_bytes=room * 1024 * 1024),
        **more,
    )


def shape(*dims, kind=BF):
    return jax.ShapeDtypeStruct(dims, kind)


def mm(a, b, dims=((1,), (0,))):
    return lax.dot_general(a, b, (dims, ((), ())), preferred_element_type=F32)


def sorter(core):
    src = lax.broadcasted_iota(jnp.int32, (256, 256), 0)
    dst = lax.broadcasted_iota(jnp.int32, (256, 256), 1)
    lane = dst % 128
    side = jnp.where(dst < 128, core, 1 - core)
    want = (lane // 64) * 128 + side * 64 + lane % 64
    return jnp.where(src == want, 1.0, 0.0).astype(BF)


def column_copies(ref, held, sems):
    copies = []
    for k in range(PARTS):
        at = pl.ds(k * (D // PARTS), D // PARTS)
        copies.append(pltpu.make_async_copy(ref.at[:, at], held.at[:, at], sems.at[k]))
        copies[-1].start()
    return copies


def sorted_tiles(held, perm, copies, scale=None):
    tiles_of = D // 128 // PARTS
    order = sorted(range(HALF // 128), key=lambda k: source_tile(2 * k // SECOND, 2 * k % SECOND + 1))
    here = 0
    for k in order:
        first, second = (2 * k) // SECOND, (2 * k) % SECOND
        one, two = source_tile(first, second), source_tile(first, second + 1)
        while here <= max(one, two) // tiles_of:
            copies[here].wait()
            here += 1
        both = [held[:, t * 128 : (t + 1) * 128] for t in (one, two)]
        if scale is not None:
            both = [(scale * b.astype(F32)).astype(BF) for b in both]
        yield slice(k * 128, (k + 1) * 128), mm(jnp.concatenate(both, axis=1), perm).astype(BF)


def staging(rows):
    return [pltpu.VMEM((rows, D), BF), pltpu.SemaphoreType.DMA((PARTS,))]


def live(len_ref):
    return len_ref[0, 0] + len_ref[0, 1] + len_ref[0, 2] + len_ref[0, 3]


def split_rows(core_ref, len_ref, tok_ref, head_out, rest_out, other_out, held, sems):
    copies = column_copies(tok_ref, held, sems)
    perm = sorter(core_ref[0])
    other_out[SLOTS:, :] = jnp.full((MARK, HALF), live(len_ref), jnp.int32).astype(F32).astype(BF)
    for at, tile in sorted_tiles(held, perm, copies):
        head_out[:, at] = tile[:HEAD, :128]
        rest_out[:, at] = tile[HEAD:, :128]
        other_out[:SLOTS, at] = tile[:, 128:]


def split_down(core_ref, down_ref, down_out, held, sems):
    copies = column_copies(down_ref, held, sems)
    perm = sorter(core_ref[0])
    for at, tile in sorted_tiles(held, perm, copies):
        down_out[:, at] = tile[:, :128]


def split_wide(core_ref, gate_ref, up_ref, wide_out, held, sems, held_up, sems_up):
    copies = column_copies(gate_ref, held, sems)
    copies_up = column_copies(up_ref, held_up, sems_up)
    perm = sorter(core_ref[0])
    wide_out[HB:UP, :] = jnp.zeros((UP - HB, HALF), BF)
    wide_out[UP + HB :, :] = jnp.zeros((UP - HB, HALF), BF)
    for at, tile in sorted_tiles(held, perm, copies):
        wide_out[:HB, at] = tile[:, :128]
    for at, tile in sorted_tiles(held_up, perm, copies_up):
        wide_out[UP : UP + HB, at] = tile[:, :128]


def split_cot(core_ref, len_ref, rew_ref, cot_ref, own_out, other_out, held, sems):
    copies = column_copies(cot_ref, held, sems)
    perm = sorter(core_ref[0])
    row = lax.broadcasted_iota(jnp.int32, (SLOTS, 1), 0)
    weight, start = jnp.zeros((SLOTS, 1), F32), jnp.int32(0)
    for j in range(4):
        end = start + len_ref[0, j]
        scaled = jnp.full((SLOTS, 1), rew_ref[0, j], jnp.int32).astype(F32) / 65536.0
        weight += jnp.where((row >= start) & (row < end), scaled, 0.0)
        start = end
    for at, tile in sorted_tiles(held, perm, copies, weight):
        own_out[:, at] = tile[:, :128]
        other_out[:SLOTS, at] = tile[:, 128:]
    other_out[SLOTS:, :] = jnp.full((MARK, HALF), live(len_ref), jnp.int32).astype(F32).astype(BF)


def merged(tail, surplus, count):
    slot = lax.broadcasted_iota(jnp.int32, (TAIL, TAIL + SPARE), 0)
    src = lax.broadcasted_iota(jnp.int32, (TAIL, TAIL + SPARE), 1)
    want = jnp.where(HEAD + slot < count, slot, TAIL + slot - jnp.maximum(count - HEAD, 0))
    pick = jnp.where(src == want, 1.0, 0.0).astype(BF)
    return mm(pick, jnp.concatenate([tail, surplus], axis=0)).astype(BF)


def other_count(ref):
    mark = ref[SLOTS : SLOTS + MARK, :128].astype(F32)
    return mark[:1, : TAIL + SPARE].astype(jnp.int32)


def merge_rows(len_ref, rest_ref, got_ref, out_ref):
    rest, got = rest_ref[...], got_ref[:SLOTS, :]
    out_ref[:TAIL, :] = merged(rest[:TAIL], got[CAP:], live(len_ref))
    out_ref[TAIL : TAIL + HEAD, :] = got[:HEAD]
    out_ref[TAIL + HEAD :, :] = merged(got[HEAD:CAP], rest[TAIL:], other_count(got_ref))


def near_terms(
    len_ref, head_ref, tail_ref, far_head_ref, own_ref, got_ref, wide_ref, down_ref, cot_out, sum_out
):
    own, got = own_ref[...], got_ref[:SLOTS, :]
    cot_out[:HEAD, :] = own[:HEAD]
    cot_out[HEAD:CAP, :] = merged(own[HEAD:CAP], got[CAP:], live(len_ref))
    cot_out[CAP : CAP + HEAD, :] = got[:HEAD]
    cot_out[CAP + HEAD :, :] = merged(got[HEAD:CAP], own[CAP:], other_count(got_ref))
    rows = jnp.concatenate([head_ref[...], tail_ref[...], far_head_ref[...]], axis=0)
    sum_out[:, : 2 * UP] = mm(rows, wide_ref[...], ((1,), (1,)))
    sum_out[: 2 * CAP, 2 * UP : 2 * UP + HB] = mm(cot_out[...], down_ref[...], ((1,), (1,)))
    sum_out[: 2 * CAP, 2 * UP + HB :] = jnp.zeros((2 * CAP, UP - HB), F32)
    sum_out[2 * CAP :, 2 * UP :] = jnp.zeros((HEAD, UP), F32)


def next_back(cot_ref, down_ref, out_ref):
    out_ref[...] = mm(cot_ref[...], down_ref[...], ((1,), (1,))).astype(out_ref.dtype)


def far_terms(tail_ref, wide_ref, out_ref):
    out_ref[...] = mm(tail_ref[...], wide_ref[...], ((1,), (1,))).astype(out_ref.dtype)


def swapped(value):
    return jnp.concatenate([value[CAP:], value[:CAP]], axis=0)


def hidden_grads(gate, up, back):
    sig = jax.nn.sigmoid(gate)
    gate_back = back * up * sig * (1.0 + gate * (1.0 - sig))
    return gate_back.astype(BF), (back * (gate * sig)).astype(BF)


def near_grads(mine_ref, other_ref, gate_out, up_out, early_out):
    total = mine_ref[: 2 * CAP] + swapped(other_ref[: 2 * CAP])
    gate_out[...], up_out[...] = hidden_grads(
        total[:, :HB], total[:, UP : UP + HB], total[:, 2 * UP : 2 * UP + HB]
    )
    early_out[...] = jnp.zeros_like(early_out)
    early_out[:HEAD] = mine_ref[2 * CAP :, : 2 * UP]
    early_out[CAP : CAP + HEAD] = other_ref[2 * CAP :, : 2 * UP]


def weight_grads(
    early_ref, mine_ref, other_ref, back_ref, cross_ref, gate_ref, up_ref,
    head_ref, tail_ref, far_head_ref, far_tail_ref, out_ref, gate_all, up_all,
):
    @pl.when(pl.program_id(0) == 0)
    def _():
        mine, other = mine_ref[...].astype(F32), other_ref[...].astype(F32)
        early = early_ref[...]
        total = jnp.concatenate(
            [
                early[:HEAD] + other[TAIL : TAIL + HEAD],
                mine[:TAIL] + other[TAIL + HEAD :],
                early[CAP : CAP + HEAD] + mine[TAIL : TAIL + HEAD],
                mine[TAIL + HEAD :] + other[:TAIL],
            ],
            axis=0,
        )
        back = back_ref[...].astype(F32) + swapped(cross_ref[...].astype(F32))
        gate_all[2 * CAP :], up_all[2 * CAP :] = hidden_grads(
            total[:, :HB], total[:, UP : UP + HB], back
        )
        gate_all[: 2 * CAP] = gate_ref[...]
        up_all[: 2 * CAP] = up_ref[...]

    rows = jnp.concatenate(
        [head_ref[...], tail_ref[...], far_head_ref[...], far_tail_ref[...]], axis=0
    )
    out_ref[0, :HB] = mm(gate_all[...], rows, ((0,), (0,))).astype(BF)
    out_ref[0, HB:] = mm(up_all[...], rows, ((0,), (0,))).astype(BF)


def first_sum(in_ref, out_ref):
    total = in_ref[0].astype(F32)
    for k in range(1, FIRST):
        total += in_ref[k].astype(F32)
    lane = lax.broadcasted_iota(jnp.int32, (HB, 128), 1)
    for k in range(SECOND // 2):
        gate = total[:HB, k * 128 : (k + 1) * 128]
        up = total[HB:, k * 128 : (k + 1) * 128]
        out_ref[2 * k] = jnp.where(lane < 64, gate, pltpu.roll(up, 64, 1)).astype(BF)
        out_ref[2 * k + 1] = jnp.where(lane < 64, pltpu.roll(gate, 64, 1), up).astype(BF)


def second_sum(in_ref, gate_out, up_out):
    total = in_ref[0].astype(F32)
    for k in range(1, SECOND):
        total += in_ref[k].astype(F32)
    full = jnp.concatenate([total, jnp.zeros((UP - HB, 128), F32)], axis=0).T
    gate_out[...] = full[:64, :HB]
    up_out[...] = full[64:, :HB]


def along_z(block, distance):
    n = lax.axis_size("z")
    return lax.ppermute(block, "z", [(i, (i + distance) % n) for i in range(n)])


def between_cores(block):
    return lax.ppermute(block, "c", [(0, 1), (1, 0)])


def along_z_crossed(block):
    n = lax.axis_size("z")
    route = [(2 * i + c, 2 * ((i + 1) % n) + 1 - c) for i in range(n) for c in range(2)]
    return lax.ppermute(block, ("z", "c"), route)


def on_device(tokens, cotangent, gate_weight, up_weight, down_weight, lengths, rewards):
    core = lax.axis_index("c").astype(jnp.int32).reshape(1)
    head, rest, row_other = call(
        split_rows,
        (shape(HEAD, HALF), shape(SLOTS - HEAD, HALF), shape(SLOTS + MARK, HALF)),
        in_specs=[SMEM, SMEM, HBM], scratch=staging(SLOTS), cost=1.7,
    )(core, lengths, tokens)
    far_head = along_z(head, 1)
    row_got = between_cores(row_other)
    down = call(
        split_down, shape(HB, HALF), in_specs=[SMEM, HBM], scratch=staging(HB), cost=1.4,
    )(core, down_weight)
    next_down = along_z(down, -1)
    cot_own, cot_other = call(
        split_cot,
        (shape(SLOTS, HALF), shape(SLOTS + MARK, HALF)),
        in_specs=[SMEM, SMEM, SMEM, HBM], scratch=staging(SLOTS), cost=1.8,
    )(core, lengths, rewards, cotangent)
    cot_got = between_cores(cot_other)
    tail = call(
        merge_rows, shape(CAP + TAIL, HALF), cost=0.8,
                in_specs=[SMEM, VMEM, VMEM],
    )(lengths, rest, row_got)
    far_tail = along_z(tail, 1)

    wide = call(
        split_wide, shape(2 * UP, HALF), in_specs=[SMEM, HBM, HBM], scratch=staging(HB) * 2, cost=2.7,
    )(core, gate_weight.T, up_weight.T)
    cot_rows, near = call(
        near_terms,
        (shape(2 * CAP, HALF), shape(2 * CAP + HEAD, 3 * UP, kind=F32)),
        cost=2.3, in_specs=[SMEM] + [VMEM] * 7,
    )(lengths, head, tail, far_head, cot_own, cot_got, wide, down)
    near_other = between_cores(near)
    back = call(
        next_back, shape(2 * CAP, HB), cost=0.5,
                in_specs=[VMEM] * 2,
    )(cot_rows, next_down)
    far_back, far_cross = along_z(back, 1), along_z_crossed(back)
    gate_near, up_near, early = call(
        near_grads,
        (shape(2 * CAP, HB), shape(2 * CAP, HB), shape(2 * CAP, 2 * UP, kind=F32)),
        cost=0.3, in_specs=[VMEM] * 2,
    )(near, near_other)
    far = call(
        far_terms, shape(CAP + TAIL, 2 * UP), cost=0.8, in_specs=[VMEM] * 2
    )(far_tail, wide)
    far_other = between_cores(far)

    cols = HALF // FIRST
    whole = lambda *dims: pl.BlockSpec(dims, lambda i: (0,) * len(dims))
    part = lambda rows: pl.BlockSpec((rows, cols), lambda i: (0, i))
    grads = call(
        weight_grads, shape(FIRST, 2 * HB, cols),
                scratch=[pltpu.VMEM((4 * CAP, HB), BF)] * 2, cost=2.1,
        grid=(FIRST,),
        in_specs=[whole(2 * CAP, 2 * UP)] + [whole(CAP + TAIL, 2 * UP)] * 2 + [whole(2 * CAP, HB)] * 4
        + [part(HEAD), part(CAP + TAIL)] * 2,
        out_specs=pl.BlockSpec((1, 2 * HB, cols), lambda i: (i, 0, 0)),
    )(early, far, far_other, far_back, far_cross, gate_near, up_near, head, tail, far_head, far_tail)
    grads = lax.all_to_all(grads, ("xh", "xl"), split_axis=0, concat_axis=0, tiled=True)
    grads = call(
        first_sum, shape(SECOND, HB, 128), cost=0.4,
    )(grads)
    grads = lax.all_to_all(grads, "y", split_axis=0, concat_axis=0, tiled=True)
    return call(
        second_sum, (shape(64, HB, kind=F32), shape(64, HB, kind=F32)),
                in_specs=[VMEM],
    )(grads)


def solution(mesh):
    planes = mesh.shape["blk"]
    fine = Mesh(mesh.devices.reshape(planes, 2, 8, 2, 2), ("z", "xl", "y", "xh", "c"))
    rows = P(("z", "xl", "y", "xh", "c"), None)
    placed = (rows, rows, P(None, "z"), P(None, "z"), P("z", None), rows, rows)
    out = P(("xl", "y", "xh", "c"), "z")
    return jax.shard_map(
        on_device, mesh=fine, in_specs=placed, out_specs=(out, out), check_vma=False
    )
```

time: 184 us -> 117 us (0.64)
  the two profiles are of different devices: /device:TPU:24 before, /device:TPU:1 now
where the time goes in v2:
time: 117 us; the launch traced here: 116 us
  blocking collectives  47.8 us (41%)
  starting transfers between devices  37.3 us (32%)
  Pallas kernels  15.1 us (13%)
  waiting for transfers between devices  12.9 us (11%)
  local copies, waits for them, and re-layouts  2 us (2%)
    all_to_all x1, blocking collectives, on_device(): lax.all_to_all(grads, ('xh', 'xl'), split_axis=0, concat_axis=0, tiled=True)  27 us
    ppermute x4, starting transfers between devices, between_cores(): return lax.ppermute(block, 'c', [(0, 1), (1, 0)])  24.2 us
    all_to_all x1, blocking collectives, on_device(): grads = lax.all_to_all(grads, 'y', split_axis=0, concat_axis=0, tiled=True)  20.9 us
    ppermute x4, starting transfers between devices, along_z(): return lax.ppermute(block, 'z', [(i, (i + distance) % n) for i in range(n)])  11.2 us
    ppermute x4, waiting for transfers between devices, along_z(): return lax.ppermute(block, 'z', [(i, (i + distance) % n) for i in range(n)])  9.09 us
    ppermute x1, waiting for transfers between devices, along_z_crossed(): return lax.ppermute(block, ('z', 'c'), route)  3.83 us
    pallas_call x1, Pallas kernels, on_device(): call(split_wide, shape(2 * UP, HALF), in_specs=[SMEM, HBM, HBM], scratch=...  2.74 us
  transfers between devices with their start and end apart: 9, of which 2 were waited for; matrix products, arithmetic and copies ran while one was open for 0% of the time, Pallas kernels for 9%

profile of v2, /device:TPU:1, one launch (start us, length us, event | category | flops | bytes accessed | tf_op | source)
XLA Modules:
  0.0 116.1 jit_solution(13513459043065807839)
XLA Ops:
  0.6 1.3 %copy-done.3 = bf16[160,4096]{1,0:T(8,128)(2,1)S(1)} copy-done((bf16[160,4096]{1,0:T(8,128)(2,1)S(1)}, bf16[160,4096]{1,0:T(8,128)(2,1)}, u32[]{:S(2)}) %copy-start.3) | copy-done | bytes 1310744
  2.0 0.7 copy-done.6
  2.6 1.7 %shard_map.86 = (bf16[96,2048]{1,0:T(8,128)(2,1)S(1)}, bf16[64,2048]{1,0:T(8,128)(2,1)S(1)}, bf16[176,2048]{1,0:T(8,128)(2,1)S(1)}) custom-call(s32[1]{0:T(128)} %bitcast.core_ref, s32[1,4]{1,0:T(1,128)S(1)} %copy-done.6, bf16[160,4096]{1,0:T(8,128)(2,1)S(1)} %copy-done.3), custom_call_target="tpu_custom_call" | custom-call | flops 16999999488 | bytes 1700000 | tf_op jit(solution)/shard_map/pallas_call | solution.py:272
  4.4 16.1 %collective-permute-start = (bf16[176,2048]{1,0:T(8,128)(2,1)S(1)}, bf16[176,2048]{1,0:T(8,128)(2,1)S(1)}, u32[]{:S(2)}, u32[]{:S(2)}) collective-permute-start(bf16[176,2048]{1,0:T(8,128)(2,1)S(1)} %get-tuple-element.14), channel_id=1, source_target_pairs={{0,1},{1,0},{2,3},{3,2},{4,5},{5,4},{6,7},{7,6},{8,9},{9,8},{10,11... | collective-permute-start | bytes 2162696 | tf_op jit(solution)/shard_map/ppermute | solution.py:261
  20.4 0.0 copy-start
  20.4 2.1 %collective-permute-start.1 = (bf16[96,2048]{1,0:T(8,128)(2,1)S(1)}, bf16[96,2048]{1,0:T(8,128)(2,1)S(1)}, u32[]{:S(2)}, u32[]{:S(2)}) collective-permute-start(bf16[96,2048]{1,0:T(8,128)(2,1)S(1)} %get-tuple-element.12.head_ref), channel_id=1, source_target_pairs={{0,64},{64,128},{128,192},{192,256},{256,320},{320,384},{384,448},... | collective-permute-start | bytes 1179656 | tf_op jit(solution)/shard_map/ppermute | solution.py:257
  22.5 1.8 %shard_map.88 = (bf16[160,2048]{1,0:T(8,128)(2,1)S(1)}, bf16[176,2048]{1,0:T(8,128)(2,1)S(1)}) custom-call(s32[1]{0:T(128)} %bitcast.core_ref, s32[1,4]{1,0:T(1,128)S(1)} %copy-done.6, s32[1,4]{1,0:T(1,128)S(1)} %copy-done.5, bf16[160,4096]{1,0:T(8,128)(2,1)S(1)} %copy-done.4), custom_call_target="tpu_custom_call" | custom-call | flops 17999998976 | bytes 1800000 | tf_op jit(solution)/shard_map/pallas_call | solution.py:283
  24.4 0.0 copy-start.1
  24.4 0.0 copy-start.2
  24.4 2.2 %collective-permute-start.2 = (bf16[176,2048]{1,0:T(8,128)(2,1)S(1)}, bf16[176,2048]{1,0:T(8,128)(2,1)S(1)}, u32[]{:S(2)}, u32[]{:S(2)}) collective-permute-start(bf16[176,2048]{1,0:T(8,128)(2,1)S(1)} %get-tuple-element.16), channel_id=1, source_target_pairs={{0,1},{1,0},{2,3},{3,2},{4,5},{5,4},{6,7},{7,6},{8,9},{9,8},{10,11... | collective-permute-start | bytes 2162696 | tf_op jit(solution)/shard_map/ppermute | solution.py:261
  26.6 1.4 %shard_map.90.down_ref = bf16[224,2048]{1,0:T(8,128)(2,1)S(1)} custom-call(s32[1]{0:T(128)} %bitcast.core_ref, bf16[224,4096]{1,0:T(8,128)(2,1)S(1)} %copy-done), custom_call_target="tpu_custom_call" | custom-call | flops 14000000000 | bytes 1400000 | tf_op jit(solution)/shard_map/pallas_call | solution.py:279
  28.0 5.3 %collective-permute-start.6 = (bf16[224,2048]{1,0:T(8,128)(2,1)S(1)}, bf16[224,2048]{1,0:T(8,128)(2,1)S(1)}, u32[]{:S(2)}, u32[]{:S(2)}) collective-permute-start(bf16[224,2048]{1,0:T(8,128)(2,1)S(1)} %shard_map.90.down_ref), channel_id=1, source_target_pairs={{0,960},{64,0},{128,64},{192,128},{256,192},{320,256},{384,320},{4... | collective-permute-start | bytes 2752520 | tf_op jit(solution)/shard_map/ppermute | solution.py:257
  33.3 0.0 copy-start.7
  33.3 2.7 %shard_map.89.wide_ref = bf16[512,2048]{1,0:T(8,128)(2,1)S(1)} custom-call(s32[1]{0:T(128)} %bitcast.core_ref, bf16[224,4096]{1,0:T(8,128)(2,1)S(1)} %bitcast.3, bf16[224,4096]{1,0:T(8,128)(2,1)S(1)} %bitcast.4), custom_call_target="tpu_custom_call" | custom-call | flops 27000000512 | bytes 2700000 | tf_op jit(solution)/shard_map/pallas_call | solution.py:295
  36.1 0.8 shard_map.87.tail_ref
  36.9 1.9 %collective-permute-start.4 = (bf16[160,2048]{1,0:T(8,128)(2,1)S(1)}, bf16[160,2048]{1,0:T(8,128)(2,1)S(1)}, u32[]{:S(2)}, u32[]{:S(2)}) collective-permute-start(bf16[160,2048]{1,0:T(8,128)(2,1)S(1)} %shard_map.87.tail_ref), channel_id=1, source_target_pairs={{0,64},{64,128},{128,192},{192,256},{256,320},{320,384},{384,448},... | collective-permute-start | bytes 1966088 | tf_op jit(solution)/shard_map/ppermute | solution.py:257
  38.8 0.0 collective-permute-done.2.got_ref
  38.8 1.9 %shard_map.91 = (bf16[256,2048]{1,0:T(8,128)(2,1)S(1)}, f32[352,768]{1,0:T(8,128)S(1)}) custom-call(s32[1,4]{1,0:T(1,128)S(1)} %copy-done.7, bf16[96,2048]{1,0:T(8,128)(2,1)S(1)} %get-tuple-element.12.head_ref, bf16[160,2048]{1,0:T(8,128)(2,1)S(1)} %shard_map.87.tail_ref, bf16[96,2048]{1,0:T(8,128)(2,1)S(1)} %collective-permute-done.1.far_head_ref, ...), custom_call_target="tpu_custom_call" | custom-call | flops 23000000512 | bytes 2300000 | tf_op jit(solution)/shard_map/pallas_call | solution.py:298
  40.7 2.7 %collective-permute-start.3 = (f32[352,768]{1,0:T(8,128)S(1)}, f32[352,768]{1,0:T(8,128)S(1)}, u32[]{:S(2)}, u32[]{:S(2)}) collective-permute-start(f32[352,768]{1,0:T(8,128)S(1)} %get-tuple-element.17.mine_ref), channel_id=1, source_target_pairs={{0,1},{1,0},{2,3},{3,2},{4,5},{5,4},{6,7},{7,6},{8,9},{9,8},{10,11... | collective-permute-start | bytes 3244040 | tf_op jit(solution)/shard_map/ppermute | solution.py:261
  43.4 9.1 %collective-permute-done.6.down_ref = bf16[224,2048]{1,0:T(8,128)(2,1)S(1)} collective-permute-done((bf16[224,2048]{1,0:T(8,128)(2,1)S(1)}, bf16[224,2048]{1,0:T(8,128)(2,1)S(1)}, u32[]{:S(2)}, u32[]{:S(2)}) %collective-permute-start.6) | collective-permute-done | bytes 917536 | tf_op jit(solution)/shard_map/ppermute | solution.py:257
  52.5 0.5 shard_map.94
  53.0 1.9 %collective-permute-start.7 = (bf16[256,224]{1,0:T(8,128)(2,1)S(1)}, bf16[256,224]{1,0:T(8,128)(2,1)S(1)}, u32[]{:S(2)}, u32[]{:S(2)}) collective-permute-start(bf16[256,224]{1,0:T(8,128)(2,1)S(1)} %shard_map.94), channel_id=1, source_target_pairs={{0,64},{64,128},{128,192},{192,256},{256,320},{320,384},{384,448},... | collective-permute-start | bytes 344072 | tf_op jit(solution)/shard_map/ppermute | solution.py:257
  54.9 1.9 %collective-permute-start.8 = (bf16[256,224]{1,0:T(8,128)(2,1)S(1)}, bf16[256,224]{1,0:T(8,128)(2,1)S(1)}, u32[]{:S(2)}, u32[]{:S(2)}) collective-permute-start(bf16[256,224]{1,0:T(8,128)(2,1)S(1)} %shard_map.94), channel_id=1, source_target_pairs={{0,65},{1,64},{64,129},{65,128},{128,193},{129,192},{192,257},{193... | collective-permute-start | bytes 344072 | tf_op jit(solution)/shard_map/ppermute | solution.py:267
  56.8 0.8 shard_map.93.mine_ref
  57.7 3.2 %collective-permute-start.5 = (bf16[160,512]{1,0:T(8,128)(2,1)S(1)}, bf16[160,512]{1,0:T(8,128)(2,1)S(1)}, u32[]{:S(2)}, u32[]{:S(2)}) collective-permute-start(bf16[160,512]{1,0:T(8,128)(2,1)S(1)} %shard_map.93.mine_ref), channel_id=1, source_target_pairs={{0,1},{1,0},{2,3},{3,2},{4,5},{5,4},{6,7},{7,6},{8,9},{9,8},{10,11... | collective-permute-start | bytes 491528 | tf_op jit(solution)/shard_map/ppermute | solution.py:261
  60.9 0.2 shard_map.92
  61.1 3.8 %collective-permute-done.8.cross_ref = bf16[256,224]{1,0:T(8,128)(2,1)S(1)} collective-permute-done((bf16[256,224]{1,0:T(8,128)(2,1)S(1)}, bf16[256,224]{1,0:T(8,128)(2,1)S(1)}, u32[]{:S(2)}, u32[]{:S(2)}) %collective-permute-start.8) | collective-permute-done | bytes 114720 | tf_op jit(solution)/shard_map/ppermute | solution.py:267
  65.0 2.2 %shard_map.95 = bf16[4,448,512]{2,1,0:T(8,128)(2,1)S(1)} custom-call(f32[256,512]{1,0:T(8,128)S(1)} %get-tuple-element.18.early_ref, bf16[160,512]{1,0:T(8,128)(2,1)S(1)} %shard_map.93.mine_ref, bf16[160,512]{1,0:T(8,128)(2,1)S(1)} %collective-permute-done.5.other_ref, bf16[256,224]{1,0:T(8,128)(2,1)S(1)} %collective-permute-done.7.back_ref, ...), custom_call_target="tpu_custom_call" | custom-call | flops 20999999488 | bytes 2100000 | tf_op jit(solution)/shard_map/pallas_call | solution.py:322
  67.1 27.0 %all_to_all.10.in_ref = bf16[4,448,512]{2,1,0:T(8,128)(2,1)S(1)} all-to-all(bf16[4,448,512]{2,1,0:T(8,128)(2,1)S(1)} %shard_map.95), channel_id=1, replica_groups=mesh['z'=16,'xl'=2,'y'=8,'xh'=2,'c'=2] {'xh','xl'}, dimensions={0} | all-to-all | bytes 3670016 | tf_op jit(solution)/shard_map/all_to_all | solution.py:330
  94.1 0.3 shard_map.96
  94.5 20.9 %all_to_all.11.in_ref = bf16[8,224,128]{2,1,0:T(8,128)(2,1)S(1)} all-to-all(bf16[8,224,128]{2,1,0:T(8,128)(2,1)S(1)} %shard_map.96), channel_id=1, replica_groups=mesh['z'=16,'xl'=2,'y'=8,'xh'=2,'c'=2] {'y'}, dimensions={0} | all-to-all | bytes 917504 | tf_op jit(solution)/shard_map/all_to_all | solution.py:334
  115.3 0.8 shard_map.97
  (16 shorter events, 0.0 us)
Async XLA Ops:
  0.6 1.3 %copy-start.3 = (bf16[160,4096]{1,0:T(8,128)(2,1)S(1)}, bf16[160,4096]{1,0:T(8,128)(2,1)}, u32[]{:S(2)}) copy-start(bf16[160,4096]{1,0:T(8,128)(2,1)} %tok_ref.1) | copy-start | bytes 3932164
  2.0 0.7 copy-start.6
  2.6 19.9 %copy-start.4 = (bf16[160,4096]{1,0:T(8,128)(2,1)S(1)}, bf16[160,4096]{1,0:T(8,128)(2,1)}, u32[]{:S(2)}) copy-start(bf16[160,4096]{1,0:T(8,128)(2,1)} %cot_ref.1) | copy-start | bytes 3932164
  2.6 19.9 %copy-start.5 = (s32[1,4]{1,0:T(1,128)S(1)}, s32[1,4]{1,0:T(1,128)}, u32[]{:S(2)}) copy-start(s32[1,4]{1,0:T(1,128)} %rew_ref.1) | copy-start | bytes 52
  4.4 31.7 %collective-permute-start = (bf16[176,2048]{1,0:T(8,128)(2,1)S(1)}, bf16[176,2048]{1,0:T(8,128)(2,1)S(1)}, u32[]{:S(2)}, u32[]{:S(2)}) collective-permute-start(bf16[176,2048]{1,0:T(8,128)(2,1)S(1)} %get-tuple-element.14), channel_id=1, source_target_pairs={{0,1},{1,0},{2,3},{3,2},{4,5},{5,4},{6,7},{7,6},{8,9},{9,8},{10,11... | collective-permute-start | bytes 2162696 | tf_op jit(solution)/shard_map/ppermute | solution.py:261
  20.4 6.2 %copy-start = (bf16[224,4096]{1,0:T(8,128)(2,1)S(1)}, bf16[224,4096]{1,0:T(8,128)(2,1)}, u32[]{:S(2)}) copy-start(bf16[224,4096]{1,0:T(8,128)(2,1)} %down_ref.1) | copy-start | bytes 5505028
  20.4 18.4 %collective-permute-start.1 = (bf16[96,2048]{1,0:T(8,128)(2,1)S(1)}, bf16[96,2048]{1,0:T(8,128)(2,1)S(1)}, u32[]{:S(2)}, u32[]{:S(2)}) collective-permute-start(bf16[96,2048]{1,0:T(8,128)(2,1)S(1)} %get-tuple-element.12.head_ref), channel_id=1, source_target_pairs={{0,64},{64,128},{128,192},{192,256},{256,320},{320,384},{384,448},... | collective-permute-start | bytes 1179656 | tf_op jit(solution)/shard_map/ppermute | solution.py:257
  24.4 8.9 %copy-start.1 = (bf16[4096,224]{0,1:T(8,128)(2,1)S(1)}, bf16[4096,224]{0,1:T(8,128)(2,1)}, u32[]{:S(2)}) copy-start(bf16[4096,224]{0,1:T(8,128)(2,1)} %param.9) | copy-start | bytes 5505028
  24.4 8.9 %copy-start.2 = (bf16[4096,224]{0,1:T(8,128)(2,1)S(1)}, bf16[4096,224]{0,1:T(8,128)(2,1)}, u32[]{:S(2)}) copy-start(bf16[4096,224]{0,1:T(8,128)(2,1)} %param.10) | copy-start | bytes 5505028
  24.4 14.4 %collective-permute-start.2 = (bf16[176,2048]{1,0:T(8,128)(2,1)S(1)}, bf16[176,2048]{1,0:T(8,128)(2,1)S(1)}, u32[]{:S(2)}, u32[]{:S(2)}) collective-permute-start(bf16[176,2048]{1,0:T(8,128)(2,1)S(1)} %get-tuple-element.16), channel_id=1, source_target_pairs={{0,1},{1,0},{2,3},{3,2},{4,5},{5,4},{6,7},{7,6},{8,9},{9,8},{10,11... | collective-permute-start | bytes 2162696 | tf_op jit(solution)/shard_map/ppermute | solution.py:261
  28.0 24.5 %collective-permute-start.6 = (bf16[224,2048]{1,0:T(8,128)(2,1)S(1)}, bf16[224,2048]{1,0:T(8,128)(2,1)S(1)}, u32[]{:S(2)}, u32[]{:S(2)}) collective-permute-start(bf16[224,2048]{1,0:T(8,128)(2,1)S(1)} %shard_map.90.down_ref), channel_id=1, source_target_pairs={{0,960},{64,0},{128,64},{192,128},{256,192},{320,256},{384,320},{4... | collective-permute-start | bytes 2752520 | tf_op jit(solution)/shard_map/ppermute | solution.py:257
  33.3 2.8 %copy-start.7 = (s32[1,4]{1,0:T(1,128)S(1)}, s32[1,4]{1,0:T(1,128)}, u32[]{:S(2)}) copy-start(s32[1,4]{1,0:T(1,128)} %len_ref.7) | copy-start | bytes 52
  36.9 19.9 %collective-permute-start.4 = (bf16[160,2048]{1,0:T(8,128)(2,1)S(1)}, bf16[160,2048]{1,0:T(8,128)(2,1)S(1)}, u32[]{:S(2)}, u32[]{:S(2)}) collective-permute-start(bf16[160,2048]{1,0:T(8,128)(2,1)S(1)} %shard_map.87.tail_ref), channel_id=1, source_target_pairs={{0,64},{64,128},{128,192},{192,256},{256,320},{320,384},{384,448},... | collective-permute-start | bytes 1966088 | tf_op jit(solution)/shard_map/ppermute | solution.py:257
  40.7 20.2 %collective-permute-start.3 = (f32[352,768]{1,0:T(8,128)S(1)}, f32[352,768]{1,0:T(8,128)S(1)}, u32[]{:S(2)}, u32[]{:S(2)}) collective-permute-start(f32[352,768]{1,0:T(8,128)S(1)} %get-tuple-element.17.mine_ref), channel_id=1, source_target_pairs={{0,1},{1,0},{2,3},{3,2},{4,5},{5,4},{6,7},{7,6},{8,9},{9,8},{10,11... | collective-permute-start | bytes 3244040 | tf_op jit(solution)/shard_map/ppermute | solution.py:261
  53.0 8.2 %collective-permute-start.7 = (bf16[256,224]{1,0:T(8,128)(2,1)S(1)}, bf16[256,224]{1,0:T(8,128)(2,1)S(1)}, u32[]{:S(2)}, u32[]{:S(2)}) collective-permute-start(bf16[256,224]{1,0:T(8,128)(2,1)S(1)} %shard_map.94), channel_id=1, source_target_pairs={{0,64},{64,128},{128,192},{192,256},{256,320},{320,384},{384,448},... | collective-permute-start | bytes 344072 | tf_op jit(solution)/shard_map/ppermute | solution.py:257
  54.9 10.1 %collective-permute-start.8 = (bf16[256,224]{1,0:T(8,128)(2,1)S(1)}, bf16[256,224]{1,0:T(8,128)(2,1)S(1)}, u32[]{:S(2)}, u32[]{:S(2)}) collective-permute-start(bf16[256,224]{1,0:T(8,128)(2,1)S(1)} %shard_map.94), channel_id=1, source_target_pairs={{0,65},{1,64},{64,129},{65,128},{128,193},{129,192},{192,257},{193... | collective-permute-start | bytes 344072 | tf_op jit(solution)/shard_map/ppermute | solution.py:267
  57.7 7.3 %collective-permute-start.5 = (bf16[160,512]{1,0:T(8,128)(2,1)S(1)}, bf16[160,512]{1,0:T(8,128)(2,1)S(1)}, u32[]{:S(2)}, u32[]{:S(2)}) collective-permute-start(bf16[160,512]{1,0:T(8,128)(2,1)S(1)} %shard_map.93.mine_ref), channel_id=1, source_target_pairs={{0,1},{1,0},{2,3},{3,2},{4,5},{5,4},{6,7},{7,6},{8,9},{9,8},{10,11... | collective-permute-start | bytes 491528 | tf_op jit(solution)/shard_map/ppermute | solution.py:261

commit v3 on v2

v3 whole, which is shorter than its diff:
```python
import functools

import jax
import jax.numpy as jnp
from jax import lax
from jax.experimental import pallas as pl
from jax.experimental.pallas import tpu as pltpu
from jax.sharding import Mesh
from jax.sharding import PartitionSpec as P

D = 4096
HALF = D // 2
HB = 224
SLOTS = 160
CAP = 128
HEAD = 96
TAIL = CAP - HEAD
SPARE = SLOTS - CAP
UP = 256
MARK = 16
HH = HB // 2
FIRST, SECOND = 8, 4
ABREAST = 2
BF, F32 = jnp.bfloat16, jnp.float32
VMEM = pl.BlockSpec(memory_space=pltpu.VMEM)
SMEM = pl.BlockSpec(memory_space=pltpu.SMEM)
ANY = pl.BlockSpec(memory_space=pl.ANY)


def source_tile(first, second):
    x_hi, x_lo, y = first // 4, first // 2 % 2, 2 * second + first % 2
    return (x_lo * 8 + y) * 2 + x_hi


def call(body, outs, scratch=(), room=32, cost=0.0, **more):
    return pl.pallas_call(
        body,
        out_shape=outs,
        scratch_shapes=scratch,
        cost_estimate=pl.CostEstimate(flops=int(cost * 1e10), bytes_accessed=int(cost * 1e6), transcendentals=0),
        compiler_params=pltpu.CompilerParams(vmem_limit_bytes=room * 1024 * 1024),
        **more,
    )


def shape(*dims, kind=BF):
    return jax.ShapeDtypeStruct(dims, kind)


def mm(a, b, dims=((1,), (0,))):
    return lax.dot_general(a, b, (dims, ((), ())), preferred_element_type=F32)


def sorter(core):
    src = lax.broadcasted_iota(jnp.int32, (256, 256), 0)
    dst = lax.broadcasted_iota(jnp.int32, (256, 256), 1)
    lane = dst % 128
    side = jnp.where(dst < 128, core, 1 - core)
    want = (lane // 64) * 128 + side * 64 + lane % 64
    return jnp.where(src == want, 1.0, 0.0).astype(BF)


def sorted_tiles(ref, perm):
    for k in range(HALF // 128):
        first, second = (2 * k) // SECOND, (2 * k) % SECOND
        both = [
            ref[:, t * 128 : (t + 1) * 128]
            for t in (source_tile(first, second), source_tile(first, second + 1))
        ]
        yield slice(k * 128, (k + 1) * 128), mm(jnp.concatenate(both, axis=1), perm).astype(BF)


def mark(len_ref, columns):
    return jnp.full((MARK, columns), live(len_ref), jnp.int32).astype(F32).astype(BF)


def live(len_ref):
    return len_ref[0, 0] + len_ref[0, 1] + len_ref[0, 2] + len_ref[0, 3]


def split_rows(core_ref, len_ref, tok_ref, head_out, rest_out, other_out):
    perm = sorter(core_ref[0])
    other_out[SLOTS:, :] = mark(len_ref, HALF)
    for at, tile in sorted_tiles(tok_ref, perm):
        head_out[:, at] = tile[:HEAD, :128]
        rest_out[:, at] = tile[HEAD:, :128]
        other_out[:SLOTS, at] = tile[:, 128:]


def split_wide(core_ref, gate_ref, up_ref, after_ref, wide_out):
    perm = sorter(core_ref[0])
    wide_out[HB:UP, :] = jnp.zeros((UP - HB, HALF), BF)
    wide_out[UP + HB :, :] = jnp.zeros((UP - HB, HALF), BF)
    for at, tile in sorted_tiles(gate_ref, perm):
        wide_out[:HB, at] = tile[:, :128]
    for at, tile in sorted_tiles(up_ref, perm):
        wide_out[UP : UP + HB, at] = tile[:, :128]


def weigh(len_ref, rew_ref, cot_ref, after_ref, out_ref):
    row = lax.broadcasted_iota(jnp.int32, (SLOTS, 1), 0)
    weight, start = jnp.zeros((SLOTS, 1), F32), jnp.int32(0)
    for j in range(4):
        end = start + len_ref[0, j]
        scaled = jnp.full((SLOTS, 1), rew_ref[0, j], jnp.int32).astype(F32) / 65536.0
        weight += jnp.where((row >= start) & (row < end), scaled, 0.0)
        start = end
    out_ref[:SLOTS, :] = (weight * cot_ref[...].astype(F32)).astype(BF)
    out_ref[SLOTS:, :] = mark(len_ref, D)


def merged(tail, surplus, count):
    slot = lax.broadcasted_iota(jnp.int32, (TAIL, TAIL + SPARE), 0)
    src = lax.broadcasted_iota(jnp.int32, (TAIL, TAIL + SPARE), 1)
    want = jnp.where(HEAD + slot < count, slot, TAIL + slot - jnp.maximum(count - HEAD, 0))
    pick = jnp.where(src == want, 1.0, 0.0).astype(BF)
    return mm(pick, jnp.concatenate([tail, surplus], axis=0)).astype(BF)


def other_count(ref):
    rows = ref[SLOTS : SLOTS + MARK, :128].astype(F32)
    return rows[:1, : TAIL + SPARE].astype(jnp.int32)


def merge_rows(len_ref, rest_ref, got_ref, out_ref):
    rest, got = rest_ref[...], got_ref[:SLOTS, :]
    out_ref[:TAIL, :] = merged(rest[:TAIL], got[CAP:], live(len_ref))
    out_ref[TAIL : TAIL + HEAD, :] = got[:HEAD]
    out_ref[TAIL + HEAD :, :] = merged(got[HEAD:CAP], rest[TAIL:], other_count(got_ref))


def order_token(after_ref, out_ref):
    out_ref[...] = jnp.zeros_like(out_ref)


def merge_cot(len_ref, own_ref, got_ref, after_ref, cot_out):
    own, got = own_ref[:SLOTS, :], got_ref[:SLOTS, :]
    cot_out[:HEAD, :] = own[:HEAD]
    cot_out[HEAD:CAP, :] = merged(own[HEAD:CAP], got[CAP:], live(len_ref))
    cot_out[CAP : CAP + HEAD, :] = got[:HEAD]
    cot_out[CAP + HEAD :, :] = merged(got[HEAD:CAP], own[CAP:], other_count(got_ref))


def near_terms(head_ref, tail_ref, far_head_ref, cot_ref, wide_ref, down_ref, sum_out):
    rows = jnp.concatenate([head_ref[...], tail_ref[...], far_head_ref[...]], axis=0)
    sum_out[:, : 2 * UP] = mm(rows, wide_ref[...], ((1,), (1,)))
    sum_out[: 2 * CAP, 2 * UP : 2 * UP + HH] = mm(cot_ref[...], down_ref[...], ((1,), (1,)))
    sum_out[: 2 * CAP, 2 * UP + HH :] = jnp.zeros((2 * CAP, 128 - HH), F32)
    sum_out[2 * CAP :, 2 * UP :] = jnp.zeros((HEAD, 128), F32)


def next_back(cot_ref, down_ref, out_ref):
    out_ref[:, :HH] = mm(cot_ref[...], down_ref[...], ((1,), (1,))).astype(out_ref.dtype)
    out_ref[:, HH:] = jnp.zeros((2 * CAP, 128 - HH), out_ref.dtype)


def far_terms(tail_ref, wide_ref, back_ref, out_ref):
    out_ref[: CAP + TAIL] = mm(tail_ref[...], wide_ref[...], ((1,), (1,))).astype(out_ref.dtype)
    for k in range(4):
        out_ref[CAP + TAIL :, k * 128 : (k + 1) * 128] = back_ref[k * 64 : (k + 1) * 64, :]


def swapped(value):
    return jnp.concatenate([value[CAP:], value[:CAP]], axis=0)


def both_halves(core, mine, other):
    low, high = jnp.where(core == 0, mine, other), jnp.where(core == 0, other, mine)
    lane = lax.broadcasted_iota(jnp.int32, low.shape, 1)
    high = pltpu.roll(high, HH, 1)
    return jnp.concatenate([jnp.where(lane < HH, low, high), high], axis=1)[:, :HB]


def hidden_grads(gate, up, back):
    sig = jax.nn.sigmoid(gate)
    gate_back = back * up * sig * (1.0 + gate * (1.0 - sig))
    return gate_back.astype(BF), (back * (gate * sig)).astype(BF)


def near_grads(core_ref, mine_ref, other_ref, gate_out, up_out, early_out):
    mine, other = mine_ref[: 2 * CAP], swapped(other_ref[: 2 * CAP])
    total = mine[:, : 2 * UP] + other[:, : 2 * UP]
    back = both_halves(core_ref[0], mine[:, 2 * UP :], other[:, 2 * UP :])
    gate_out[...], up_out[...] = hidden_grads(total[:, :HB], total[:, UP : UP + HB], back)
    early_out[...] = jnp.zeros_like(early_out)
    early_out[:HEAD] = mine_ref[2 * CAP :, : 2 * UP]
    early_out[CAP : CAP + HEAD] = other_ref[2 * CAP :, : 2 * UP]


def weight_grads(
    core_ref, early_ref, mine_ref, other_ref, back_ref, gate_ref, up_ref,
    head_ref, tail_ref, far_head_ref, far_tail_ref, out_ref, gate_all, up_all,
):
    @pl.when(pl.program_id(0) == 0)
    def _():
        mine, other = mine_ref[...].astype(F32), other_ref[...].astype(F32)
        early = early_ref[...]
        total = jnp.concatenate(
            [
                early[:HEAD] + other[TAIL : TAIL + HEAD],
                mine[:TAIL] + other[TAIL + HEAD : CAP + TAIL],
                early[CAP : CAP + HEAD] + mine[TAIL : TAIL + HEAD],
                mine[TAIL + HEAD : CAP + TAIL] + other[:TAIL],
            ],
            axis=0,
        )
        cross = other[CAP + TAIL :]
        cross = jnp.concatenate([cross[:, k * 128 : (k + 1) * 128] for k in range(4)], axis=0)
        back = both_halves(core_ref[0], back_ref[...].astype(F32), swapped(cross))
        gate_all[2 * CAP :], up_all[2 * CAP :] = hidden_grads(
            total[:, :HB], total[:, UP : UP + HB], back
        )
        gate_all[: 2 * CAP] = gate_ref[...]
        up_all[: 2 * CAP] = up_ref[...]

    rows = jnp.concatenate(
        [head_ref[...], tail_ref[...], far_head_ref[...], far_tail_ref[...]], axis=0
    )
    each = HALF // FIRST
    for at, weights in ((0, gate_all), (HB, up_all)):
        total = mm(weights[...], rows, ((0,), (0,))).astype(BF)
        for k in range(ABREAST):
            out_ref[k, at : at + HB] = total[:, k * each : (k + 1) * each]


def first_sum(in_ref, out_ref):
    total = in_ref[0].astype(F32)
    for k in range(1, FIRST):
        total += in_ref[k].astype(F32)
    lane = lax.broadcasted_iota(jnp.int32, (HB, 128), 1)
    for k in range(SECOND // 2):
        gate = total[:HB, k * 128 : (k + 1) * 128]
        up = total[HB:, k * 128 : (k + 1) * 128]
        out_ref[2 * k] = jnp.where(lane < 64, gate, pltpu.roll(up, 64, 1)).astype(BF)
        out_ref[2 * k + 1] = jnp.where(lane < 64, pltpu.roll(gate, 64, 1), up).astype(BF)


def second_sum(in_ref, gate_out, up_out):
    total = in_ref[0].astype(F32)
    for k in range(1, SECOND):
        total += in_ref[k].astype(F32)
    full = jnp.concatenate([total, jnp.zeros((UP - HB, 128), F32)], axis=0).T
    gate_out[...] = full[:64, :HB]
    up_out[...] = full[64:, :HB]


def along_z(block, distance):
    n = lax.axis_size("z")
    return lax.ppermute(block, "z", [(i, (i + distance) % n) for i in range(n)])


def between_cores(block):
    return lax.ppermute(block, "c", [(0, 1), (1, 0)])


def on_device(tokens, cotangent, gate_weight, up_weight, down_weight, lengths, rewards):
    core = lax.axis_index("c").astype(jnp.int32).reshape(1)
    half = lax.dynamic_slice_in_dim(down_weight, lax.axis_index("c") * HH, HH, 0)
    next_half = along_z(half, -1)
    head, rest, row_other = call(
        split_rows,
        (shape(HEAD, HALF), shape(SLOTS - HEAD, HALF), shape(SLOTS + MARK, HALF)),
        in_specs=[SMEM, SMEM, VMEM], cost=1.7,
    )(core, lengths, tokens)
    far_head = along_z(head, 1)
    row_got = between_cores(row_other)
    tail = call(
        merge_rows, shape(CAP + TAIL, HALF), cost=0.01,
                in_specs=[SMEM, VMEM, VMEM],
    )(lengths, rest, row_got)
    far_tail = along_z(tail, 1)
    cot_own = call(
        weigh, shape(SLOTS + MARK, D), in_specs=[SMEM, SMEM, VMEM, ANY], cost=0.01,
    )(lengths, rewards, cotangent, tail)
    cot_got = between_cores(cot_own)

    token = call(
        order_token, shape(8, 128, kind=F32), cost=2.7, in_specs=[ANY],
    )(next_half)
    cot_rows = call(
        merge_cot, shape(2 * CAP, D), cost=1, in_specs=[SMEM] + [VMEM] * 2 + [ANY],
    )(lengths, cot_own, cot_got, token)
    back = call(
        next_back, shape(2 * CAP, 128), cost=0.5,
        in_specs=[VMEM] * 2,
    )(cot_rows, next_half)
    far_back = along_z(back, 1)
    wide = call(
        split_wide, shape(2 * UP, HALF), in_specs=[SMEM, VMEM, VMEM, ANY], cost=0.01,
    )(core, gate_weight.T, up_weight.T, back)
    near = call(
        near_terms, shape(2 * CAP + HEAD, 2 * UP + 128, kind=F32),
        cost=0.01, in_specs=[VMEM] * 6,
    )(head, tail, far_head, cot_rows, wide, half)
    near_other = between_cores(near)
    gate_near, up_near, early = call(
        near_grads,
        (shape(2 * CAP, HB), shape(2 * CAP, HB), shape(2 * CAP, 2 * UP, kind=F32)),
        cost=0.3, in_specs=[SMEM] + [VMEM] * 2,
    )(core, near, near_other)
    far = call(
        far_terms, shape(CAP + TAIL + 64, 2 * UP), cost=10, in_specs=[VMEM] * 3
    )(far_tail, wide, far_back)
    far_other = between_cores(far)

    each = HALF // FIRST
    whole = lambda *dims: pl.BlockSpec(dims, lambda i: (0,) * len(dims))
    part = lambda rows: pl.BlockSpec((rows, ABREAST * each), lambda i: (0, i))
    grads = call(
        weight_grads, shape(FIRST, 2 * HB, each),
        scratch=[pltpu.VMEM((4 * CAP, HB), BF)] * 2, cost=2.1,
        grid=(FIRST // ABREAST,),
        in_specs=[SMEM, whole(2 * CAP, 2 * UP)] + [whole(CAP + TAIL + 64, 2 * UP)] * 2
        + [whole(2 * CAP, 128)] + [whole(2 * CAP, HB)] * 2
        + [part(HEAD), part(CAP + TAIL)] * 2,
        out_specs=pl.BlockSpec((ABREAST, 2 * HB, each), lambda i: (i, 0, 0)),
    )(core, early, far, far_other, far_back, gate_near, up_near, head, tail, far_head, far_tail)
    grads = lax.all_to_all(grads, ("xh", "xl", "yl"), split_axis=0, concat_axis=0, tiled=True)
    grads = call(
        first_sum, shape(SECOND, HB, 128), cost=0.4,
    )(grads)
    grads = lax.all_to_all(grads, "yh", split_axis=0, concat_axis=0, tiled=True)
    return call(
        second_sum, (shape(64, HB, kind=F32), shape(64, HB, kind=F32)),
                in_specs=[VMEM],
    )(grads)


def solution(mesh):
    planes = mesh.shape["blk"]
    names = ("z", "xl", "yh", "yl", "xh", "c")
    fine = Mesh(mesh.devices.reshape(planes, 2, 4, 2, 2, 2), names)
    rows = P(names, None)
    placed = (rows, rows, P(None, "z"), P(None, "z"), P("z", None), rows, rows)
    out = P(names[1:], "z")
    return jax.shard_map(
        on_device, mesh=fine, in_specs=placed, out_specs=(out, out), check_vma=False
    )
```

time: 117 us -> 106 us (0.906)
  blocking collectives: 47.8 us -> 42 us
  Pallas kernels: 15.1 us -> 11.2 us
  starting transfers between devices: 37.3 us -> 36 us
    ppermute x4, starting transfers between devices: 11.2 us -> 24.7 us  [along_z(): return lax.ppermute(block, 'z', [(i, (i + distance) % n) for i in range(n)])]
    ppermute x4, starting transfers between devices: 24.2 us -> 11.3 us  [between_cores(): return lax.ppermute(block, 'c', [(0, 1), (1, 0)])]
    all_to_all x2, blocking collectives: 47.8 us -> 42 us  [the longest x1 28.1 us: on_device(): lax.all_to_all(grads, ('xh', 'xl', 'yl'), split_axis=0, concat_axis=0, ti...]
    ppermute x1 -> x0, waiting for transfers between devices: 3.83 us -> none  [along_z_crossed(): return lax.ppermute(block, ('z', 'c'), route)]
    pallas_call x8 -> x9, Pallas kernels: 12.1 us -> 8.88 us  [the longest x1 2.16 us: on_device(): call(weight_grads, shape(FIRST, 2 * HB, each), scratch=[pltpu.VMEM((4 * C...]
    ppermute x4, waiting for transfers between devices: 9.09 us -> 11.8 us  [along_z(): return lax.ppermute(block, 'z', [(i, (i + distance) % n) for i in range(n)])]
    ppermute x1 -> x0, starting transfers between devices: 1.92 us -> none  [along_z_crossed(): return lax.ppermute(block, ('z', 'c'), route)]
  transfers between devices with their start and end apart: 9 -> 8, of which waited for: 2 -> 4; matrix products, arithmetic and copies ran while one was open for 0% -> 0% of each run, Pallas kernels for 9% -> 8%
where the time goes in v3:
time: 106 us; the launch traced here: 104 us
  blocking collectives  42 us (40%)
  starting transfers between devices  36 us (34%)
  waiting for transfers between devices  12.6 us (12%)
  Pallas kernels  11.2 us (11%)
  local copies, waits for them, and re-layouts  1.57 us (1%)
    all_to_all x1, blocking collectives, on_device(): lax.all_to_all(grads, ('xh', 'xl', 'yl'), split_axis=0, concat_axis=0, ti...  28.1 us
    ppermute x4, starting transfers between devices, along_z(): return lax.ppermute(block, 'z', [(i, (i + distance) % n) for i in range(n)])  24.7 us
    all_to_all x1, blocking collectives, on_device(): grads = lax.all_to_all(grads, 'yh', split_axis=0, concat_axis=0, tiled=True)  13.9 us
    ppermute x4, waiting for transfers between devices, along_z(): return lax.ppermute(block, 'z', [(i, (i + distance) % n) for i in range(n)])  11.8 us
    ppermute x4, starting transfers between devices, between_cores(): return lax.ppermute(block, 'c', [(0, 1), (1, 0)])  11.3 us
    pallas_call x1, Pallas kernels, on_device(): call(weight_grads, shape(FIRST, 2 * HB, each), scratch=[pltpu.VMEM((4 * C...  2.16 us
  transfers between devices with their start and end apart: 8, of which 4 were waited for; matrix products, arithmetic and copies ran while one was open for 0% of the time, Pallas kernels for 8%

profile of v3, /device:TPU:1, one launch (start us, length us, event | category | flops | bytes accessed | tf_op | source)
XLA Modules:
  0.0 104.3 jit_solution(16583584793435686524)
XLA Ops:
  0.6 0.0 copy-start
  0.7 1.5 %copy-done = bf16[224,4096]{1,0:T(8,128)(2,1)S(1)} copy-done((bf16[224,4096]{1,0:T(8,128)(2,1)S(1)}, bf16[224,4096]{1,0:T(8,128)(2,1)}, u32[]{:S(2)}) %copy-start) | copy-done | bytes 1835032
  2.1 0.1 constant_dynamic-slice_fusion.down_ref
  2.2 18.8 %collective-permute-start.3 = (bf16[112,4096]{1,0:T(8,128)(2,1)S(1)}, bf16[112,4096]{1,0:T(8,128)(2,1)S(1)}, u32[]{:S(2)}, u32[]{:S(2)}) collective-permute-start(bf16[112,4096]{1,0:T(8,128)(2,1)S(1)} %constant_dynamic-slice_fusion.down_ref), channel_id=1, source_target_pairs={{0,960},{64,0},{128,64},{192,128},{256,192},{320,256},{384,320},{4... | collective-permute-start | bytes 2752520 | tf_op jit(solution)/shard_map/ppermute | solution.py:249
  21.0 0.0 copy-start.5
  21.0 1.1 %shard_map.86 = (bf16[96,2048]{1,0:T(8,128)(2,1)S(1)}, bf16[64,2048]{1,0:T(8,128)(2,1)S(1)}, bf16[176,2048]{1,0:T(8,128)(2,1)S(1)}) custom-call(s32[1]{0:T(128)} %bitcast.core_ref, s32[1,4]{1,0:T(1,128)S(1)} %copy-done.4, bf16[160,4096]{1,0:T(8,128)(2,1)S(1)} %copy-done.6), custom_call_target="tpu_custom_call" | custom-call | flops 16999999488 | bytes 1700000 | tf_op jit(solution)/shard_map/pallas_call | solution.py:260
  22.1 0.0 copy-start.3
  22.1 3.0 %collective-permute-start = (bf16[176,2048]{1,0:T(8,128)(2,1)S(1)}, bf16[176,2048]{1,0:T(8,128)(2,1)S(1)}, u32[]{:S(2)}, u32[]{:S(2)}) collective-permute-start(bf16[176,2048]{1,0:T(8,128)(2,1)S(1)} %get-tuple-element.10), channel_id=1, source_target_pairs={{0,1},{1,0},{2,3},{3,2},{4,5},{5,4},{6,7},{7,6},{8,9},{9,8},{10,11... | collective-permute-start | bytes 2162696 | tf_op jit(solution)/shard_map/ppermute | solution.py:253
  25.1 1.9 %collective-permute-start.1 = (bf16[96,2048]{1,0:T(8,128)(2,1)S(1)}, bf16[96,2048]{1,0:T(8,128)(2,1)S(1)}, u32[]{:S(2)}, u32[]{:S(2)}) collective-permute-start(bf16[96,2048]{1,0:T(8,128)(2,1)S(1)} %get-tuple-element.8.head_ref), channel_id=1, source_target_pairs={{0,64},{64,128},{128,192},{192,256},{256,320},{320,384},{384,448},... | collective-permute-start | bytes 1179656 | tf_op jit(solution)/shard_map/ppermute | solution.py:249
  27.0 0.8 shard_map.87.after_ref.tail_ref
  27.8 1.9 %collective-permute-start.5 = (bf16[160,2048]{1,0:T(8,128)(2,1)S(1)}, bf16[160,2048]{1,0:T(8,128)(2,1)S(1)}, u32[]{:S(2)}, u32[]{:S(2)}) collective-permute-start(bf16[160,2048]{1,0:T(8,128)(2,1)S(1)} %shard_map.87.after_ref.tail_ref), channel_id=1, source_target_pairs={{0,64},{64,128},{128,192},{192,256},{256,320},{320,384},{384,448},... | collective-permute-start | bytes 1966088 | tf_op jit(solution)/shard_map/ppermute | solution.py:249
  29.8 0.8 shard_map.88.own_ref
  30.6 2.1 %collective-permute-start.2 = (bf16[176,4096]{1,0:T(8,128)(2,1)S(1)}, bf16[176,4096]{1,0:T(8,128)(2,1)S(1)}, u32[]{:S(2)}, u32[]{:S(2)}) collective-permute-start(bf16[176,4096]{1,0:T(8,128)(2,1)S(1)} %shard_map.88.own_ref), channel_id=1, source_target_pairs={{0,1},{1,0},{2,3},{3,2},{4,5},{5,4},{6,7},{7,6},{8,9},{9,8},{10,11... | collective-permute-start | bytes 4325384 | tf_op jit(solution)/shard_map/ppermute | solution.py:253
  32.8 7.2 %collective-permute-done.3.after_ref.down_ref = bf16[112,4096]{1,0:T(8,128)(2,1)S(1)} collective-permute-done((bf16[112,4096]{1,0:T(8,128)(2,1)S(1)}, bf16[112,4096]{1,0:T(8,128)(2,1)S(1)}, u32[]{:S(2)}, u32[]{:S(2)}) %collective-permute-start.3) | collective-permute-done | bytes 917536 | tf_op jit(solution)/shard_map/ppermute | solution.py:249
  40.0 0.9 shard_map.90.cot_ref
  40.9 0.0 copy-start.1
  41.0 0.7 shard_map.91.after_ref
  41.7 2.1 %collective-permute-start.6 = (bf16[256,128]{1,0:T(8,128)(2,1)S(1)}, bf16[256,128]{1,0:T(8,128)(2,1)S(1)}, u32[]{:S(2)}, u32[]{:S(2)}) collective-permute-start(bf16[256,128]{1,0:T(8,128)(2,1)S(1)} %shard_map.91.after_ref), channel_id=1, source_target_pairs={{0,64},{64,128},{128,192},{192,256},{256,320},{320,384},{384,448},... | collective-permute-start | bytes 196616 | tf_op jit(solution)/shard_map/ppermute | solution.py:249
  43.7 1.1 %shard_map.92.wide_ref = bf16[512,2048]{1,0:T(8,128)(2,1)S(1)} custom-call(s32[1]{0:T(128)} %bitcast.core_ref, bf16[224,4096]{1,0:T(8,128)(2,1)S(1)} %bitcast.3, bf16[224,4096]{1,0:T(8,128)(2,1)S(1)} %bitcast.4, bf16[256,128]{1,0:T(8,128)(2,1)S(1)} %shard_map.91.after_ref), custom_call_target="tpu_custom_call" | custom-call | flops 100000000 | bytes 10000 | tf_op jit(solution)/shard_map/pallas_call | solution.py:288
  44.9 1.5 %shard_map.93.mine_ref = f32[352,640]{1,0:T(8,128)S(1)} custom-call(bf16[96,2048]{1,0:T(8,128)(2,1)S(1)} %get-tuple-element.8.head_ref, bf16[160,2048]{1,0:T(8,128)(2,1)S(1)} %shard_map.87.after_ref.tail_ref, bf16[96,2048]{1,0:T(8,128)(2,1)S(1)} %collective-permute-done.1.far_head_ref, bf16[256,4096]{1,0:T(8,128)(2,1)S(1)} %shard_map.90.cot_ref, ...), custom_call_target="tpu_custom_call" | custom-call | flops 100000000 | bytes 10000 | tf_op jit(solution)/shard_map/pallas_call | solution.py:291
  46.4 3.5 %collective-permute-start.4 = (f32[352,640]{1,0:T(8,128)S(1)}, f32[352,640]{1,0:T(8,128)S(1)}, u32[]{:S(2)}, u32[]{:S(2)}) collective-permute-start(f32[352,640]{1,0:T(8,128)S(1)} %shard_map.93.mine_ref), channel_id=1, source_target_pairs={{0,1},{1,0},{2,3},{3,2},{4,5},{5,4},{6,7},{7,6},{8,9},{9,8},{10,11... | collective-permute-start | bytes 2703368 | tf_op jit(solution)/shard_map/ppermute | solution.py:253
  49.8 3.1 %collective-permute-done.5.tail_ref.far_tail_ref = bf16[160,2048]{1,0:T(8,128)(2,1)S(1)} collective-permute-done((bf16[160,2048]{1,0:T(8,128)(2,1)S(1)}, bf16[160,2048]{1,0:T(8,128)(2,1)S(1)}, u32[]{:S(2)}, u32[]{:S(2)}) %collective-permute-start.5) | collective-permute-done | bytes 655392 | tf_op jit(solution)/shard_map/ppermute | solution.py:249
  53.0 1.4 %collective-permute-done.6.back_ref = bf16[256,128]{1,0:T(8,128)(2,1)S(1)} collective-permute-done((bf16[256,128]{1,0:T(8,128)(2,1)S(1)}, bf16[256,128]{1,0:T(8,128)(2,1)S(1)}, u32[]{:S(2)}, u32[]{:S(2)}) %collective-permute-start.6) | collective-permute-done | bytes 65568 | tf_op jit(solution)/shard_map/ppermute | solution.py:249
  54.4 0.8 shard_map.95.mine_ref
  55.2 2.7 %collective-permute-start.7 = (bf16[224,512]{1,0:T(8,128)(2,1)S(1)}, bf16[224,512]{1,0:T(8,128)(2,1)S(1)}, u32[]{:S(2)}, u32[]{:S(2)}) collective-permute-start(bf16[224,512]{1,0:T(8,128)(2,1)S(1)} %shard_map.95.mine_ref), channel_id=1, source_target_pairs={{0,1},{1,0},{2,3},{3,2},{4,5},{5,4},{6,7},{7,6},{8,9},{9,8},{10,11... | collective-permute-start | bytes 688136 | tf_op jit(solution)/shard_map/ppermute | solution.py:253
  58.0 0.2 shard_map.94
  58.2 0.9 collective-permute-done.7.other_ref
  59.0 2.2 %shard_map.96 = bf16[8,448,256]{2,1,0:T(8,128)(2,1)S(1)} custom-call(s32[1]{0:T(128)} %bitcast.core_ref, f32[256,512]{1,0:T(8,128)S(1)} %get-tuple-element.11.early_ref, bf16[224,512]{1,0:T(8,128)(2,1)S(1)} %shard_map.95.mine_ref, bf16[224,512]{1,0:T(8,128)(2,1)S(1)} %collective-permute-done.7.other_ref, ...), custom_call_target="tpu_custom_call" | custom-call | flops 20999999488 | bytes 2100000 | tf_op jit(solution)/shard_map/pallas_call | solution.py:309
  61.2 28.1 %all_to_all.10.in_ref = bf16[8,448,256]{2,1,0:T(8,128)(2,1)S(1)} all-to-all(bf16[8,448,256]{2,1,0:T(8,128)(2,1)S(1)} %shard_map.96), channel_id=1, replica_groups=mesh['z'=16,'xl'=2,'yh'=4,'yl'=2,'xh'=2,'c'=2] {'xh','xl','yl'}, dimensions={0} | all-to-all | bytes 3670016 | tf_op jit(solution)/shard_map/all_to_all | solution.py:318
  89.3 0.3 shard_map.97
  89.6 13.9 %all_to_all.11.in_ref = bf16[4,224,128]{2,1,0:T(8,128)(2,1)S(1)} all-to-all(bf16[4,224,128]{2,1,0:T(8,128)(2,1)S(1)} %shard_map.97), channel_id=1, replica_groups=mesh['z'=16,'xl'=2,'yh'=4,'yl'=2,'xh'=2,'c'=2] {'yh'}, dimensions={0} | all-to-all | bytes 458752 | tf_op jit(solution)/shard_map/all_to_all | solution.py:322
  103.6 0.7 shard_map.98
  (14 shorter events, 0.0 us)
Async XLA Ops:
  0.6 1.5 %copy-start = (bf16[224,4096]{1,0:T(8,128)(2,1)S(1)}, bf16[224,4096]{1,0:T(8,128)(2,1)}, u32[]{:S(2)}) copy-start(bf16[224,4096]{1,0:T(8,128)(2,1)} %param.11) | copy-start | bytes 5505028
  0.6 20.3 %copy-start.4 = (s32[1,4]{1,0:T(1,128)S(1)}, s32[1,4]{1,0:T(1,128)}, u32[]{:S(2)}) copy-start(s32[1,4]{1,0:T(1,128)} %len_ref.7) | copy-start | bytes 52
  0.7 20.3 %copy-start.6 = (bf16[160,4096]{1,0:T(8,128)(2,1)S(1)}, bf16[160,4096]{1,0:T(8,128)(2,1)}, u32[]{:S(2)}) copy-start(bf16[160,4096]{1,0:T(8,128)(2,1)} %tok_ref.1) | copy-start | bytes 3932164
  2.2 37.8 %collective-permute-start.3 = (bf16[112,4096]{1,0:T(8,128)(2,1)S(1)}, bf16[112,4096]{1,0:T(8,128)(2,1)S(1)}, u32[]{:S(2)}, u32[]{:S(2)}) collective-permute-start(bf16[112,4096]{1,0:T(8,128)(2,1)S(1)} %constant_dynamic-slice_fusion.down_ref), channel_id=1, source_target_pairs={{0,960},{64,0},{128,64},{192,128},{256,192},{320,256},{384,320},{4... | collective-permute-start | bytes 2752520 | tf_op jit(solution)/shard_map/ppermute | solution.py:249
  21.0 8.8 %copy-start.5 = (s32[1,4]{1,0:T(1,128)S(1)}, s32[1,4]{1,0:T(1,128)}, u32[]{:S(2)}) copy-start(s32[1,4]{1,0:T(1,128)} %rew_ref.1) | copy-start | bytes 52
  22.1 7.7 %copy-start.3 = (bf16[160,4096]{1,0:T(8,128)(2,1)S(1)}, bf16[160,4096]{1,0:T(8,128)(2,1)}, u32[]{:S(2)}) copy-start(bf16[160,4096]{1,0:T(8,128)(2,1)} %cot_ref.1) | copy-start | bytes 3932164
  22.1 4.9 %collective-permute-start = (bf16[176,2048]{1,0:T(8,128)(2,1)S(1)}, bf16[176,2048]{1,0:T(8,128)(2,1)S(1)}, u32[]{:S(2)}, u32[]{:S(2)}) collective-permute-start(bf16[176,2048]{1,0:T(8,128)(2,1)S(1)} %get-tuple-element.10), channel_id=1, source_target_pairs={{0,1},{1,0},{2,3},{3,2},{4,5},{5,4},{6,7},{7,6},{8,9},{9,8},{10,11... | collective-permute-start | bytes 2162696 | tf_op jit(solution)/shard_map/ppermute | solution.py:253
  25.1 19.8 %collective-permute-start.1 = (bf16[96,2048]{1,0:T(8,128)(2,1)S(1)}, bf16[96,2048]{1,0:T(8,128)(2,1)S(1)}, u32[]{:S(2)}, u32[]{:S(2)}) collective-permute-start(bf16[96,2048]{1,0:T(8,128)(2,1)S(1)} %get-tuple-element.8.head_ref), channel_id=1, source_target_pairs={{0,64},{64,128},{128,192},{192,256},{256,320},{320,384},{384,448},... | collective-permute-start | bytes 1179656 | tf_op jit(solution)/shard_map/ppermute | solution.py:249
  27.8 25.2 %collective-permute-start.5 = (bf16[160,2048]{1,0:T(8,128)(2,1)S(1)}, bf16[160,2048]{1,0:T(8,128)(2,1)S(1)}, u32[]{:S(2)}, u32[]{:S(2)}) collective-permute-start(bf16[160,2048]{1,0:T(8,128)(2,1)S(1)} %shard_map.87.after_ref.tail_ref), channel_id=1, source_target_pairs={{0,64},{64,128},{128,192},{192,256},{256,320},{320,384},{384,448},... | collective-permute-start | bytes 1966088 | tf_op jit(solution)/shard_map/ppermute | solution.py:249
  30.6 9.4 %collective-permute-start.2 = (bf16[176,4096]{1,0:T(8,128)(2,1)S(1)}, bf16[176,4096]{1,0:T(8,128)(2,1)S(1)}, u32[]{:S(2)}, u32[]{:S(2)}) collective-permute-start(bf16[176,4096]{1,0:T(8,128)(2,1)S(1)} %shard_map.88.own_ref), channel_id=1, source_target_pairs={{0,1},{1,0},{2,3},{3,2},{4,5},{5,4},{6,7},{7,6},{8,9},{9,8},{10,11... | collective-permute-start | bytes 4325384 | tf_op jit(solution)/shard_map/ppermute | solution.py:253
  40.9 2.8 %copy-start.1 = (bf16[4096,224]{0,1:T(8,128)(2,1)S(1)}, bf16[4096,224]{0,1:T(8,128)(2,1)}, u32[]{:S(2)}) copy-start(bf16[4096,224]{0,1:T(8,128)(2,1)} %param.9) | copy-start | bytes 5505028
  40.9 2.8 %copy-start.2 = (bf16[4096,224]{0,1:T(8,128)(2,1)S(1)}, bf16[4096,224]{0,1:T(8,128)(2,1)}, u32[]{:S(2)}) copy-start(bf16[4096,224]{0,1:T(8,128)(2,1)} %param.10) | copy-start | bytes 5505028
  41.7 12.7 %collective-permute-start.6 = (bf16[256,128]{1,0:T(8,128)(2,1)S(1)}, bf16[256,128]{1,0:T(8,128)(2,1)S(1)}, u32[]{:S(2)}, u32[]{:S(2)}) collective-permute-start(bf16[256,128]{1,0:T(8,128)(2,1)S(1)} %shard_map.91.after_ref), channel_id=1, source_target_pairs={{0,64},{64,128},{128,192},{192,256},{256,320},{320,384},{384,448},... | collective-permute-start | bytes 196616 | tf_op jit(solution)/shard_map/ppermute | solution.py:249
  46.4 11.6 %collective-permute-start.4 = (f32[352,640]{1,0:T(8,128)S(1)}, f32[352,640]{1,0:T(8,128)S(1)}, u32[]{:S(2)}, u32[]{:S(2)}) collective-permute-start(f32[352,640]{1,0:T(8,128)S(1)} %shard_map.93.mine_ref), channel_id=1, source_target_pairs={{0,1},{1,0},{2,3},{3,2},{4,5},{5,4},{6,7},{7,6},{8,9},{9,8},{10,11... | collective-permute-start | bytes 2703368 | tf_op jit(solution)/shard_map/ppermute | solution.py:253
  55.2 3.8 %collective-permute-start.7 = (bf16[224,512]{1,0:T(8,128)(2,1)S(1)}, bf16[224,512]{1,0:T(8,128)(2,1)S(1)}, u32[]{:S(2)}, u32[]{:S(2)}) collective-permute-start(bf16[224,512]{1,0:T(8,128)(2,1)S(1)} %shard_map.95.mine_ref), channel_id=1, source_target_pairs={{0,1},{1,0},{2,3},{3,2},{4,5},{5,4},{6,7},{7,6},{8,9},{9,8},{10,11... | collective-permute-start | bytes 688136 | tf_op jit(solution)/shard_map/ppermute | solution.py:253

commit v4 on v3

v4 whole, which is shorter than its diff:
```python
import functools

import jax
import jax.numpy as jnp
from jax import lax
from jax.experimental import pallas as pl
from jax.experimental.pallas import tpu as pltpu
from jax.sharding import Mesh
from jax.sharding import PartitionSpec as P

D = 4096
HALF = D // 2
HB = 224
SLOTS = 160
CAP = 128
HEAD = 96
TAIL = CAP - HEAD
SPARE = SLOTS - CAP
FAR = HEAD + 2 * TAIL
UP = 256
MARK = 16
HH = HB // 2
FIRST, SECOND = 8, 4
ABREAST = 2
BF, F32 = jnp.bfloat16, jnp.float32
VMEM = pl.BlockSpec(memory_space=pltpu.VMEM)
SMEM = pl.BlockSpec(memory_space=pltpu.SMEM)
ANY = pl.BlockSpec(memory_space=pl.ANY)


def source_tile(first, second):
    x_hi, x_lo, y = first // 4, first // 2 % 2, 2 * second + first % 2
    return (x_lo * 8 + y) * 2 + x_hi


def call(body, outs, scratch=(), room=32, cost=0.0, **more):
    return pl.pallas_call(
        body,
        out_shape=outs,
        scratch_shapes=scratch,
        cost_estimate=pl.CostEstimate(flops=int(cost * 1e10), bytes_accessed=int(cost * 1e6), transcendentals=0),
        compiler_params=pltpu.CompilerParams(vmem_limit_bytes=room * 1024 * 1024),
        **more,
    )


def shape(*dims, kind=BF):
    return jax.ShapeDtypeStruct(dims, kind)


def mm(a, b, dims=((1,), (0,))):
    return lax.dot_general(a, b, (dims, ((), ())), preferred_element_type=F32)


def sorter(core):
    src = lax.broadcasted_iota(jnp.int32, (256, 256), 0)
    dst = lax.broadcasted_iota(jnp.int32, (256, 256), 1)
    lane = dst % 128
    side = jnp.where(dst < 128, core, 1 - core)
    want = (lane // 64) * 128 + side * 64 + lane % 64
    return jnp.where(src == want, 1.0, 0.0).astype(BF)


def sorted_tiles(ref, perm):
    for k in range(HALF // 128):
        first, second = (2 * k) // SECOND, (2 * k) % SECOND
        both = [
            ref[:, t * 128 : (t + 1) * 128]
            for t in (source_tile(first, second), source_tile(first, second + 1))
        ]
        yield slice(k * 128, (k + 1) * 128), mm(jnp.concatenate(both, axis=1), perm).astype(BF)


def mark(len_ref, columns):
    return jnp.full((MARK, columns), live(len_ref), jnp.int32).astype(F32).astype(BF)


def live(len_ref):
    return len_ref[0, 0] + len_ref[0, 1] + len_ref[0, 2] + len_ref[0, 3]


def take_head(tok_ref, after_ref, out_ref):
    out_ref[...] = tok_ref[:HEAD, :]


def split_rows(core_ref, len_ref, tok_ref, own_out, other_out):
    other_out[SLOTS:, :] = mark(len_ref, HALF)
    for at, tile in sorted_tiles(tok_ref, sorter(core_ref[0])):
        own_out[:, at] = tile[:, :128]
        other_out[:SLOTS, at] = tile[:, 128:]


def split_far(core_ref, row_ref, after_ref, own_out, other_out):
    for at, tile in sorted_tiles(row_ref, sorter(core_ref[0])):
        own_out[:, at] = tile[:, :128]
        other_out[:, at] = tile[:, 128:]


def split_wide(core_ref, gate_ref, up_ref, after_ref, wide_out):
    perm = sorter(core_ref[0])
    wide_out[HB:UP, :] = jnp.zeros((UP - HB, HALF), BF)
    wide_out[UP + HB :, :] = jnp.zeros((UP - HB, HALF), BF)
    for at, tile in sorted_tiles(gate_ref, perm):
        wide_out[:HB, at] = tile[:, :128]
    for at, tile in sorted_tiles(up_ref, perm):
        wide_out[UP : UP + HB, at] = tile[:, :128]


def weigh(len_ref, rew_ref, cot_ref, after_ref, out_ref):
    row = lax.broadcasted_iota(jnp.int32, (SLOTS, 1), 0)
    weight, start = jnp.zeros((SLOTS, 1), F32), jnp.int32(0)
    for j in range(4):
        end = start + len_ref[0, j]
        scaled = jnp.full((SLOTS, 1), rew_ref[0, j], jnp.int32).astype(F32) / 65536.0
        weight += jnp.where((row >= start) & (row < end), scaled, 0.0)
        start = end
    out_ref[:SLOTS, :] = (weight * cot_ref[...].astype(F32)).astype(BF)
    out_ref[SLOTS:, :] = mark(len_ref, D)


def merged(tail, surplus, count):
    slot = lax.broadcasted_iota(jnp.int32, (TAIL, TAIL + SPARE), 0)
    src = lax.broadcasted_iota(jnp.int32, (TAIL, TAIL + SPARE), 1)
    want = jnp.where(HEAD + slot < count, slot, TAIL + slot - jnp.maximum(count - HEAD, 0))
    pick = jnp.where(src == want, 1.0, 0.0).astype(BF)
    return mm(pick, jnp.concatenate([tail, surplus], axis=0)).astype(BF)


def other_count(ref):
    rows = ref[SLOTS : SLOTS + MARK, :128].astype(F32)
    return rows[:1, : TAIL + SPARE].astype(jnp.int32)


def merge_rows(len_ref, own_ref, got_ref, row_out, tail_out):
    own, got = own_ref[...], got_ref[:SLOTS, :]
    tail_out[:TAIL, :] = merged(own[HEAD:CAP], got[CAP:], live(len_ref))
    tail_out[TAIL:, :] = merged(got[HEAD:CAP], own[CAP:], other_count(got_ref))
    row_out[:HEAD, :] = own[:HEAD]
    row_out[HEAD:CAP, :] = tail_out[:TAIL, :]
    row_out[CAP : CAP + HEAD, :] = got[:HEAD]
    row_out[CAP + HEAD :, :] = tail_out[TAIL:, :]


def order_token(after_ref, behind_ref, out_ref):
    out_ref[...] = jnp.zeros_like(out_ref)


def near_terms(row_ref, wide_ref, sum_out):
    sum_out[...] = mm(row_ref[...], wide_ref[...], ((1,), (1,)))


def next_back(len_ref, own_ref, got_ref, next_ref, after_ref, behind_ref, cot_out, back_out):
    own, got, weights = own_ref[:SLOTS, :], got_ref[:SLOTS, :], next_ref[...]
    own_tail = merged(own[HEAD:CAP], got[CAP:], live(len_ref))
    got_tail = merged(got[HEAD:CAP], own[CAP:], other_count(got_ref))
    back_out[:, HH:] = jnp.zeros((2 * CAP, 128 - HH), BF)
    at = 0
    for part in (own[:HEAD], own_tail, got[:HEAD], got_tail):
        here = slice(at, at + part.shape[0])
        back_out[here, :HH] = mm(part, weights, ((1,), (1,))).astype(BF)
        at += part.shape[0]
    cot_out[:TAIL, :] = own_tail
    cot_out[TAIL:, :] = got_tail


def near_back(own_ref, got_ref, tail_ref, down_ref, after_ref, back_out):
    tail = tail_ref[...]
    parts = (own_ref[:HEAD, :], tail[:TAIL], got_ref[:HEAD, :], tail[TAIL:])
    back_out[:, HH:] = jnp.zeros((2 * CAP, 128 - HH), BF)
    cot = jnp.concatenate(parts, axis=0)
    back_out[:, :HH] = mm(cot, down_ref[...], ((1,), (1,))).astype(BF)


def far_rows(own_ref, got_ref, tail_ref):
    tail = tail_ref[...]
    return jnp.concatenate([own_ref[...], tail[:TAIL], got_ref[...], tail[TAIL:]], axis=0)


def far_terms(head_ref, gate_ref, up_ref, tail_ref, wide_ref, back_ref, near_ref, out_ref):
    out_ref[:HEAD, :] = jnp.zeros((HEAD, 2 * UP), BF)
    head = head_ref[...]
    out_ref[:HEAD, :HB] = mm(head, gate_ref[...], ((1,), (1,))).astype(BF)
    out_ref[:HEAD, UP : UP + HB] = mm(head, up_ref[...], ((1,), (1,))).astype(BF)
    out_ref[HEAD:FAR] = mm(tail_ref[...], wide_ref[...], ((1,), (1,))).astype(BF)
    for at, ref in ((FAR, back_ref), (FAR + 64, near_ref)):
        for k in range(4):
            out_ref[at : at + 64, k * 128 : (k + 1) * 128] = ref[k * 64 : (k + 1) * 64, :]


def swapped(value):
    return jnp.concatenate([value[CAP:], value[:CAP]], axis=0)


def both_halves(core, mine, other):
    low, high = jnp.where(core == 0, mine, other), jnp.where(core == 0, other, mine)
    lane = lax.broadcasted_iota(jnp.int32, low.shape, 1)
    high = pltpu.roll(high, HH, 1)
    return jnp.concatenate([jnp.where(lane < HH, low, high), high], axis=1)[:, :HB]


def hidden_grads(gate, up, back):
    sig = jax.nn.sigmoid(gate)
    gate_back = back * up * sig * (1.0 + gate * (1.0 - sig))
    return gate_back.astype(BF), (back * (gate * sig)).astype(BF)


def weight_grads(
    core_ref, near_ref, near_got_ref, mine_ref, other_ref, back_ref, near_back_ref,
    row_ref, far_own_ref, far_got_ref, far_tail_ref, out_ref, gate_all, up_all,
):
    def one(start, total, back, packed):
        cross = jnp.concatenate([packed[:, k * 128 : (k + 1) * 128] for k in range(4)], axis=0)
        back = both_halves(core_ref[0], back.astype(F32), swapped(cross.astype(F32)))
        at = slice(start, start + 2 * CAP)
        gate_all[at], up_all[at] = hidden_grads(total[:, :HB], total[:, UP : UP + HB], back)

    @pl.when(pl.program_id(0) == 0)
    def _():
        near = near_ref[...] + swapped(near_got_ref[...])
        one(0, near, near_back_ref[...], other_ref[FAR + 64 :, :])
        mine, other = mine_ref[:FAR, :].astype(F32), other_ref[:FAR, :].astype(F32)
        far = jnp.concatenate(
            [
                mine[:HEAD],
                mine[HEAD:CAP] + other[CAP:],
                other[:HEAD],
                mine[CAP:] + other[HEAD:CAP],
            ],
            axis=0,
        )
        one(2 * CAP, far, back_ref[...], other_ref[FAR : FAR + 64, :])

    rows = jnp.concatenate([row_ref[...], far_rows(far_own_ref, far_got_ref, far_tail_ref)], axis=0)
    each = HALF // FIRST
    for k in range(ABREAST):
        at = slice(k * each, (k + 1) * each)
        out_ref[k, :HB] = mm(gate_all[...], rows[:, at], ((0,), (0,))).astype(BF)
        out_ref[k, HB:] = mm(up_all[...], rows[:, at], ((0,), (0,))).astype(BF)


def first_sum(in_ref, out_ref):
    total = in_ref[0].astype(F32)
    for k in range(1, FIRST):
        total += in_ref[k].astype(F32)
    lane = lax.broadcasted_iota(jnp.int32, (HB, 128), 1)
    for k in range(SECOND // 2):
        gate = total[:HB, k * 128 : (k + 1) * 128]
        up = total[HB:, k * 128 : (k + 1) * 128]
        out_ref[2 * k] = jnp.where(lane < 64, gate, pltpu.roll(up, 64, 1)).astype(BF)
        out_ref[2 * k + 1] = jnp.where(lane < 64, pltpu.roll(gate, 64, 1), up).astype(BF)


def second_sum(in_ref, gate_out, up_out):
    total = in_ref[0].astype(F32)
    for k in range(1, SECOND):
        total += in_ref[k].astype(F32)
    full = jnp.concatenate([total, jnp.zeros((UP - HB, 128), F32)], axis=0).T
    gate_out[...] = full[:64, :HB]
    up_out[...] = full[64:, :HB]


def along_z(block, distance):
    n = lax.axis_size("z")
    return lax.ppermute(block, "z", [(i, (i + distance) % n) for i in range(n)])


def between_cores(block):
    return lax.ppermute(block, "c", [(0, 1), (1, 0)])


def on_device(tokens, cotangent, gate_weight, up_weight, down_weight, lengths, rewards):
    core = lax.axis_index("c").astype(jnp.int32).reshape(1)
    half = lax.dynamic_slice_in_dim(down_weight, lax.axis_index("c") * HH, HH, 0)
    next_half = along_z(half, -1)
    head = call(
        take_head, shape(HEAD, D), cost=0.01, in_specs=[VMEM, ANY],
    )(tokens, half)
    far_head = along_z(head, 1)
    own, other = call(
        split_rows, (shape(SLOTS, HALF), shape(SLOTS + MARK, HALF)),
        in_specs=[SMEM, SMEM, VMEM], cost=1.7,
    )(core, lengths, tokens)
    row_got = between_cores(other)
    rows, tail = call(
        merge_rows, (shape(2 * CAP, HALF), shape(2 * TAIL, HALF)), cost=0.01,
        in_specs=[SMEM, VMEM, VMEM],
    )(lengths, own, row_got)
    far_tail = along_z(tail, 1)
    cot_own = call(
        weigh, shape(SLOTS + MARK, D), in_specs=[SMEM, SMEM, VMEM, ANY], cost=0.01,
    )(lengths, rewards, cotangent, tail)
    cot_got = between_cores(cot_own)

    wide = call(
        split_wide, shape(2 * UP, HALF), in_specs=[SMEM, VMEM, VMEM, ANY], cost=0.01,
    )(core, gate_weight.T, up_weight.T, cot_own)
    near = call(
        near_terms, shape(2 * CAP, 2 * UP, kind=F32), cost=0.01, in_specs=[VMEM] * 2,
    )(rows, wide)
    near_got = between_cores(near)
    token = call(
        order_token, shape(8, 128, kind=F32), cost=2.7, in_specs=[ANY, ANY],
    )(next_half, far_head)
    cot_tail, back = call(
        next_back, (shape(2 * TAIL, D), shape(2 * CAP, 128)), cost=1.5,
        in_specs=[SMEM] + [VMEM] * 3 + [ANY, ANY],
    )(lengths, cot_own, cot_got, next_half, token, near_got)
    far_back = along_z(back, 1)
    back_near = call(
        near_back, shape(2 * CAP, 128), cost=0.01, in_specs=[VMEM] * 4 + [ANY],
    )(cot_own, cot_got, cot_tail, half, back)
    far_own, far_other_half = call(
        split_far, (shape(HEAD, HALF), shape(HEAD, HALF)), cost=0.01, in_specs=[SMEM, VMEM, ANY],
    )(core, far_head, back)
    far_got = between_cores(far_other_half)
    far = call(
        far_terms, shape(FAR + 128, 2 * UP), cost=10, in_specs=[VMEM] * 7
    )(far_head, gate_weight.T, up_weight.T, far_tail, wide, far_back, back_near)
    far_other = between_cores(far)

    each = HALF // FIRST
    whole = lambda *dims: pl.BlockSpec(dims, lambda i: (0,) * len(dims))
    part = lambda rows: pl.BlockSpec((rows, ABREAST * each), lambda i: (0, i))
    grads = call(
        weight_grads, shape(FIRST, 2 * HB, each),
        scratch=[pltpu.VMEM((4 * CAP, HB), BF)] * 2, cost=2.1,
        grid=(FIRST // ABREAST,),
        in_specs=[SMEM] + [whole(2 * CAP, 2 * UP)] * 2 + [whole(FAR + 128, 2 * UP)] * 2
        + [whole(2 * CAP, 128)] * 2
        + [part(2 * CAP), part(HEAD), part(HEAD), part(2 * TAIL)],
        out_specs=pl.BlockSpec((ABREAST, 2 * HB, each), lambda i: (i, 0, 0)),
    )(
        core, near, near_got, far, far_other, far_back, back_near,
        rows, far_own, far_got, far_tail,
    )
    grads = lax.all_to_all(grads, ("xh", "xl", "yl"), split_axis=0, concat_axis=0, tiled=True)
    grads = call(
        first_sum, shape(SECOND, HB, 128), cost=0.4,
    )(grads)
    grads = lax.all_to_all(grads, "yh", split_axis=0, concat_axis=0, tiled=True)
    return call(
        second_sum, (shape(64, HB, kind=F32), shape(64, HB, kind=F32)),
                in_specs=[VMEM],
    )(grads)


def solution(mesh):
    planes = mesh.shape["blk"]
    names = ("z", "xl", "yh", "yl", "xh", "c")
    fine = Mesh(mesh.devices.reshape(planes, 2, 4, 2, 2, 2), names)
    rows = P(names, None)
    placed = (rows, rows, P(None, "z"), P(None, "z"), P("z", None), rows, rows)
    out = P(names[1:], "z")
    return jax.shard_map(
        on_device, mesh=fine, in_specs=placed, out_specs=(out, out), check_vma=False
    )
```

time: 106 us -> 107 us (level)
  waiting for transfers between devices: 12.6 us -> 6.5 us
  starting transfers between devices: 36 us -> 41.3 us
  Pallas kernels: 11.2 us -> 13.2 us
    ppermute x4, waiting for transfers between devices: 11.8 us -> 3.51 us  [along_z(): return lax.ppermute(block, 'z', [(i, (i + distance) % n) for i in range(n)])]
    ppermute x4 -> x5, starting transfers between devices: 11.3 us -> 16.7 us  [between_cores(): return lax.ppermute(block, 'c', [(0, 1), (1, 0)])]
    ppermute x4 -> x5, waiting for transfers between devices: 0.87 us -> 2.99 us  [between_cores(): return lax.ppermute(block, 'c', [(0, 1), (1, 0)])]
    pallas_call x8 -> x9, Pallas kernels: 6.04 us -> 7.52 us  [the longest x1 1.88 us: on_device(): call(far_terms, shape(FAR + 128, 2 * UP), cost=10, in_specs=[VMEM] * 7)]
  transfers between devices with their start and end apart: 8 -> 9, of which waited for: 4 -> 3; matrix products, arithmetic and copies ran while one was open for 0% -> 0% of each run, Pallas kernels for 8% -> 9%
where the time goes in v4:
time: 107 us; the launch traced here: 106 us
  blocking collectives  42 us (39%)
  starting transfers between devices  41.3 us (39%)
  Pallas kernels  13.2 us (12%)
  waiting for transfers between devices  6.5 us (6%)
  local copies, waits for them, and re-layouts  1.58 us (1%)
    all_to_all x1, blocking collectives, on_device(): lax.all_to_all(grads, ('xh', 'xl', 'yl'), split_axis=0, concat_axis=0, ti...  28.1 us
    ppermute x4, starting transfers between devices, along_z(): return lax.ppermute(block, 'z', [(i, (i + distance) % n) for i in range(n)])  24.7 us
    ppermute x5, starting transfers between devices, between_cores(): return lax.ppermute(block, 'c', [(0, 1), (1, 0)])  16.7 us
    all_to_all x1, blocking collectives, on_device(): grads = lax.all_to_all(grads, 'yh', split_axis=0, concat_axis=0, tiled=True)  14 us
    ppermute x4, waiting for transfers between devices, along_z(): return lax.ppermute(block, 'z', [(i, (i + distance) % n) for i in range(n)])  3.51 us
    ppermute x5, waiting for transfers between devices, between_cores(): return lax.ppermute(block, 'c', [(0, 1), (1, 0)])  2.99 us
    pallas_call x1, Pallas kernels, on_device(): call(weight_grads, shape(FIRST, 2 * HB, each), scratch=[pltpu.VMEM((4 * C...  2.65 us
  transfers between devices with their start and end apart: 9, of which 3 were waited for; matrix products, arithmetic and copies ran while one was open for 0% of the time, Pallas kernels for 9%

profile of v4, /device:TPU:1, one launch (start us, length us, event | category | flops | bytes accessed | tf_op | source)
XLA Modules:
  0.0 105.5 jit_solution(1816856724519561769)
XLA Ops:
  0.6 0.0 copy-start
  0.7 1.5 %copy-done = bf16[224,4096]{1,0:T(8,128)(2,1)S(1)} copy-done((bf16[224,4096]{1,0:T(8,128)(2,1)S(1)}, bf16[224,4096]{1,0:T(8,128)(2,1)}, u32[]{:S(2)}) %copy-start) | copy-done | bytes 1835032
  2.1 0.1 constant_dynamic-slice_fusion.after_ref.down_ref
  2.2 18.8 %collective-permute-start.5 = (bf16[112,4096]{1,0:T(8,128)(2,1)S(1)}, bf16[112,4096]{1,0:T(8,128)(2,1)S(1)}, u32[]{:S(2)}, u32[]{:S(2)}) collective-permute-start(bf16[112,4096]{1,0:T(8,128)(2,1)S(1)} %constant_dynamic-slice_fusion.after_ref.down_ref), channel_id=1, source_target_pairs={{0,960},{64,0},{128,64},{192,128},{256,192},{320,256},{384,320},{4... | collective-permute-start | bytes 2752520 | tf_op jit(solution)/shard_map/ppermute | solution.py:264
  21.0 0.1 shard_map.91
  21.1 1.9 %collective-permute-start.2 = (bf16[96,4096]{1,0:T(8,128)(2,1)S(1)}, bf16[96,4096]{1,0:T(8,128)(2,1)S(1)}, u32[]{:S(2)}, u32[]{:S(2)}) collective-permute-start(bf16[96,4096]{1,0:T(8,128)(2,1)S(1)} %shard_map.91), channel_id=1, source_target_pairs={{0,64},{64,128},{128,192},{192,256},{256,320},{320,384},{384,448},... | collective-permute-start | bytes 2359304 | tf_op jit(solution)/shard_map/ppermute | solution.py:264
  23.0 0.0 copy-start.4
  23.0 0.0 copy-start.6
  23.0 1.1 %shard_map.86 = (bf16[160,2048]{1,0:T(8,128)(2,1)S(1)}, bf16[176,2048]{1,0:T(8,128)(2,1)S(1)}) custom-call(s32[1]{0:T(128)} %bitcast.core_ref, s32[1,4]{1,0:T(1,128)S(1)} %copy-done.5, bf16[160,4096]{1,0:T(8,128)(2,1)S(1)} %copy-done.3), custom_call_target="tpu_custom_call" | custom-call | flops 16999999488 | bytes 1700000 | tf_op jit(solution)/shard_map/pallas_call | solution.py:279
  24.1 2.9 %collective-permute-start = (bf16[176,2048]{1,0:T(8,128)(2,1)S(1)}, bf16[176,2048]{1,0:T(8,128)(2,1)S(1)}, u32[]{:S(2)}, u32[]{:S(2)}) collective-permute-start(bf16[176,2048]{1,0:T(8,128)(2,1)S(1)} %get-tuple-element.11), channel_id=1, source_target_pairs={{0,1},{1,0},{2,3},{3,2},{4,5},{5,4},{6,7},{7,6},{8,9},{9,8},{10,11... | collective-permute-start | bytes 2162696 | tf_op jit(solution)/shard_map/ppermute | solution.py:268
  27.0 1.8 %collective-permute-done.got_ref = bf16[176,2048]{1,0:T(8,128)(2,1)S(1)} collective-permute-done((bf16[176,2048]{1,0:T(8,128)(2,1)S(1)}, bf16[176,2048]{1,0:T(8,128)(2,1)S(1)}, u32[]{:S(2)}, u32[]{:S(2)}) %collective-permute-start) | collective-permute-done | bytes 720928 | tf_op jit(solution)/shard_map/ppermute | solution.py:268
  28.8 0.8 shard_map.87
  29.6 2.1 %collective-permute-start.3 = (bf16[64,2048]{1,0:T(8,128)(2,1)S(1)}, bf16[64,2048]{1,0:T(8,128)(2,1)S(1)}, u32[]{:S(2)}, u32[]{:S(2)}) collective-permute-start(bf16[64,2048]{1,0:T(8,128)(2,1)S(1)} %get-tuple-element.13.after_ref), channel_id=1, source_target_pairs={{0,64},{64,128},{128,192},{192,256},{256,320},{320,384},{384,448},... | collective-permute-start | bytes 786440 | tf_op jit(solution)/shard_map/ppermute | solution.py:264
  31.7 0.8 shard_map.88.after_ref.own_ref
  32.5 2.3 %collective-permute-start.4 = (bf16[176,4096]{1,0:T(8,128)(2,1)S(1)}, bf16[176,4096]{1,0:T(8,128)(2,1)S(1)}, u32[]{:S(2)}, u32[]{:S(2)}) collective-permute-start(bf16[176,4096]{1,0:T(8,128)(2,1)S(1)} %shard_map.88.after_ref.own_ref), channel_id=1, source_target_pairs={{0,1},{1,0},{2,3},{3,2},{4,5},{5,4},{6,7},{7,6},{8,9},{9,8},{10,11... | collective-permute-start | bytes 4325384 | tf_op jit(solution)/shard_map/ppermute | solution.py:268
  34.8 1.1 %shard_map.89.wide_ref = bf16[512,2048]{1,0:T(8,128)(2,1)S(1)} custom-call(s32[1]{0:T(128)} %bitcast.core_ref, bf16[224,4096]{1,0:T(8,128)(2,1)S(1)} %bitcast.3, bf16[224,4096]{1,0:T(8,128)(2,1)S(1)} %bitcast.5, bf16[176,4096]{1,0:T(8,128)(2,1)S(1)} %shard_map.88.after_ref.own_ref), custom_call_target="tpu_custom_call" | custom-call | flops 100000000 | bytes 10000 | tf_op jit(solution)/shard_map/pallas_call | solution.py:294
  36.0 0.7 shard_map.90.near_ref
  36.7 2.0 %collective-permute-start.1 = (f32[256,512]{1,0:T(8,128)S(1)}, f32[256,512]{1,0:T(8,128)S(1)}, u32[]{:S(2)}, u32[]{:S(2)}) collective-permute-start(f32[256,512]{1,0:T(8,128)S(1)} %shard_map.90.near_ref), channel_id=1, source_target_pairs={{0,1},{1,0},{2,3},{3,2},{4,5},{5,4},{6,7},{7,6},{8,9},{9,8},{10,11... | collective-permute-start | bytes 1572872 | tf_op jit(solution)/shard_map/ppermute | solution.py:268
  38.8 3.5 %collective-permute-done.2.behind_ref.head_ref.row_ref = bf16[96,4096]{1,0:T(8,128)(2,1)S(1)} collective-permute-done((bf16[96,4096]{1,0:T(8,128)(2,1)S(1)}, bf16[96,4096]{1,0:T(8,128)(2,1)S(1)}, u32[]{:S(2)}, u32[]{:S(2)}) %collective-permute-start.2) | collective-permute-done | bytes 786464 | tf_op jit(solution)/shard_map/ppermute | solution.py:264
  42.3 1.8 %shard_map.93 = (bf16[64,4096]{1,0:T(8,128)(2,1)S(1)}, bf16[256,128]{1,0:T(8,128)(2,1)S(1)}) custom-call(s32[1,4]{1,0:T(1,128)S(1)} %copy-done.5, bf16[176,4096]{1,0:T(8,128)(2,1)S(1)} %shard_map.88.after_ref.own_ref, bf16[176,4096]{1,0:T(8,128)(2,1)S(1)} %collective-permute-done.4.got_ref, bf16[112,4096]{1,0:T(8,128)(2,1)S(1)} %collective-permute-done.5.after_ref.next_ref, ...), custom_call_target="tpu_custom_call" | custom-call | flops 15000000512 | bytes 1500000 | tf_op jit(solution)/shard_map/pallas_call | solution.py:304
  44.1 1.9 %collective-permute-start.6 = (bf16[256,128]{1,0:T(8,128)(2,1)S(1)}, bf16[256,128]{1,0:T(8,128)(2,1)S(1)}, u32[]{:S(2)}, u32[]{:S(2)}) collective-permute-start(bf16[256,128]{1,0:T(8,128)(2,1)S(1)} %get-tuple-element.14.after_ref), channel_id=1, source_target_pairs={{0,64},{64,128},{128,192},{192,256},{256,320},{320,384},{384,448},... | collective-permute-start | bytes 196616 | tf_op jit(solution)/shard_map/ppermute | solution.py:264
  46.0 0.5 shard_map.96
  46.5 5.2 %collective-permute-start.8 = (bf16[96,2048]{1,0:T(8,128)(2,1)S(1)}, bf16[96,2048]{1,0:T(8,128)(2,1)S(1)}, u32[]{:S(2)}, u32[]{:S(2)}) collective-permute-start(bf16[96,2048]{1,0:T(8,128)(2,1)S(1)} %get-tuple-element.17), channel_id=1, source_target_pairs={{0,1},{1,0},{2,3},{3,2},{4,5},{5,4},{6,7},{7,6},{8,9},{9,8},{10,11... | collective-permute-start | bytes 1179656 | tf_op jit(solution)/shard_map/ppermute | solution.py:268
  51.7 0.7 shard_map.94.near_ref.near_back_ref
  52.5 1.9 %shard_map.95.mine_ref = bf16[288,512]{1,0:T(8,128)(2,1)S(1)} custom-call(bf16[96,4096]{1,0:T(8,128)(2,1)S(1)} %collective-permute-done.2.behind_ref.head_ref.row_ref, bf16[224,4096]{1,0:T(8,128)(2,1)S(1)} %bitcast.4, bf16[224,4096]{1,0:T(8,128)(2,1)S(1)} %bitcast.6, bf16[64,2048]{1,0:T(8,128)(2,1)S(1)} %collective-permute-done.3.tail_ref.far_tail_ref, ...), custom_call_target="tpu_custom_call" | custom-call | flops 99999997952 | bytes 10000000 | tf_op jit(solution)/shard_map/pallas_call | solution.py:316
  54.4 4.2 %collective-permute-start.7 = (bf16[288,512]{1,0:T(8,128)(2,1)S(1)}, bf16[288,512]{1,0:T(8,128)(2,1)S(1)}, u32[]{:S(2)}, u32[]{:S(2)}) collective-permute-start(bf16[288,512]{1,0:T(8,128)(2,1)S(1)} %shard_map.95.mine_ref), channel_id=1, source_target_pairs={{0,1},{1,0},{2,3},{3,2},{4,5},{5,4},{6,7},{7,6},{8,9},{9,8},{10,11... | collective-permute-start | bytes 884744 | tf_op jit(solution)/shard_map/ppermute | solution.py:268
  58.6 1.2 %collective-permute-done.7.other_ref = bf16[288,512]{1,0:T(8,128)(2,1)S(1)} collective-permute-done((bf16[288,512]{1,0:T(8,128)(2,1)S(1)}, bf16[288,512]{1,0:T(8,128)(2,1)S(1)}, u32[]{:S(2)}, u32[]{:S(2)}) %collective-permute-start.7) | collective-permute-done | bytes 294944 | tf_op jit(solution)/shard_map/ppermute | solution.py:268
  59.8 2.7 %shard_map.97 = bf16[8,448,256]{2,1,0:T(8,128)(2,1)S(1)} custom-call(s32[1]{0:T(128)} %bitcast.core_ref, f32[256,512]{1,0:T(8,128)S(1)} %shard_map.90.near_ref, f32[256,512]{1,0:T(8,128)S(1)} %collective-permute-done.1.behind_ref.near_got_ref, bf16[288,512]{1,0:T(8,128)(2,1)S(1)} %shard_map.95.mine_ref, ...), custom_call_target="tpu_custom_call" | custom-call | flops 20999999488 | bytes 2100000 | tf_op jit(solution)/shard_map/pallas_call | solution.py:324
  62.4 28.1 %all_to_all.10.in_ref = bf16[8,448,256]{2,1,0:T(8,128)(2,1)S(1)} all-to-all(bf16[8,448,256]{2,1,0:T(8,128)(2,1)S(1)} %shard_map.97), channel_id=1, replica_groups=mesh['z'=16,'xl'=2,'yh'=4,'yl'=2,'xh'=2,'c'=2] {'xh','xl','yl'}, dimensions={0} | all-to-all | bytes 3670016 | tf_op jit(solution)/shard_map/all_to_all | solution.py:336
  90.5 0.3 shard_map.98
  90.8 14.0 %all_to_all.11.in_ref = bf16[4,224,128]{2,1,0:T(8,128)(2,1)S(1)} all-to-all(bf16[4,224,128]{2,1,0:T(8,128)(2,1)S(1)} %shard_map.98), channel_id=1, replica_groups=mesh['z'=16,'xl'=2,'yh'=4,'yl'=2,'xh'=2,'c'=2] {'yh'}, dimensions={0} | all-to-all | bytes 458752 | tf_op jit(solution)/shard_map/all_to_all | solution.py:340
  104.8 0.7 shard_map.99
  (17 shorter events, 0.0 us)
Async XLA Ops:
  0.6 1.5 %copy-start = (bf16[224,4096]{1,0:T(8,128)(2,1)S(1)}, bf16[224,4096]{1,0:T(8,128)(2,1)}, u32[]{:S(2)}) copy-start(bf16[224,4096]{1,0:T(8,128)(2,1)} %param.11) | copy-start | bytes 5505028
  0.6 20.4 %copy-start.3 = (bf16[160,4096]{1,0:T(8,128)(2,1)S(1)}, bf16[160,4096]{1,0:T(8,128)(2,1)}, u32[]{:S(2)}) copy-start(bf16[160,4096]{1,0:T(8,128)(2,1)} %tok_ref.3) | copy-start | bytes 3932164
  2.2 20.8 %copy-start.5 = (s32[1,4]{1,0:T(1,128)S(1)}, s32[1,4]{1,0:T(1,128)}, u32[]{:S(2)}) copy-start(s32[1,4]{1,0:T(1,128)} %len_ref.7) | copy-start | bytes 52
  2.2 40.1 %collective-permute-start.5 = (bf16[112,4096]{1,0:T(8,128)(2,1)S(1)}, bf16[112,4096]{1,0:T(8,128)(2,1)S(1)}, u32[]{:S(2)}, u32[]{:S(2)}) collective-permute-start(bf16[112,4096]{1,0:T(8,128)(2,1)S(1)} %constant_dynamic-slice_fusion.after_ref.down_ref), channel_id=1, source_target_pairs={{0,960},{64,0},{128,64},{192,128},{256,192},{320,256},{384,320},{4... | collective-permute-start | bytes 2752520 | tf_op jit(solution)/shard_map/ppermute | solution.py:264
  21.1 21.2 %collective-permute-start.2 = (bf16[96,4096]{1,0:T(8,128)(2,1)S(1)}, bf16[96,4096]{1,0:T(8,128)(2,1)S(1)}, u32[]{:S(2)}, u32[]{:S(2)}) collective-permute-start(bf16[96,4096]{1,0:T(8,128)(2,1)S(1)} %shard_map.91), channel_id=1, source_target_pairs={{0,64},{64,128},{128,192},{192,256},{256,320},{320,384},{384,448},... | collective-permute-start | bytes 2359304 | tf_op jit(solution)/shard_map/ppermute | solution.py:264
  23.0 8.7 %copy-start.4 = (bf16[160,4096]{1,0:T(8,128)(2,1)S(1)}, bf16[160,4096]{1,0:T(8,128)(2,1)}, u32[]{:S(2)}) copy-start(bf16[160,4096]{1,0:T(8,128)(2,1)} %cot_ref.1) | copy-start | bytes 3932164
  23.0 8.7 %copy-start.6 = (s32[1,4]{1,0:T(1,128)S(1)}, s32[1,4]{1,0:T(1,128)}, u32[]{:S(2)}) copy-start(s32[1,4]{1,0:T(1,128)} %rew_ref.1) | copy-start | bytes 52
  24.1 4.7 %collective-permute-start = (bf16[176,2048]{1,0:T(8,128)(2,1)S(1)}, bf16[176,2048]{1,0:T(8,128)(2,1)S(1)}, u32[]{:S(2)}, u32[]{:S(2)}) collective-permute-start(bf16[176,2048]{1,0:T(8,128)(2,1)S(1)} %get-tuple-element.11), channel_id=1, source_target_pairs={{0,1},{1,0},{2,3},{3,2},{4,5},{5,4},{6,7},{7,6},{8,9},{9,8},{10,11... | collective-permute-start | bytes 2162696 | tf_op jit(solution)/shard_map/ppermute | solution.py:268
  28.8 6.0 %copy-start.2 = (bf16[4096,224]{0,1:T(8,128)(2,1)S(1)}, bf16[4096,224]{0,1:T(8,128)(2,1)}, u32[]{:S(2)}) copy-start(bf16[4096,224]{0,1:T(8,128)(2,1)} %param.10) | copy-start | bytes 5505028
  29.6 5.2 %copy-start.1 = (bf16[4096,224]{0,1:T(8,128)(2,1)S(1)}, bf16[4096,224]{0,1:T(8,128)(2,1)}, u32[]{:S(2)}) copy-start(bf16[4096,224]{0,1:T(8,128)(2,1)} %param.9) | copy-start | bytes 5505028
  29.6 22.9 %collective-permute-start.3 = (bf16[64,2048]{1,0:T(8,128)(2,1)S(1)}, bf16[64,2048]{1,0:T(8,128)(2,1)S(1)}, u32[]{:S(2)}, u32[]{:S(2)}) collective-permute-start(bf16[64,2048]{1,0:T(8,128)(2,1)S(1)} %get-tuple-element.13.after_ref), channel_id=1, source_target_pairs={{0,64},{64,128},{128,192},{192,256},{256,320},{320,384},{384,448},... | collective-permute-start | bytes 786440 | tf_op jit(solution)/shard_map/ppermute | solution.py:264
  32.5 9.8 %collective-permute-start.4 = (bf16[176,4096]{1,0:T(8,128)(2,1)S(1)}, bf16[176,4096]{1,0:T(8,128)(2,1)S(1)}, u32[]{:S(2)}, u32[]{:S(2)}) collective-permute-start(bf16[176,4096]{1,0:T(8,128)(2,1)S(1)} %shard_map.88.after_ref.own_ref), channel_id=1, source_target_pairs={{0,1},{1,0},{2,3},{3,2},{4,5},{5,4},{6,7},{7,6},{8,9},{9,8},{10,11... | collective-permute-start | bytes 4325384 | tf_op jit(solution)/shard_map/ppermute | solution.py:268
  36.7 5.6 %collective-permute-start.1 = (f32[256,512]{1,0:T(8,128)S(1)}, f32[256,512]{1,0:T(8,128)S(1)}, u32[]{:S(2)}, u32[]{:S(2)}) collective-permute-start(f32[256,512]{1,0:T(8,128)S(1)} %shard_map.90.near_ref), channel_id=1, source_target_pairs={{0,1},{1,0},{2,3},{3,2},{4,5},{5,4},{6,7},{7,6},{8,9},{9,8},{10,11... | collective-permute-start | bytes 1572872 | tf_op jit(solution)/shard_map/ppermute | solution.py:268
  44.1 8.4 %collective-permute-start.6 = (bf16[256,128]{1,0:T(8,128)(2,1)S(1)}, bf16[256,128]{1,0:T(8,128)(2,1)S(1)}, u32[]{:S(2)}, u32[]{:S(2)}) collective-permute-start(bf16[256,128]{1,0:T(8,128)(2,1)S(1)} %get-tuple-element.14.after_ref), channel_id=1, source_target_pairs={{0,64},{64,128},{128,192},{192,256},{256,320},{320,384},{384,448},... | collective-permute-start | bytes 196616 | tf_op jit(solution)/shard_map/ppermute | solution.py:264
  46.5 13.3 %collective-permute-start.8 = (bf16[96,2048]{1,0:T(8,128)(2,1)S(1)}, bf16[96,2048]{1,0:T(8,128)(2,1)S(1)}, u32[]{:S(2)}, u32[]{:S(2)}) collective-permute-start(bf16[96,2048]{1,0:T(8,128)(2,1)S(1)} %get-tuple-element.17), channel_id=1, source_target_pairs={{0,1},{1,0},{2,3},{3,2},{4,5},{5,4},{6,7},{7,6},{8,9},{9,8},{10,11... | collective-permute-start | bytes 1179656 | tf_op jit(solution)/shard_map/ppermute | solution.py:268
  54.4 5.4 %collective-permute-start.7 = (bf16[288,512]{1,0:T(8,128)(2,1)S(1)}, bf16[288,512]{1,0:T(8,128)(2,1)S(1)}, u32[]{:S(2)}, u32[]{:S(2)}) collective-permute-start(bf16[288,512]{1,0:T(8,128)(2,1)S(1)} %shard_map.95.mine_ref), channel_id=1, source_target_pairs={{0,1},{1,0},{2,3},{3,2},{4,5},{5,4},{6,7},{7,6},{8,9},{9,8},{10,11... | collective-permute-start | bytes 884744 | tf_op jit(solution)/shard_map/ppermute | solution.py:268

commit v5 on v3

--- a/solution.py
+++ b/solution.py
@@ -133,25 +133,27 @@
     out_ref[...] = jnp.zeros_like(out_ref)
 
 
-def merge_cot(len_ref, own_ref, got_ref, after_ref, cot_out):
-    own, got = own_ref[:SLOTS, :], got_ref[:SLOTS, :]
-    cot_out[:HEAD, :] = own[:HEAD]
-    cot_out[HEAD:CAP, :] = merged(own[HEAD:CAP], got[CAP:], live(len_ref))
-    cot_out[CAP : CAP + HEAD, :] = got[:HEAD]
-    cot_out[CAP + HEAD :, :] = merged(got[HEAD:CAP], own[CAP:], other_count(got_ref))
-
-
-def near_terms(head_ref, tail_ref, far_head_ref, cot_ref, wide_ref, down_ref, sum_out):
+def near_terms(
+    head_ref, tail_ref, far_head_ref, own_ref, got_ref, cot_ref, wide_ref, down_ref, sum_out
+):
+    parts = (own_ref[:HEAD, :], cot_ref[:TAIL, :], got_ref[:HEAD, :], cot_ref[TAIL:, :])
+    cot = jnp.concatenate(parts, axis=0)
     rows = jnp.concatenate([head_ref[...], tail_ref[...], far_head_ref[...]], axis=0)
     sum_out[:, : 2 * UP] = mm(rows, wide_ref[...], ((1,), (1,)))
-    sum_out[: 2 * CAP, 2 * UP : 2 * UP + HH] = mm(cot_ref[...], down_ref[...], ((1,), (1,)))
+    sum_out[: 2 * CAP, 2 * UP : 2 * UP + HH] = mm(cot, down_ref[...], ((1,), (1,)))
     sum_out[: 2 * CAP, 2 * UP + HH :] = jnp.zeros((2 * CAP, 128 - HH), F32)
     sum_out[2 * CAP :, 2 * UP :] = jnp.zeros((HEAD, 128), F32)
 
 
-def next_back(cot_ref, down_ref, out_ref):
-    out_ref[:, :HH] = mm(cot_ref[...], down_ref[...], ((1,), (1,))).astype(out_ref.dtype)
-    out_ref[:, HH:] = jnp.zeros((2 * CAP, 128 - HH), out_ref.dtype)
+def next_back(len_ref, own_ref, got_ref, next_ref, after_ref, cot_out, back_out):
+    own, got, weights = own_ref[:SLOTS, :], got_ref[:SLOTS, :], next_ref[...]
+    own_tail = merged(own[HEAD:CAP], got[CAP:], live(len_ref))
+    got_tail = merged(got[HEAD:CAP], own[CAP:], other_count(got_ref))
+    back_out[:, HH:] = jnp.zeros((2 * CAP, 128 - HH), BF)
+    cot = jnp.concatenate([own[:HEAD], own_tail, got[:HEAD], got_tail], axis=0)
+    back_out[:, :HH] = mm(cot, weights, ((1,), (1,))).astype(BF)
+    cot_out[:TAIL, :] = own_tail
+    cot_out[TAIL:, :] = got_tail
 
 
 def far_terms(tail_ref, wide_ref, back_ref, out_ref):
@@ -189,38 +191,33 @@
 
 def weight_grads(
     core_ref, early_ref, mine_ref, other_ref, back_ref, gate_ref, up_ref,
-    head_ref, tail_ref, far_head_ref, far_tail_ref, out_ref, gate_all, up_all,
+    head_ref, tail_ref, far_head_ref, far_tail_ref, out_ref,
 ):
-    @pl.when(pl.program_id(0) == 0)
-    def _():
-        mine, other = mine_ref[...].astype(F32), other_ref[...].astype(F32)
-        early = early_ref[...]
-        total = jnp.concatenate(
-            [
-                early[:HEAD] + other[TAIL : TAIL + HEAD],
-                mine[:TAIL] + other[TAIL + HEAD : CAP + TAIL],
-                early[CAP : CAP + HEAD] + mine[TAIL : TAIL + HEAD],
-                mine[TAIL + HEAD : CAP + TAIL] + other[:TAIL],
-            ],
-            axis=0,
-        )
-        cross = other[CAP + TAIL :]
-        cross = jnp.concatenate([cross[:, k * 128 : (k + 1) * 128] for k in range(4)], axis=0)
-        back = both_halves(core_ref[0], back_ref[...].astype(F32), swapped(cross))
-        gate_all[2 * CAP :], up_all[2 * CAP :] = hidden_grads(
-            total[:, :HB], total[:, UP : UP + HB], back
-        )
-        gate_all[: 2 * CAP] = gate_ref[...]
-        up_all[: 2 * CAP] = up_ref[...]
-
-    rows = jnp.concatenate(
-        [head_ref[...], tail_ref[...], far_head_ref[...], far_tail_ref[...]], axis=0
+    mine, other = mine_ref[...].astype(F32), other_ref[...].astype(F32)
+    early = early_ref[...]
+    total = jnp.concatenate(
+        [
+            early[:HEAD] + other[TAIL : TAIL + HEAD],
+            mine[:TAIL] + other[TAIL + HEAD : CAP + TAIL],
+            early[CAP : CAP + HEAD] + mine[TAIL : TAIL + HEAD],
+            mine[TAIL + HEAD : CAP + TAIL] + other[:TAIL],
+        ],
+        axis=0,
     )
-    each = HALF // FIRST
-    for at, weights in ((0, gate_all), (HB, up_all)):
-        total = mm(weights[...], rows, ((0,), (0,))).astype(BF)
-        for k in range(ABREAST):
-            out_ref[k, at : at + HB] = total[:, k * each : (k + 1) * each]
+    cross = other[CAP + TAIL :]
+    cross = jnp.concatenate([cross[:, k * 128 : (k + 1) * 128] for k in range(4)], axis=0)
+    back = both_halves(core_ref[0], back_ref[...].astype(F32), swapped(cross))
+    gate, up = hidden_grads(total[:, :HB], total[:, UP : UP + HB], back)
+    gate = jnp.concatenate([gate_ref[...], gate], axis=0)
+    up = jnp.concatenate([up_ref[...], up], axis=0)
+    each, parts = HALF // FIRST, (head_ref, tail_ref, far_head_ref, far_tail_ref)
+    for k in range(0, FIRST, ABREAST):
+        columns = slice(k * each, (k + ABREAST) * each)
+        rows = jnp.concatenate([ref[:, columns] for ref in parts], axis=0)
+        for at, weights in ((0, gate), (HB, up)):
+            grads = mm(weights, rows, ((0,), (0,))).astype(BF)
+            for m in range(ABREAST):
+                out_ref[k + m, at : at + HB] = grads[:, m * each : (m + 1) * each]
 
 
 def first_sum(in_ref, out_ref):
@@ -277,21 +274,18 @@
     token = call(
         order_token, shape(8, 128, kind=F32), cost=2.7, in_specs=[ANY],
     )(next_half)
-    cot_rows = call(
-        merge_cot, shape(2 * CAP, D), cost=1, in_specs=[SMEM] + [VMEM] * 2 + [ANY],
-    )(lengths, cot_own, cot_got, token)
-    back = call(
-        next_back, shape(2 * CAP, 128), cost=0.5,
-        in_specs=[VMEM] * 2,
-    )(cot_rows, next_half)
+    cot_tail, back = call(
+        next_back, (shape(2 * TAIL, D), shape(2 * CAP, 128)), cost=1.5,
+        in_specs=[SMEM] + [VMEM] * 3 + [ANY],
+    )(lengths, cot_own, cot_got, next_half, token)
     far_back = along_z(back, 1)
     wide = call(
         split_wide, shape(2 * UP, HALF), in_specs=[SMEM, VMEM, VMEM, ANY], cost=0.01,
     )(core, gate_weight.T, up_weight.T, back)
     near = call(
         near_terms, shape(2 * CAP + HEAD, 2 * UP + 128, kind=F32),
-        cost=0.01, in_specs=[VMEM] * 6,
-    )(head, tail, far_head, cot_rows, wide, half)
+        cost=0.01, in_specs=[VMEM] * 8,
+    )(head, tail, far_head, cot_own, cot_got, cot_tail, wide, half)
     near_other = between_cores(near)
     gate_near, up_near, early = call(
         near_grads,
@@ -303,17 +297,8 @@
     )(far_tail, wide, far_back)
     far_other = between_cores(far)
 
-    each = HALF // FIRST
-    whole = lambda *dims: pl.BlockSpec(dims, lambda i: (0,) * len(dims))
-    part = lambda rows: pl.BlockSpec((rows, ABREAST * each), lambda i: (0, i))
     grads = call(
-        weight_grads, shape(FIRST, 2 * HB, each),
-        scratch=[pltpu.VMEM((4 * CAP, HB), BF)] * 2, cost=2.1,
-        grid=(FIRST // ABREAST,),
-        in_specs=[SMEM, whole(2 * CAP, 2 * UP)] + [whole(CAP + TAIL + 64, 2 * UP)] * 2
-        + [whole(2 * CAP, 128)] + [whole(2 * CAP, HB)] * 2
-        + [part(HEAD), part(CAP + TAIL)] * 2,
-        out_specs=pl.BlockSpec((ABREAST, 2 * HB, each), lambda i: (i, 0, 0)),
+        weight_grads, shape(FIRST, 2 * HB, HALF // FIRST), cost=2.1, in_specs=[SMEM] + [VMEM] * 10,
     )(core, early, far, far_other, far_back, gate_near, up_near, head, tail, far_head, far_tail)
     grads = lax.all_to_all(grads, ("xh", "xl", "yl"), split_axis=0, concat_axis=0, tiled=True)
     grads = call(

time: 106 us -> 105 us (level)
  Pallas kernels: 11.2 us -> 10.1 us
    pallas_call x3 -> x2, Pallas kernels: 3.79 us -> 2.71 us  [the longest x1 1.43 us: on_device(): call(next_back, (shape(2 * TAIL, D), shape(2 * CAP, 128)), cost=1.5, in_s...]
where the time goes in v5:
time: 105 us; the launch traced here: 103 us
  blocking collectives  42 us (40%)
  starting transfers between devices  35.8 us (34%)
  waiting for transfers between devices  13 us (12%)
  Pallas kernels  10.1 us (10%)
  local copies, waits for them, and re-layouts  1.57 us (1%)
    all_to_all x1, blocking collectives, on_device(): lax.all_to_all(grads, ('xh', 'xl', 'yl'), split_axis=0, concat_axis=0, ti...  28.1 us
    ppermute x4, starting transfers between devices, along_z(): return lax.ppermute(block, 'z', [(i, (i + distance) % n) for i in range(n)])  24.5 us
    all_to_all x1, blocking collectives, on_device(): grads = lax.all_to_all(grads, 'yh', split_axis=0, concat_axis=0, tiled=True)  14 us
    ppermute x4, waiting for transfers between devices, along_z(): return lax.ppermute(block, 'z', [(i, (i + distance) % n) for i in range(n)])  12.1 us
    ppermute x4, starting transfers between devices, between_cores(): return lax.ppermute(block, 'c', [(0, 1), (1, 0)])  11.3 us
  transfers between devices with their start and end apart: 8, of which 4 were waited for; matrix products, arithmetic and copies ran while one was open for 0% of the time, Pallas kernels for 8%

profile of v5, /device:TPU:1, one launch (start us, length us, event | category | flops | bytes accessed | tf_op | source)
XLA Modules:
  0.0 103.4 jit_solution(18280918991193174233)
XLA Ops:
  0.6 0.0 copy-start
  0.7 1.5 %copy-done = bf16[224,4096]{1,0:T(8,128)(2,1)S(1)} copy-done((bf16[224,4096]{1,0:T(8,128)(2,1)S(1)}, bf16[224,4096]{1,0:T(8,128)(2,1)}, u32[]{:S(2)}) %copy-start) | copy-done | bytes 1835032
  2.1 0.1 constant_dynamic-slice_fusion.down_ref
  2.2 18.8 %collective-permute-start.3 = (bf16[112,4096]{1,0:T(8,128)(2,1)S(1)}, bf16[112,4096]{1,0:T(8,128)(2,1)S(1)}, u32[]{:S(2)}, u32[]{:S(2)}) collective-permute-start(bf16[112,4096]{1,0:T(8,128)(2,1)S(1)} %constant_dynamic-slice_fusion.down_ref), channel_id=1, source_target_pairs={{0,960},{64,0},{128,64},{192,128},{256,192},{320,256},{384,320},{4... | collective-permute-start | bytes 2752520 | tf_op jit(solution)/shard_map/ppermute | solution.py:246
  21.0 0.0 copy-start.5
  21.0 1.1 %shard_map.86 = (bf16[96,2048]{1,0:T(8,128)(2,1)S(1)}, bf16[64,2048]{1,0:T(8,128)(2,1)S(1)}, bf16[176,2048]{1,0:T(8,128)(2,1)S(1)}) custom-call(s32[1]{0:T(128)} %bitcast.core_ref, s32[1,4]{1,0:T(1,128)S(1)} %copy-done.4, bf16[160,4096]{1,0:T(8,128)(2,1)S(1)} %copy-done.6), custom_call_target="tpu_custom_call" | custom-call | flops 16999999488 | bytes 1700000 | tf_op jit(solution)/shard_map/pallas_call | solution.py:257
  22.1 0.0 copy-start.3
  22.1 3.0 %collective-permute-start = (bf16[176,2048]{1,0:T(8,128)(2,1)S(1)}, bf16[176,2048]{1,0:T(8,128)(2,1)S(1)}, u32[]{:S(2)}, u32[]{:S(2)}) collective-permute-start(bf16[176,2048]{1,0:T(8,128)(2,1)S(1)} %get-tuple-element.12), channel_id=1, source_target_pairs={{0,1},{1,0},{2,3},{3,2},{4,5},{5,4},{6,7},{7,6},{8,9},{9,8},{10,11... | collective-permute-start | bytes 2162696 | tf_op jit(solution)/shard_map/ppermute | solution.py:250
  25.1 1.9 %collective-permute-start.1 = (bf16[96,2048]{1,0:T(8,128)(2,1)S(1)}, bf16[96,2048]{1,0:T(8,128)(2,1)S(1)}, u32[]{:S(2)}, u32[]{:S(2)}) collective-permute-start(bf16[96,2048]{1,0:T(8,128)(2,1)S(1)} %get-tuple-element.10.head_ref), channel_id=1, source_target_pairs={{0,64},{64,128},{128,192},{192,256},{256,320},{320,384},{384,448},... | collective-permute-start | bytes 1179656 | tf_op jit(solution)/shard_map/ppermute | solution.py:246
  27.0 0.0 collective-permute-done.got_ref
  27.0 0.8 shard_map.87.after_ref.tail_ref
  27.8 1.9 %collective-permute-start.5 = (bf16[160,2048]{1,0:T(8,128)(2,1)S(1)}, bf16[160,2048]{1,0:T(8,128)(2,1)S(1)}, u32[]{:S(2)}, u32[]{:S(2)}) collective-permute-start(bf16[160,2048]{1,0:T(8,128)(2,1)S(1)} %shard_map.87.after_ref.tail_ref), channel_id=1, source_target_pairs={{0,64},{64,128},{128,192},{192,256},{256,320},{320,384},{384,448},... | collective-permute-start | bytes 1966088 | tf_op jit(solution)/shard_map/ppermute | solution.py:246
  29.8 0.8 shard_map.88.own_ref
  30.6 2.1 %collective-permute-start.2 = (bf16[176,4096]{1,0:T(8,128)(2,1)S(1)}, bf16[176,4096]{1,0:T(8,128)(2,1)S(1)}, u32[]{:S(2)}, u32[]{:S(2)}) collective-permute-start(bf16[176,4096]{1,0:T(8,128)(2,1)S(1)} %shard_map.88.own_ref), channel_id=1, source_target_pairs={{0,1},{1,0},{2,3},{3,2},{4,5},{5,4},{6,7},{7,6},{8,9},{9,8},{10,11... | collective-permute-start | bytes 4325384 | tf_op jit(solution)/shard_map/ppermute | solution.py:250
  32.8 7.2 %collective-permute-done.3.after_ref.next_ref = bf16[112,4096]{1,0:T(8,128)(2,1)S(1)} collective-permute-done((bf16[112,4096]{1,0:T(8,128)(2,1)S(1)}, bf16[112,4096]{1,0:T(8,128)(2,1)S(1)}, u32[]{:S(2)}, u32[]{:S(2)}) %collective-permute-start.3) | collective-permute-done | bytes 917536 | tf_op jit(solution)/shard_map/ppermute | solution.py:246
  40.0 1.4 %shard_map.90 = (bf16[64,4096]{1,0:T(8,128)(2,1)S(1)}, bf16[256,128]{1,0:T(8,128)(2,1)S(1)}) custom-call(s32[1,4]{1,0:T(1,128)S(1)} %copy-done.4, bf16[176,4096]{1,0:T(8,128)(2,1)S(1)} %shard_map.88.own_ref, bf16[176,4096]{1,0:T(8,128)(2,1)S(1)} %collective-permute-done.2.got_ref, bf16[112,4096]{1,0:T(8,128)(2,1)S(1)} %collective-permute-done.3.after_ref.next_ref, ...), custom_call_target="tpu_custom_call" | custom-call | flops 15000000512 | bytes 1500000 | tf_op jit(solution)/shard_map/pallas_call | solution.py:277
  41.4 1.9 %collective-permute-start.6 = (bf16[256,128]{1,0:T(8,128)(2,1)S(1)}, bf16[256,128]{1,0:T(8,128)(2,1)S(1)}, u32[]{:S(2)}, u32[]{:S(2)}) collective-permute-start(bf16[256,128]{1,0:T(8,128)(2,1)S(1)} %get-tuple-element.14.after_ref), channel_id=1, source_target_pairs={{0,64},{64,128},{128,192},{192,256},{256,320},{320,384},{384,448},... | collective-permute-start | bytes 196616 | tf_op jit(solution)/shard_map/ppermute | solution.py:246
  43.4 1.1 %shard_map.91.wide_ref = bf16[512,2048]{1,0:T(8,128)(2,1)S(1)} custom-call(s32[1]{0:T(128)} %bitcast.core_ref, bf16[224,4096]{1,0:T(8,128)(2,1)S(1)} %bitcast.3, bf16[224,4096]{1,0:T(8,128)(2,1)S(1)} %bitcast.4, bf16[256,128]{1,0:T(8,128)(2,1)S(1)} %get-tuple-element.14.after_ref), custom_call_target="tpu_custom_call" | custom-call | flops 100000000 | bytes 10000 | tf_op jit(solution)/shard_map/pallas_call | solution.py:282
  44.5 0.0 collective-permute-done.1.far_head_ref
  44.5 1.5 %shard_map.92.mine_ref = f32[352,640]{1,0:T(8,128)S(1)} custom-call(bf16[96,2048]{1,0:T(8,128)(2,1)S(1)} %get-tuple-element.10.head_ref, bf16[160,2048]{1,0:T(8,128)(2,1)S(1)} %shard_map.87.after_ref.tail_ref, bf16[96,2048]{1,0:T(8,128)(2,1)S(1)} %collective-permute-done.1.far_head_ref, bf16[176,4096]{1,0:T(8,128)(2,1)S(1)} %shard_map.88.own_ref, ...), custom_call_target="tpu_custom_call" | custom-call | flops 100000000 | bytes 10000 | tf_op jit(solution)/shard_map/pallas_call | solution.py:285
  46.0 3.4 %collective-permute-start.4 = (f32[352,640]{1,0:T(8,128)S(1)}, f32[352,640]{1,0:T(8,128)S(1)}, u32[]{:S(2)}, u32[]{:S(2)}) collective-permute-start(f32[352,640]{1,0:T(8,128)S(1)} %shard_map.92.mine_ref), channel_id=1, source_target_pairs={{0,1},{1,0},{2,3},{3,2},{4,5},{5,4},{6,7},{7,6},{8,9},{9,8},{10,11... | collective-permute-start | bytes 2703368 | tf_op jit(solution)/shard_map/ppermute | solution.py:250
  49.5 3.5 %collective-permute-done.5.tail_ref.far_tail_ref = bf16[160,2048]{1,0:T(8,128)(2,1)S(1)} collective-permute-done((bf16[160,2048]{1,0:T(8,128)(2,1)S(1)}, bf16[160,2048]{1,0:T(8,128)(2,1)S(1)}, u32[]{:S(2)}, u32[]{:S(2)}) %collective-permute-start.5) | collective-permute-done | bytes 655392 | tf_op jit(solution)/shard_map/ppermute | solution.py:246
  53.0 1.4 %collective-permute-done.6.back_ref = bf16[256,128]{1,0:T(8,128)(2,1)S(1)} collective-permute-done((bf16[256,128]{1,0:T(8,128)(2,1)S(1)}, bf16[256,128]{1,0:T(8,128)(2,1)S(1)}, u32[]{:S(2)}, u32[]{:S(2)}) %collective-permute-start.6) | collective-permute-done | bytes 65568 | tf_op jit(solution)/shard_map/ppermute | solution.py:246
  54.4 0.8 shard_map.94.mine_ref
  55.2 2.7 %collective-permute-start.7 = (bf16[224,512]{1,0:T(8,128)(2,1)S(1)}, bf16[224,512]{1,0:T(8,128)(2,1)S(1)}, u32[]{:S(2)}, u32[]{:S(2)}) collective-permute-start(bf16[224,512]{1,0:T(8,128)(2,1)S(1)} %shard_map.94.mine_ref), channel_id=1, source_target_pairs={{0,1},{1,0},{2,3},{3,2},{4,5},{5,4},{6,7},{7,6},{8,9},{9,8},{10,11... | collective-permute-start | bytes 688136 | tf_op jit(solution)/shard_map/ppermute | solution.py:250
  58.0 0.2 shard_map.93
  58.2 0.9 collective-permute-done.7.other_ref
  59.0 1.3 %shard_map.95 = bf16[8,448,256]{2,1,0:T(8,128)(2,1)S(1)} custom-call(s32[1]{0:T(128)} %bitcast.core_ref, f32[256,512]{1,0:T(8,128)S(1)} %get-tuple-element.15.early_ref, bf16[224,512]{1,0:T(8,128)(2,1)S(1)} %shard_map.94.mine_ref, bf16[224,512]{1,0:T(8,128)(2,1)S(1)} %collective-permute-done.7.other_ref, ...), custom_call_target="tpu_custom_call" | custom-call | flops 20999999488 | bytes 2100000 | tf_op jit(solution)/shard_map/pallas_call | solution.py:300
  60.3 28.1 %all_to_all.10.in_ref = bf16[8,448,256]{2,1,0:T(8,128)(2,1)S(1)} all-to-all(bf16[8,448,256]{2,1,0:T(8,128)(2,1)S(1)} %shard_map.95), channel_id=1, replica_groups=mesh['z'=16,'xl'=2,'yh'=4,'yl'=2,'xh'=2,'c'=2] {'xh','xl','yl'}, dimensions={0} | all-to-all | bytes 3670016 | tf_op jit(solution)/shard_map/all_to_all | solution.py:303
  88.4 0.3 shard_map.96
  88.7 14.0 %all_to_all.11.in_ref = bf16[4,224,128]{2,1,0:T(8,128)(2,1)S(1)} all-to-all(bf16[4,224,128]{2,1,0:T(8,128)(2,1)S(1)} %shard_map.96), channel_id=1, replica_groups=mesh['z'=16,'xl'=2,'yh'=4,'yl'=2,'xh'=2,'c'=2] {'yh'}, dimensions={0} | all-to-all | bytes 458752 | tf_op jit(solution)/shard_map/all_to_all | solution.py:307
  102.7 0.7 shard_map.97
  (13 shorter events, 0.0 us)
Async XLA Ops:
  0.6 1.5 %copy-start = (bf16[224,4096]{1,0:T(8,128)(2,1)S(1)}, bf16[224,4096]{1,0:T(8,128)(2,1)}, u32[]{:S(2)}) copy-start(bf16[224,4096]{1,0:T(8,128)(2,1)} %param.11) | copy-start | bytes 5505028
  0.6 20.3 %copy-start.4 = (s32[1,4]{1,0:T(1,128)S(1)}, s32[1,4]{1,0:T(1,128)}, u32[]{:S(2)}) copy-start(s32[1,4]{1,0:T(1,128)} %len_ref.7) | copy-start | bytes 52
  0.7 20.3 %copy-start.6 = (bf16[160,4096]{1,0:T(8,128)(2,1)S(1)}, bf16[160,4096]{1,0:T(8,128)(2,1)}, u32[]{:S(2)}) copy-start(bf16[160,4096]{1,0:T(8,128)(2,1)} %tok_ref.1) | copy-start | bytes 3932164
  2.2 37.8 %collective-permute-start.3 = (bf16[112,4096]{1,0:T(8,128)(2,1)S(1)}, bf16[112,4096]{1,0:T(8,128)(2,1)S(1)}, u32[]{:S(2)}, u32[]{:S(2)}) collective-permute-start(bf16[112,4096]{1,0:T(8,128)(2,1)S(1)} %constant_dynamic-slice_fusion.down_ref), channel_id=1, source_target_pairs={{0,960},{64,0},{128,64},{192,128},{256,192},{320,256},{384,320},{4... | collective-permute-start | bytes 2752520 | tf_op jit(solution)/shard_map/ppermute | solution.py:246
  21.0 8.8 %copy-start.5 = (s32[1,4]{1,0:T(1,128)S(1)}, s32[1,4]{1,0:T(1,128)}, u32[]{:S(2)}) copy-start(s32[1,4]{1,0:T(1,128)} %rew_ref.1) | copy-start | bytes 52
  22.1 7.7 %copy-start.3 = (bf16[160,4096]{1,0:T(8,128)(2,1)S(1)}, bf16[160,4096]{1,0:T(8,128)(2,1)}, u32[]{:S(2)}) copy-start(bf16[160,4096]{1,0:T(8,128)(2,1)} %cot_ref.1) | copy-start | bytes 3932164
  22.1 4.9 %collective-permute-start = (bf16[176,2048]{1,0:T(8,128)(2,1)S(1)}, bf16[176,2048]{1,0:T(8,128)(2,1)S(1)}, u32[]{:S(2)}, u32[]{:S(2)}) collective-permute-start(bf16[176,2048]{1,0:T(8,128)(2,1)S(1)} %get-tuple-element.12), channel_id=1, source_target_pairs={{0,1},{1,0},{2,3},{3,2},{4,5},{5,4},{6,7},{7,6},{8,9},{9,8},{10,11... | collective-permute-start | bytes 2162696 | tf_op jit(solution)/shard_map/ppermute | solution.py:250
  25.1 19.4 %collective-permute-start.1 = (bf16[96,2048]{1,0:T(8,128)(2,1)S(1)}, bf16[96,2048]{1,0:T(8,128)(2,1)S(1)}, u32[]{:S(2)}, u32[]{:S(2)}) collective-permute-start(bf16[96,2048]{1,0:T(8,128)(2,1)S(1)} %get-tuple-element.10.head_ref), channel_id=1, source_target_pairs={{0,64},{64,128},{128,192},{192,256},{256,320},{320,384},{384,448},... | collective-permute-start | bytes 1179656 | tf_op jit(solution)/shard_map/ppermute | solution.py:246
  27.8 25.2 %collective-permute-start.5 = (bf16[160,2048]{1,0:T(8,128)(2,1)S(1)}, bf16[160,2048]{1,0:T(8,128)(2,1)S(1)}, u32[]{:S(2)}, u32[]{:S(2)}) collective-permute-start(bf16[160,2048]{1,0:T(8,128)(2,1)S(1)} %shard_map.87.after_ref.tail_ref), channel_id=1, source_target_pairs={{0,64},{64,128},{128,192},{192,256},{256,320},{320,384},{384,448},... | collective-permute-start | bytes 1966088 | tf_op jit(solution)/shard_map/ppermute | solution.py:246
  30.6 9.4 %collective-permute-start.2 = (bf16[176,4096]{1,0:T(8,128)(2,1)S(1)}, bf16[176,4096]{1,0:T(8,128)(2,1)S(1)}, u32[]{:S(2)}, u32[]{:S(2)}) collective-permute-start(bf16[176,4096]{1,0:T(8,128)(2,1)S(1)} %shard_map.88.own_ref), channel_id=1, source_target_pairs={{0,1},{1,0},{2,3},{3,2},{4,5},{5,4},{6,7},{7,6},{8,9},{9,8},{10,11... | collective-permute-start | bytes 4325384 | tf_op jit(solution)/shard_map/ppermute | solution.py:250
  40.0 3.4 %copy-start.1 = (bf16[4096,224]{0,1:T(8,128)(2,1)S(1)}, bf16[4096,224]{0,1:T(8,128)(2,1)}, u32[]{:S(2)}) copy-start(bf16[4096,224]{0,1:T(8,128)(2,1)} %param.9) | copy-start | bytes 5505028
  40.0 3.4 %copy-start.2 = (bf16[4096,224]{0,1:T(8,128)(2,1)S(1)}, bf16[4096,224]{0,1:T(8,128)(2,1)}, u32[]{:S(2)}) copy-start(bf16[4096,224]{0,1:T(8,128)(2,1)} %param.10) | copy-start | bytes 5505028
  41.4 13.0 %collective-permute-start.6 = (bf16[256,128]{1,0:T(8,128)(2,1)S(1)}, bf16[256,128]{1,0:T(8,128)(2,1)S(1)}, u32[]{:S(2)}, u32[]{:S(2)}) collective-permute-start(bf16[256,128]{1,0:T(8,128)(2,1)S(1)} %get-tuple-element.14.after_ref), channel_id=1, source_target_pairs={{0,64},{64,128},{128,192},{192,256},{256,320},{320,384},{384,448},... | collective-permute-start | bytes 196616 | tf_op jit(solution)/shard_map/ppermute | solution.py:246
  46.0 11.9 %collective-permute-start.4 = (f32[352,640]{1,0:T(8,128)S(1)}, f32[352,640]{1,0:T(8,128)S(1)}, u32[]{:S(2)}, u32[]{:S(2)}) collective-permute-start(f32[352,640]{1,0:T(8,128)S(1)} %shard_map.92.mine_ref), channel_id=1, source_target_pairs={{0,1},{1,0},{2,3},{3,2},{4,5},{5,4},{6,7},{7,6},{8,9},{9,8},{10,11... | collective-permute-start | bytes 2703368 | tf_op jit(solution)/shard_map/ppermute | solution.py:250
  55.2 3.8 %collective-permute-start.7 = (bf16[224,512]{1,0:T(8,128)(2,1)S(1)}, bf16[224,512]{1,0:T(8,128)(2,1)S(1)}, u32[]{:S(2)}, u32[]{:S(2)}) collective-permute-start(bf16[224,512]{1,0:T(8,128)(2,1)S(1)} %shard_map.94.mine_ref), channel_id=1, source_target_pairs={{0,1},{1,0},{2,3},{3,2},{4,5},{5,4},{6,7},{7,6},{8,9},{9,8},{10,11... | collective-permute-start | bytes 688136 | tf_op jit(solution)/shard_map/ppermute | solution.py:250

commit v6 on v5

--- a/solution.py
+++ b/solution.py
@@ -156,10 +156,8 @@
     cot_out[TAIL:, :] = got_tail
 
 
-def far_terms(tail_ref, wide_ref, back_ref, out_ref):
-    out_ref[: CAP + TAIL] = mm(tail_ref[...], wide_ref[...], ((1,), (1,))).astype(out_ref.dtype)
-    for k in range(4):
-        out_ref[CAP + TAIL :, k * 128 : (k + 1) * 128] = back_ref[k * 64 : (k + 1) * 64, :]
+def far_terms(tail_ref, wide_ref, out_ref):
+    out_ref[...] = mm(tail_ref[...], wide_ref[...], ((1,), (1,))).astype(out_ref.dtype)
 
 
 def swapped(value):
@@ -190,7 +188,7 @@
 
 
 def weight_grads(
-    core_ref, early_ref, mine_ref, other_ref, back_ref, gate_ref, up_ref,
+    core_ref, early_ref, mine_ref, other_ref, back_ref, cross_ref, gate_ref, up_ref,
     head_ref, tail_ref, far_head_ref, far_tail_ref, out_ref,
 ):
     mine, other = mine_ref[...].astype(F32), other_ref[...].astype(F32)
@@ -204,9 +202,8 @@
         ],
         axis=0,
     )
-    cross = other[CAP + TAIL :]
-    cross = jnp.concatenate([cross[:, k * 128 : (k + 1) * 128] for k in range(4)], axis=0)
-    back = both_halves(core_ref[0], back_ref[...].astype(F32), swapped(cross))
+    cross = swapped(cross_ref[...].astype(F32))
+    back = both_halves(core_ref[0], back_ref[...].astype(F32), cross)
     gate, up = hidden_grads(total[:, :HB], total[:, UP : UP + HB], back)
     gate = jnp.concatenate([gate_ref[...], gate], axis=0)
     up = jnp.concatenate([up_ref[...], up], axis=0)
@@ -244,6 +241,12 @@
 def along_z(block, distance):
     n = lax.axis_size("z")
     return lax.ppermute(block, "z", [(i, (i + distance) % n) for i in range(n)])
+
+
+def along_z_crossed(block):
+    n = lax.axis_size("z")
+    route = [(2 * i + c, 2 * ((i + 1) % n) + 1 - c) for i in range(n) for c in range(2)]
+    return lax.ppermute(block, ("z", "c"), route)
 
 
 def between_cores(block):
@@ -278,7 +281,7 @@
         next_back, (shape(2 * TAIL, D), shape(2 * CAP, 128)), cost=1.5,
         in_specs=[SMEM] + [VMEM] * 3 + [ANY],
     )(lengths, cot_own, cot_got, next_half, token)
-    far_back = along_z(back, 1)
+    far_back, far_cross = along_z(back, 1), along_z_crossed(back)
     wide = call(
         split_wide, shape(2 * UP, HALF), in_specs=[SMEM, VMEM, VMEM, ANY], cost=0.01,
     )(core, gate_weight.T, up_weight.T, back)
@@ -293,13 +296,13 @@
         cost=0.3, in_specs=[SMEM] + [VMEM] * 2,
     )(core, near, near_other)
     far = call(
-        far_terms, shape(CAP + TAIL + 64, 2 * UP), cost=10, in_specs=[VMEM] * 3
-    )(far_tail, wide, far_back)
+        far_terms, shape(CAP + TAIL, 2 * UP), cost=10, in_specs=[VMEM] * 2
+    )(far_tail, wide)
     far_other = between_cores(far)
 
     grads = call(
-        weight_grads, shape(FIRST, 2 * HB, HALF // FIRST), cost=2.1, in_specs=[SMEM] + [VMEM] * 10,
-    )(core, early, far, far_other, far_back, gate_near, up_near, head, tail, far_head, far_tail)
+        weight_grads, shape(FIRST, 2 * HB, HALF // FIRST), cost=2.1, in_specs=[SMEM] + [VMEM] * 11,
+    )(core, early, far, far_other, far_back, far_cross, gate_near, up_near, head, tail, far_head, far_tail)
     grads = lax.all_to_all(grads, ("xh", "xl", "yl"), split_axis=0, concat_axis=0, tiled=True)
     grads = call(
         first_sum, shape(SECOND, HB, 128), cost=0.4,

time: 105 us -> 104 us (level)
  waiting for transfers between devices: 13 us -> 9.56 us
  starting transfers between devices: 35.8 us -> 38.1 us
    ppermute x4, waiting for transfers between devices: 12.1 us -> 8.8 us  [along_z(): return lax.ppermute(block, 'z', [(i, (i + distance) % n) for i in range(n)])]
    ppermute x0 -> x1, starting transfers between devices: none -> 1.92 us  [along_z_crossed(): return lax.ppermute(block, ('z', 'c'), route)]
  transfers between devices with their start and end apart: 8 -> 9, of which waited for: 4 -> 3; matrix products, arithmetic and copies ran while one was open for 0% -> 0% of each run, Pallas kernels for 8% -> 8%
where the time goes in v6:
time: 104 us; the launch traced here: 102 us
  blocking collectives  42 us (40%)
  starting transfers between devices  38.1 us (37%)
  Pallas kernels  10.1 us (10%)
  waiting for transfers between devices  9.56 us (9%)
  local copies, waits for them, and re-layouts  1.57 us (2%)
    all_to_all x1, blocking collectives, on_device(): lax.all_to_all(grads, ('xh', 'xl', 'yl'), split_axis=0, concat_axis=0, ti...  28.1 us
    ppermute x4, starting transfers between devices, along_z(): return lax.ppermute(block, 'z', [(i, (i + distance) % n) for i in range(n)])  24.5 us
    all_to_all x1, blocking collectives, on_device(): grads = lax.all_to_all(grads, 'yh', split_axis=0, concat_axis=0, tiled=True)  13.9 us
    ppermute x4, starting transfers between devices, between_cores(): return lax.ppermute(block, 'c', [(0, 1), (1, 0)])  11.7 us
    ppermute x4, waiting for transfers between devices, along_z(): return lax.ppermute(block, 'z', [(i, (i + distance) % n) for i in range(n)])  8.8 us
  transfers between devices with their start and end apart: 9, of which 3 were waited for; matrix products, arithmetic and copies ran while one was open for 0% of the time, Pallas kernels for 8%

profile of v6, /device:TPU:1, one launch (start us, length us, event | category | flops | bytes accessed | tf_op | source)
XLA Modules:
  0.0 102.3 jit_solution(14508546839289040602)
XLA Ops:
  0.6 0.0 copy-start
  0.7 1.5 %copy-done = bf16[224,4096]{1,0:T(8,128)(2,1)S(1)} copy-done((bf16[224,4096]{1,0:T(8,128)(2,1)S(1)}, bf16[224,4096]{1,0:T(8,128)(2,1)}, u32[]{:S(2)}) %copy-start) | copy-done | bytes 1835032
  2.1 0.1 constant_dynamic-slice_fusion.down_ref
  2.2 18.8 %collective-permute-start.3 = (bf16[112,4096]{1,0:T(8,128)(2,1)S(1)}, bf16[112,4096]{1,0:T(8,128)(2,1)S(1)}, u32[]{:S(2)}, u32[]{:S(2)}) collective-permute-start(bf16[112,4096]{1,0:T(8,128)(2,1)S(1)} %constant_dynamic-slice_fusion.down_ref), channel_id=1, source_target_pairs={{0,960},{64,0},{128,64},{192,128},{256,192},{320,256},{384,320},{4... | collective-permute-start | bytes 2752520 | tf_op jit(solution)/shard_map/ppermute | solution.py:243
  21.0 0.0 copy-start.5
  21.0 1.1 %shard_map.86 = (bf16[96,2048]{1,0:T(8,128)(2,1)S(1)}, bf16[64,2048]{1,0:T(8,128)(2,1)S(1)}, bf16[176,2048]{1,0:T(8,128)(2,1)S(1)}) custom-call(s32[1]{0:T(128)} %bitcast.core_ref, s32[1,4]{1,0:T(1,128)S(1)} %copy-done.4, bf16[160,4096]{1,0:T(8,128)(2,1)S(1)} %copy-done.6), custom_call_target="tpu_custom_call" | custom-call | flops 16999999488 | bytes 1700000 | tf_op jit(solution)/shard_map/pallas_call | solution.py:260
  22.1 0.0 copy-start.3
  22.1 3.0 %collective-permute-start = (bf16[176,2048]{1,0:T(8,128)(2,1)S(1)}, bf16[176,2048]{1,0:T(8,128)(2,1)S(1)}, u32[]{:S(2)}, u32[]{:S(2)}) collective-permute-start(bf16[176,2048]{1,0:T(8,128)(2,1)S(1)} %get-tuple-element.12), channel_id=1, source_target_pairs={{0,1},{1,0},{2,3},{3,2},{4,5},{5,4},{6,7},{7,6},{8,9},{9,8},{10,11... | collective-permute-start | bytes 2162696 | tf_op jit(solution)/shard_map/ppermute | solution.py:253
  25.1 1.9 %collective-permute-start.1 = (bf16[96,2048]{1,0:T(8,128)(2,1)S(1)}, bf16[96,2048]{1,0:T(8,128)(2,1)S(1)}, u32[]{:S(2)}, u32[]{:S(2)}) collective-permute-start(bf16[96,2048]{1,0:T(8,128)(2,1)S(1)} %get-tuple-element.10.head_ref), channel_id=1, source_target_pairs={{0,64},{64,128},{128,192},{192,256},{256,320},{320,384},{384,448},... | collective-permute-start | bytes 1179656 | tf_op jit(solution)/shard_map/ppermute | solution.py:243
  27.0 0.8 shard_map.87.after_ref.tail_ref
  27.8 1.9 %collective-permute-start.5 = (bf16[160,2048]{1,0:T(8,128)(2,1)S(1)}, bf16[160,2048]{1,0:T(8,128)(2,1)S(1)}, u32[]{:S(2)}, u32[]{:S(2)}) collective-permute-start(bf16[160,2048]{1,0:T(8,128)(2,1)S(1)} %shard_map.87.after_ref.tail_ref), channel_id=1, source_target_pairs={{0,64},{64,128},{128,192},{192,256},{256,320},{320,384},{384,448},... | collective-permute-start | bytes 1966088 | tf_op jit(solution)/shard_map/ppermute | solution.py:243
  29.8 0.8 shard_map.88.own_ref
  30.6 2.1 %collective-permute-start.2 = (bf16[176,4096]{1,0:T(8,128)(2,1)S(1)}, bf16[176,4096]{1,0:T(8,128)(2,1)S(1)}, u32[]{:S(2)}, u32[]{:S(2)}) collective-permute-start(bf16[176,4096]{1,0:T(8,128)(2,1)S(1)} %shard_map.88.own_ref), channel_id=1, source_target_pairs={{0,1},{1,0},{2,3},{3,2},{4,5},{5,4},{6,7},{7,6},{8,9},{9,8},{10,11... | collective-permute-start | bytes 4325384 | tf_op jit(solution)/shard_map/ppermute | solution.py:253
  32.8 7.2 %collective-permute-done.3.after_ref.next_ref = bf16[112,4096]{1,0:T(8,128)(2,1)S(1)} collective-permute-done((bf16[112,4096]{1,0:T(8,128)(2,1)S(1)}, bf16[112,4096]{1,0:T(8,128)(2,1)S(1)}, u32[]{:S(2)}, u32[]{:S(2)}) %collective-permute-start.3) | collective-permute-done | bytes 917536 | tf_op jit(solution)/shard_map/ppermute | solution.py:243
  40.0 1.4 %shard_map.90 = (bf16[64,4096]{1,0:T(8,128)(2,1)S(1)}, bf16[256,128]{1,0:T(8,128)(2,1)S(1)}) custom-call(s32[1,4]{1,0:T(1,128)S(1)} %copy-done.4, bf16[176,4096]{1,0:T(8,128)(2,1)S(1)} %shard_map.88.own_ref, bf16[176,4096]{1,0:T(8,128)(2,1)S(1)} %collective-permute-done.2.got_ref, bf16[112,4096]{1,0:T(8,128)(2,1)S(1)} %collective-permute-done.3.after_ref.next_ref, ...), custom_call_target="tpu_custom_call" | custom-call | flops 15000000512 | bytes 1500000 | tf_op jit(solution)/shard_map/pallas_call | solution.py:280
  41.4 1.9 %collective-permute-start.7 = (bf16[256,128]{1,0:T(8,128)(2,1)S(1)}, bf16[256,128]{1,0:T(8,128)(2,1)S(1)}, u32[]{:S(2)}, u32[]{:S(2)}) collective-permute-start(bf16[256,128]{1,0:T(8,128)(2,1)S(1)} %get-tuple-element.14.after_ref), channel_id=1, source_target_pairs={{0,64},{64,128},{128,192},{192,256},{256,320},{320,384},{384,448},... | collective-permute-start | bytes 196616 | tf_op jit(solution)/shard_map/ppermute | solution.py:243
  43.4 1.9 %collective-permute-start.8 = (bf16[256,128]{1,0:T(8,128)(2,1)S(1)}, bf16[256,128]{1,0:T(8,128)(2,1)S(1)}, u32[]{:S(2)}, u32[]{:S(2)}) collective-permute-start(bf16[256,128]{1,0:T(8,128)(2,1)S(1)} %get-tuple-element.14.after_ref), channel_id=1, source_target_pairs={{0,65},{1,64},{64,129},{65,128},{128,193},{129,192},{192,257},{193... | collective-permute-start | bytes 196616 | tf_op jit(solution)/shard_map/ppermute | solution.py:249
  45.3 1.1 %shard_map.91.wide_ref = bf16[512,2048]{1,0:T(8,128)(2,1)S(1)} custom-call(s32[1]{0:T(128)} %bitcast.core_ref, bf16[224,4096]{1,0:T(8,128)(2,1)S(1)} %bitcast.3, bf16[224,4096]{1,0:T(8,128)(2,1)S(1)} %bitcast.4, bf16[256,128]{1,0:T(8,128)(2,1)S(1)} %get-tuple-element.14.after_ref), custom_call_target="tpu_custom_call" | custom-call | flops 100000000 | bytes 10000 | tf_op jit(solution)/shard_map/pallas_call | solution.py:285
  46.5 0.0 collective-permute-done.1.far_head_ref
  46.5 1.5 %shard_map.92.mine_ref = f32[352,640]{1,0:T(8,128)S(1)} custom-call(bf16[96,2048]{1,0:T(8,128)(2,1)S(1)} %get-tuple-element.10.head_ref, bf16[160,2048]{1,0:T(8,128)(2,1)S(1)} %shard_map.87.after_ref.tail_ref, bf16[96,2048]{1,0:T(8,128)(2,1)S(1)} %collective-permute-done.1.far_head_ref, bf16[176,4096]{1,0:T(8,128)(2,1)S(1)} %shard_map.88.own_ref, ...), custom_call_target="tpu_custom_call" | custom-call | flops 100000000 | bytes 10000 | tf_op jit(solution)/shard_map/pallas_call | solution.py:288
  48.0 3.4 %collective-permute-start.4 = (f32[352,640]{1,0:T(8,128)S(1)}, f32[352,640]{1,0:T(8,128)S(1)}, u32[]{:S(2)}, u32[]{:S(2)}) collective-permute-start(f32[352,640]{1,0:T(8,128)S(1)} %shard_map.92.mine_ref), channel_id=1, source_target_pairs={{0,1},{1,0},{2,3},{3,2},{4,5},{5,4},{6,7},{7,6},{8,9},{9,8},{10,11... | collective-permute-start | bytes 2703368 | tf_op jit(solution)/shard_map/ppermute | solution.py:253
  51.4 1.6 %collective-permute-done.5.tail_ref.far_tail_ref = bf16[160,2048]{1,0:T(8,128)(2,1)S(1)} collective-permute-done((bf16[160,2048]{1,0:T(8,128)(2,1)S(1)}, bf16[160,2048]{1,0:T(8,128)(2,1)S(1)}, u32[]{:S(2)}, u32[]{:S(2)}) %collective-permute-start.5) | collective-permute-done | bytes 655392 | tf_op jit(solution)/shard_map/ppermute | solution.py:243
  53.0 0.8 shard_map.94.mine_ref
  53.8 3.1 %collective-permute-start.6 = (bf16[160,512]{1,0:T(8,128)(2,1)S(1)}, bf16[160,512]{1,0:T(8,128)(2,1)S(1)}, u32[]{:S(2)}, u32[]{:S(2)}) collective-permute-start(bf16[160,512]{1,0:T(8,128)(2,1)S(1)} %shard_map.94.mine_ref), channel_id=1, source_target_pairs={{0,1},{1,0},{2,3},{3,2},{4,5},{5,4},{6,7},{7,6},{8,9},{9,8},{10,11... | collective-permute-start | bytes 491528 | tf_op jit(solution)/shard_map/ppermute | solution.py:253
  56.9 0.0 collective-permute-done.4.other_ref
  57.0 0.2 shard_map.93
  57.2 0.8 collective-permute-done.6.other_ref
  58.0 1.3 %shard_map.95 = bf16[8,448,256]{2,1,0:T(8,128)(2,1)S(1)} custom-call(s32[1]{0:T(128)} %bitcast.core_ref, f32[256,512]{1,0:T(8,128)S(1)} %get-tuple-element.15.early_ref, bf16[160,512]{1,0:T(8,128)(2,1)S(1)} %shard_map.94.mine_ref, bf16[160,512]{1,0:T(8,128)(2,1)S(1)} %collective-permute-done.6.other_ref, ...), custom_call_target="tpu_custom_call" | custom-call | flops 20999999488 | bytes 2100000 | tf_op jit(solution)/shard_map/pallas_call | solution.py:303
  59.3 28.1 %all_to_all.10.in_ref = bf16[8,448,256]{2,1,0:T(8,128)(2,1)S(1)} all-to-all(bf16[8,448,256]{2,1,0:T(8,128)(2,1)S(1)} %shard_map.95), channel_id=1, replica_groups=mesh['z'=16,'xl'=2,'yh'=4,'yl'=2,'xh'=2,'c'=2] {'xh','xl','yl'}, dimensions={0} | all-to-all | bytes 3670016 | tf_op jit(solution)/shard_map/all_to_all | solution.py:306
  87.4 0.3 shard_map.96
  87.7 13.9 %all_to_all.11.in_ref = bf16[4,224,128]{2,1,0:T(8,128)(2,1)S(1)} all-to-all(bf16[4,224,128]{2,1,0:T(8,128)(2,1)S(1)} %shard_map.96), channel_id=1, replica_groups=mesh['z'=16,'xl'=2,'yh'=4,'yl'=2,'xh'=2,'c'=2] {'yh'}, dimensions={0} | all-to-all | bytes 458752 | tf_op jit(solution)/shard_map/all_to_all | solution.py:310
  101.6 0.7 shard_map.97
  (15 shorter events, 0.0 us)
Async XLA Ops:
  0.6 1.5 %copy-start = (bf16[224,4096]{1,0:T(8,128)(2,1)S(1)}, bf16[224,4096]{1,0:T(8,128)(2,1)}, u32[]{:S(2)}) copy-start(bf16[224,4096]{1,0:T(8,128)(2,1)} %param.11) | copy-start | bytes 5505028
  0.6 20.3 %copy-start.4 = (s32[1,4]{1,0:T(1,128)S(1)}, s32[1,4]{1,0:T(1,128)}, u32[]{:S(2)}) copy-start(s32[1,4]{1,0:T(1,128)} %len_ref.7) | copy-start | bytes 52
  0.7 20.3 %copy-start.6 = (bf16[160,4096]{1,0:T(8,128)(2,1)S(1)}, bf16[160,4096]{1,0:T(8,128)(2,1)}, u32[]{:S(2)}) copy-start(bf16[160,4096]{1,0:T(8,128)(2,1)} %tok_ref.1) | copy-start | bytes 3932164
  2.2 37.8 %collective-permute-start.3 = (bf16[112,4096]{1,0:T(8,128)(2,1)S(1)}, bf16[112,4096]{1,0:T(8,128)(2,1)S(1)}, u32[]{:S(2)}, u32[]{:S(2)}) collective-permute-start(bf16[112,4096]{1,0:T(8,128)(2,1)S(1)} %constant_dynamic-slice_fusion.down_ref), channel_id=1, source_target_pairs={{0,960},{64,0},{128,64},{192,128},{256,192},{320,256},{384,320},{4... | collective-permute-start | bytes 2752520 | tf_op jit(solution)/shard_map/ppermute | solution.py:243
  21.0 8.8 %copy-start.5 = (s32[1,4]{1,0:T(1,128)S(1)}, s32[1,4]{1,0:T(1,128)}, u32[]{:S(2)}) copy-start(s32[1,4]{1,0:T(1,128)} %rew_ref.1) | copy-start | bytes 52
  22.1 7.7 %copy-start.3 = (bf16[160,4096]{1,0:T(8,128)(2,1)S(1)}, bf16[160,4096]{1,0:T(8,128)(2,1)}, u32[]{:S(2)}) copy-start(bf16[160,4096]{1,0:T(8,128)(2,1)} %cot_ref.1) | copy-start | bytes 3932164
  22.1 4.9 %collective-permute-start = (bf16[176,2048]{1,0:T(8,128)(2,1)S(1)}, bf16[176,2048]{1,0:T(8,128)(2,1)S(1)}, u32[]{:S(2)}, u32[]{:S(2)}) collective-permute-start(bf16[176,2048]{1,0:T(8,128)(2,1)S(1)} %get-tuple-element.12), channel_id=1, source_target_pairs={{0,1},{1,0},{2,3},{3,2},{4,5},{5,4},{6,7},{7,6},{8,9},{9,8},{10,11... | collective-permute-start | bytes 2162696 | tf_op jit(solution)/shard_map/ppermute | solution.py:253
  25.1 21.3 %collective-permute-start.1 = (bf16[96,2048]{1,0:T(8,128)(2,1)S(1)}, bf16[96,2048]{1,0:T(8,128)(2,1)S(1)}, u32[]{:S(2)}, u32[]{:S(2)}) collective-permute-start(bf16[96,2048]{1,0:T(8,128)(2,1)S(1)} %get-tuple-element.10.head_ref), channel_id=1, source_target_pairs={{0,64},{64,128},{128,192},{192,256},{256,320},{320,384},{384,448},... | collective-permute-start | bytes 1179656 | tf_op jit(solution)/shard_map/ppermute | solution.py:243
  27.8 25.2 %collective-permute-start.5 = (bf16[160,2048]{1,0:T(8,128)(2,1)S(1)}, bf16[160,2048]{1,0:T(8,128)(2,1)S(1)}, u32[]{:S(2)}, u32[]{:S(2)}) collective-permute-start(bf16[160,2048]{1,0:T(8,128)(2,1)S(1)} %shard_map.87.after_ref.tail_ref), channel_id=1, source_target_pairs={{0,64},{64,128},{128,192},{192,256},{256,320},{320,384},{384,448},... | collective-permute-start | bytes 1966088 | tf_op jit(solution)/shard_map/ppermute | solution.py:243
  30.6 9.4 %collective-permute-start.2 = (bf16[176,4096]{1,0:T(8,128)(2,1)S(1)}, bf16[176,4096]{1,0:T(8,128)(2,1)S(1)}, u32[]{:S(2)}, u32[]{:S(2)}) collective-permute-start(bf16[176,4096]{1,0:T(8,128)(2,1)S(1)} %shard_map.88.own_ref), channel_id=1, source_target_pairs={{0,1},{1,0},{2,3},{3,2},{4,5},{5,4},{6,7},{7,6},{8,9},{9,8},{10,11... | collective-permute-start | bytes 4325384 | tf_op jit(solution)/shard_map/ppermute | solution.py:253
  40.0 5.3 %copy-start.1 = (bf16[4096,224]{0,1:T(8,128)(2,1)S(1)}, bf16[4096,224]{0,1:T(8,128)(2,1)}, u32[]{:S(2)}) copy-start(bf16[4096,224]{0,1:T(8,128)(2,1)} %param.9) | copy-start | bytes 5505028
  40.0 5.3 %copy-start.2 = (bf16[4096,224]{0,1:T(8,128)(2,1)S(1)}, bf16[4096,224]{0,1:T(8,128)(2,1)}, u32[]{:S(2)}) copy-start(bf16[4096,224]{0,1:T(8,128)(2,1)} %param.10) | copy-start | bytes 5505028
  41.4 15.7 %collective-permute-start.7 = (bf16[256,128]{1,0:T(8,128)(2,1)S(1)}, bf16[256,128]{1,0:T(8,128)(2,1)S(1)}, u32[]{:S(2)}, u32[]{:S(2)}) collective-permute-start(bf16[256,128]{1,0:T(8,128)(2,1)S(1)} %get-tuple-element.14.after_ref), channel_id=1, source_target_pairs={{0,64},{64,128},{128,192},{192,256},{256,320},{320,384},{384,448},... | collective-permute-start | bytes 196616 | tf_op jit(solution)/shard_map/ppermute | solution.py:243
  43.4 13.8 %collective-permute-start.8 = (bf16[256,128]{1,0:T(8,128)(2,1)S(1)}, bf16[256,128]{1,0:T(8,128)(2,1)S(1)}, u32[]{:S(2)}, u32[]{:S(2)}) collective-permute-start(bf16[256,128]{1,0:T(8,128)(2,1)S(1)} %get-tuple-element.14.after_ref), channel_id=1, source_target_pairs={{0,65},{1,64},{64,129},{65,128},{128,193},{129,192},{192,257},{193... | collective-permute-start | bytes 196616 | tf_op jit(solution)/shard_map/ppermute | solution.py:249
  48.0 9.0 %collective-permute-start.4 = (f32[352,640]{1,0:T(8,128)S(1)}, f32[352,640]{1,0:T(8,128)S(1)}, u32[]{:S(2)}, u32[]{:S(2)}) collective-permute-start(f32[352,640]{1,0:T(8,128)S(1)} %shard_map.92.mine_ref), channel_id=1, source_target_pairs={{0,1},{1,0},{2,3},{3,2},{4,5},{5,4},{6,7},{7,6},{8,9},{9,8},{10,11... | collective-permute-start | bytes 2703368 | tf_op jit(solution)/shard_map/ppermute | solution.py:253
  53.8 4.1 %collective-permute-start.6 = (bf16[160,512]{1,0:T(8,128)(2,1)S(1)}, bf16[160,512]{1,0:T(8,128)(2,1)S(1)}, u32[]{:S(2)}, u32[]{:S(2)}) collective-permute-start(bf16[160,512]{1,0:T(8,128)(2,1)S(1)} %shard_map.94.mine_ref), channel_id=1, source_target_pairs={{0,1},{1,0},{2,3},{3,2},{4,5},{5,4},{6,7},{7,6},{8,9},{9,8},{10,11... | collective-permute-start | bytes 491528 | tf_op jit(solution)/shard_map/ppermute | solution.py:253
